TPU v7x, 32 devices: a whole 2x2x4 slice. The times are simulated.
32 devices in a mesh: prow: 8 (over z, core), pcol: 4 (over y, x).
Axes of the slice: x: 2, y: 2, z: 4, core: 2. Of those that a mesh axis runs over, the one named last changes fastest.
Arguments:
- grace_slab: float32 [90112, 2048], P('prow', 'pcol'), may hold values from -6 to 6
- goce_slab: float32 [90112, 2048], P('prow', 'pcol'), may hold values from -6 to 240
- grace_weight: float32 [1], replicated, may hold values from 0.8 to 1.25
- goce_weight: float32 [1], replicated, may hold values from 0.8 to 1.25
- kaula_prior: float32 [2048], P('pcol'), may hold values from 2 to 20
- row_target: int32 [90112], replicated, may hold values from 0 to 90111, as said below
- column_target: int32 [2048], replicated, may hold values from 0 to 2047, as said below
Outputs:
- factored: float32 [90112, 2048], P('prow', 'pcol')
Inputs may be any that keep to these rules, and one draw needn't show every extreme that they name: `row_target`: a permutation; each aligned block of 11264 entries holds exactly 1408 values in each aligned range of 11264 values. `column_target`: a permutation; each aligned block of 512 entries holds exactly 128 values in each aligned range of 512 values.
All inputs are finite; a program needn't handle non-finite values.
Results may differ from a plain program's by a relative error of at most 0.00005.
Values sent between devices are 32-bit elements; how exact they have to be, the bound alone decides.
No kernel may reach another device: no remote copies, remote signals or barrier semaphores. Data moves between devices by JAX's collectives and lax.ppermute only.
A program may use at most 256 MiB of HBM per device.

v0:
```python
import jax
import jax.numpy as jnp
from jax import lax
from jax.sharding import PartitionSpec as P

SLAB = 2048
PANEL = 512
BLOCK = 128


def order_index(amount, device, groups, block_size):
    local = jnp.arange(amount, dtype=jnp.int32)
    return (local // block_size * groups + device) * block_size + local % block_size


def to_order(gathered, row_devices, per_device):
    width = gathered.shape[1]
    shaped = gathered.reshape(row_devices, per_device, BLOCK, width)
    return shaped.transpose(1, 0, 2, 3).reshape(-1, width)


def factor_rows(raw_rows, order_rows, factor, inverse):
    solved = jnp.dot(raw_rows, inverse.T, precision=lax.Precision.HIGHEST)
    known = jnp.take(factor, jnp.minimum(order_rows, PANEL - 1), axis=0)
    return jnp.where(order_rows[:, None] < PANEL, known, solved)


def cholesky_block(diag_block):
    symmetric = jnp.tril(diag_block) + jnp.tril(diag_block, -1).T
    factor = jnp.linalg.cholesky(symmetric)
    inverse = jax.scipy.linalg.solve_triangular(
        factor, jnp.eye(PANEL, dtype=jnp.float32), lower=True
    )
    return (factor, inverse)


def placement(targets, owners, device, amount):
    sources = lax.dynamic_slice_in_dim(jnp.argsort(owners, stable=True), device * amount, amount)
    places = jnp.take(targets, sources) - device * amount
    return jnp.argsort(places)


def shards(
    grace_slab, goce_slab, grace_weight, goce_weight, kaula_prior, row_target, column_target
):
    row_devices = lax.axis_size("prow")
    col_devices = lax.axis_size("pcol")
    row_id = lax.axis_index("prow")
    col_id = lax.axis_index("pcol")
    rows_here, cols_here = grace_slab.shape
    row_owner = row_target // rows_here
    col_owner = column_target // cols_here
    send_rows = jnp.argsort(
        lax.dynamic_slice_in_dim(row_owner, row_id * rows_here, rows_here), stable=True
    )
    send_cols = jnp.argsort(
        lax.dynamic_slice_in_dim(col_owner, col_id * cols_here, cols_here), stable=True
    )
    outgoing = jnp.take(jnp.take(grace_slab, send_rows, axis=0), send_cols, axis=1)
    row_group = rows_here // row_devices
    packed = (
        outgoing.reshape(row_devices, row_group, cols_here)
        .transpose(1, 0, 2)
        .reshape(row_group, row_devices * cols_here)
    )
    received = lax.all_to_all(packed, ("prow", "pcol"), split_axis=1, concat_axis=1, tiled=True)
    arrived = (
        received.reshape(row_group, row_devices, cols_here)
        .transpose(1, 0, 2)
        .reshape(rows_here, cols_here)
    )
    arrived = jnp.take(arrived, placement(row_target, row_owner, row_id, rows_here), axis=0)
    arrived = jnp.take(arrived, placement(column_target, col_owner, col_id, cols_here), axis=1)
    order_rows = order_index(rows_here, row_id, row_devices, BLOCK)
    order_cols = order_index(cols_here, col_id, col_devices, BLOCK)
    on_diagonal = order_rows[:, None] == order_cols[None, :]
    combined = grace_weight[0] * arrived + goce_weight[0] * goce_slab
    combined = combined + jnp.where(on_diagonal, kaula_prior[None, :], 0.0)
    first_block = combined[:, :BLOCK]
    panel_block = lax.all_gather(first_block, "pcol", axis=1, tiled=True)[:, :PANEL]
    per_device = SLAB // (BLOCK * row_devices)
    raw_rows = to_order(
        lax.all_gather(panel_block[:BLOCK], "prow", axis=0, tiled=True), row_devices, 1
    )
    factor, inverse = cholesky_block(raw_rows[:PANEL])
    local_factors = factor_rows(panel_block, order_rows, factor, inverse)
    leading = to_order(
        lax.all_gather(local_factors[: per_device * BLOCK], "prow", axis=0, tiled=True),
        row_devices,
        per_device,
    )
    col_factors = jnp.take(leading, order_cols, axis=0)
    update = combined - jnp.dot(local_factors, col_factors.T, precision=lax.Precision.HIGHEST)
    panel_part = jnp.take(local_factors, jnp.minimum(order_cols, PANEL - 1), axis=1)
    kept = jnp.where(order_rows[:, None] < PANEL, combined, update)
    return jnp.where(order_cols[None, :] < PANEL, panel_part, kept)


def solution(mesh):
    return jax.shard_map(
        shards,
        mesh=mesh,
        in_specs=(P("prow", "pcol"), P("prow", "pcol"), P(), P(), P("pcol"), P(), P()),
        out_specs=P("prow", "pcol"),
        check_vma=False,
    )
```

profile of v0, /device:TPU:0, one launch (start us, length us, event | category | flops | bytes accessed | tf_op | source)
XLA Modules:
  0.0 1523.4 jit_solution(3447007436161315285)
XLA Ops:
  7.8 8.2 sort.102
  16.9 3.8 sort.103
  20.7 55.1 %gather_fusion.4 = f32[11264,512]{1,0:T(8,128)} fusion(f32[11264,512]{1,0:T(8,128)} %param.11, s32[11264]{0:T(1024)S(1)} %fusion.61), kind=kCustom, calls=%fused_computation.clone | custom fusion | bytes 46182400 | tf_op jit(solution)/shard_map/jit(_take)/gather | solution.py:59
  75.8 17.8 %broadcast_select_fusion.2 = f32[11264,512]{1,0:T(8,128)} fusion(f32[11264,512]{1,0:T(8,128)} %gather_fusion.4, pred[11264]{0:T(1024)(128)(4,1)S(1)} %compare_and_fusion.1), kind=kLoop, calls=%fused_computation.20 | loop fusion | flops 5767168 | bytes 46148608 | tf_op jit(solution)/shard_map/jit(_take)/select_n | solution.py:59
  93.6 23.5 %copy.16 = f32[11264,512]{0,1:T(8,128)} copy(f32[11264,512]{1,0:T(8,128)} %broadcast_select_fusion.2) | data formatting | bytes 46137344 | tf_op jit(solution)/shard_map/jit(_take)/select_n | solution.py:59
  117.2 29.1 %gather_fusion.5 = f32[512,11264]{1,0:T(8,128)} fusion(f32[11264,512]{0,1:T(8,128)} %copy.16, s32[1024]{0:T(1024)S(1)} %pad_clamp_fusion.3), kind=kCustom, calls=%fused_computation.1.clone | custom fusion | bytes 46139392 | tf_op jit(solution)/shard_map/jit(_take)/gather | solution.py:59
  146.3 8.7 broadcast_select_fusion
  154.9 8.2 copy.28
  163.1 7.4 all-to-all-start
  170.6 61.8 %sort.104 = (s32[90112]{0:T(1024)}, s32[90112]{0:T(1024)S(1)}) sort(s32[90112]{0:T(1024)S(1)} %copy-done.6, s32[90112]{0:T(1024)S(1)} %iota.184), dimensions={0}, to_apply=%region_2.5 | sort | flops 1531904 | bytes 1441792 | tf_op jit(solution)/shard_map/jit(argsort)/sort | solution.py:38
  232.5 62.4 %gather_fusion = s32[11264]{0:T(1024)S(1)} fusion(s32[90112]{0:T(1024)S(1)} %copy-done, s32[11264]{0:T(1024)S(1)} %fusion.63), kind=kCustom, calls=%fused_computation.5 | custom fusion | bytes 135168 | tf_op jit(solution)/shard_map/jit(_take)/gather | solution.py:39
  294.9 5.0 sort.106
  300.1 3.1 gather_fusion.1
  304.5 8.2 sort.105
  312.9 3.8 sort.107
  318.4 381.6 %all-to-all-done = f32[1408,32,128]{0,2,1:T(8,128)} async-done(((f32[1408,32,128]{0,2,1:T(8,128)}), f32[1408,32,128]{0,2,1:T(8,128)}, u32[]{:S(2)}, u32[]{:S(2)}) %all-to-all-start) | async-done | bytes 23068704 | tf_op jit(solution)/shard_map/all_to_all | solution.py:66
  700.1 23.3 %copy.18 = f32[8,1408,512]{2,1,0:T(8,128)} copy(f32[8,1408,512]{1,2,0:T(8,128)} %bitcast.5) | data formatting | bytes 46137344 | tf_op jit(solution)/shard_map/transpose | solution.py:69
  723.3 55.3 %gather_fusion.6 = f32[11264,512]{1,0:T(8,128)} fusion(f32[11264,512]{1,0:T(8,128)} %bitcast.82, s32[11264]{0:T(1024)S(1)} %fusion.62), kind=kCustom, calls=%fused_computation.2.clone | custom fusion | bytes 46182400 | tf_op jit(solution)/shard_map/jit(_take)/gather | solution.py:72
  778.6 18.0 %broadcast_select_fusion.1 = f32[11264,512]{1,0:T(8,128)} fusion(f32[11264,512]{1,0:T(8,128)} %gather_fusion.6, pred[11264]{0:T(1024)(128)(4,1)S(1)} %compare_and_fusion), kind=kLoop, calls=%fused_computation.19 | loop fusion | flops 5767168 | bytes 46148608 | tf_op jit(solution)/shard_map/jit(_take)/select_n | solution.py:72
  796.6 23.5 %copy.19 = f32[11264,512]{0,1:T(8,128)} copy(f32[11264,512]{1,0:T(8,128)} %broadcast_select_fusion.1) | data formatting | bytes 46137344 | tf_op jit(solution)/shard_map/jit(_take)/select_n | solution.py:72
  820.1 29.1 %gather_fusion.7 = f32[512,11264]{1,0:T(8,128)} fusion(f32[11264,512]{0,1:T(8,128)} %copy.19, s32[1024]{0:T(1024)S(1)} %pad_clamp_fusion.2), kind=kCustom, calls=%fused_computation.3.clone | custom fusion | bytes 46139392 | tf_op jit(solution)/shard_map/jit(_take)/gather | solution.py:73
  849.2 23.6 %copy.20 = f32[512,11264]{0,1:T(8,128)} copy(f32[512,11264]{1,0:T(8,128)} %gather_fusion.7) | data formatting | bytes 46137344 | tf_op jit(solution)/shard_map/jit(_take)/gather | solution.py:73
  872.8 15.6 %fusion.2 = f32[11264,512]{1,0:T(8,128)S(1)} fusion(f32[512,11264]{0,1:T(8,128)} %copy.20, f32[11264,512]{1,0:T(8,128)} %param.12, f32[512]{0:T(512)S(1)} %copy-done.11, s32[512]{0:T(512)S(1)} %copy-done.10, f32[]{:T(128)} %bitcast.81, f32[]{:T(128)} %bitcast.80, s32[11264]{0:T(1024)S(1)} %copy-done.7, pred[512]{0:T(512)(128)(4,1)S(1)} %copy-done.12), kind=kLoop, calls=%fused_computation.16 | loop fusion | flops 40370176 | bytes 69255688 | tf_op jit(solution)/shard_map/add | solution.py:78
  888.4 8.2 copy-done.3
  896.7 2.9 slice.159
  899.6 206.3 %all-gather.4.cloned.1.call-done = f32[11264,512]{1,0:T(8,128)} async-done(((f32[11264,128]{1,0:T(8,128)}), f32[11264,512]{1,0:T(8,128)}) %all-gather.4.cloned.1.call-update) | async-done | bytes 23068688 | tf_op jit(solution)/shard_map/all_gather | solution.py:80
  1110.1 26.8 %all-gather.6.cloned.1.call-done = f32[1024,512]{1,0:T(8,128)} async-done(((f32[128,512]{1,0:T(8,128)}), f32[1024,512]{1,0:T(8,128)}) %all-gather.6.cloned.1.call-update) | async-done | bytes 2097168 | tf_op jit(solution)/shard_map/all_gather | solution.py:83
  1140.6 11.7 cholesky.103
  1152.4 9.8 custom-call.31
  1162.9 11.7 cholesky.215
  1174.7 10.0 custom-call.32
  1185.3 11.7 cholesky.236
  1197.7 9.8 custom-call.33
  1208.2 12.1 cholesky.253
  1225.1 10.2 while.1
  1228.2 1.9 bitcast_dynamic-update-slice_fusion.2
  1230.8 1.9 bitcast_dynamic-update-slice_fusion.2
  1233.3 1.9 bitcast_dynamic-update-slice_fusion.2
  1236.2 40.1 %custom-call.34 = f32[4,128,128]{1,2,0:T(8,128)S(1)} custom-call(f32[4,128,128]{2,1,0:T(8,128)} %get-tuple-element.26), custom_call_target="InvertDiagBlocksLowerTriangular" | custom-call | tf_op jit(solution)/shard_map/jit(_solve_triangular)/triangular_solve | solution.py:31
  1282.5 44.4 %gather_fusion.2 = f32[11264,512]{1,0:T(8,128)} fusion(f32[512,512]{1,0:T(8,128)S(1)} %get-tuple-element.36, s32[11264]{0:T(1024)S(1)} %broadcast_clamp_fusion), kind=kCustom, calls=%fused_computation.7 | custom fusion | bytes 46182400 | tf_op jit(solution)/shard_map/jit(_take)/gather | solution.py:24
  1326.9 47.4 %select_select_fusion = f32[11264,512]{1,0:T(8,128)S(1)} fusion(f32[11264,512]{1,0:T(8,128)} %gather_fusion.2, f32[11264,512]{1,0:T(8,128)} %all-gather.4.cloned.1.call-done, pred[11264]{0:T(1024)(128)(4,1)S(1)} %get-tuple-element.51, pred[11264]{0:T(1024)(128)(4,1)S(1)} %get-tuple-element.52, f32[128,512]{1,0:T(8,128)S(1)} %fusion.40, ...), kind=kOutput, calls=%fused_computation.17 | convolution fusion | flops 35445800960 | bytes 70277120 | tf_op jit(solution)/shard_map/dot_general | solution.py:23
  1374.3 7.7 copy-done.2
  1382.9 23.7 %copy.23 = f32[11264,512]{0,1:T(8,128)} copy(f32[11264,512]{1,0:T(8,128)} %copy-done.2) | data formatting | bytes 46137344 | tf_op jit(solution)/shard_map/jit(_where)/select_n | solution.py:25
  1406.6 29.2 %gather_fusion.8 = f32[512,11264]{1,0:T(8,128)} fusion(f32[11264,512]{0,1:T(8,128)} %copy.23, s32[1024]{0:T(1024)S(1)} %pad_clamp_fusion.1), kind=kCustom, calls=%fused_computation.4.clone | custom fusion | bytes 46139392 | tf_op jit(solution)/shard_map/jit(_take)/gather | solution.py:94
  1435.9 23.5 %copy.24 = f32[512,11264]{0,1:T(8,128)} copy(f32[512,11264]{1,0:T(8,128)} %gather_fusion.8) | data formatting | bytes 46137344 | tf_op jit(solution)/shard_map/jit(_take)/gather | solution.py:94
  1459.3 4.7 copy.25
  1464.1 4.2 gather_fusion.3
  1468.3 48.3 %fusion = f32[11264,512]{1,0:T(8,128)} fusion(f32[11264,512]{1,0:T(8,128)} %copy-done.3, f32[512,11264]{0,1:T(8,128)} %copy.24, f32[11264,512]{1,0:T(8,128)} %copy-done.2, pred[11264]{0:T(1024)(128)(4,1)S(1)} %get-tuple-element.52, pred[512]{0:T(512)(128)(4,1)S(1)} %get-tuple-element.53, pred[512]{0:T(512)(128)(4,1)S(1)} %broadcast_compare_fusion.1, ...), kind=kOutput, calls=%fused_computation.12 | convolution fusion | flops 35456811008 | bytes 93336064 | tf_op jit(solution)/shard_map/dot_general | solution.py:93
  (114 shorter events, 29.5 us)
Async XLA Ops:
  7.8 68.0 %copy-start.5 = (s32[90112]{0:T(1024)}, s32[90112]{0:T(1024)S(1)}, u32[]{:S(2)}) copy-start(s32[90112]{0:T(1024)S(1)} %add_select_fusion) | copy-start | bytes 1081348
  16.8 59.0 %copy-start.8 = (s32[2048]{0:T(1024)}, s32[2048]{0:T(1024)S(1)}, u32[]{:S(2)}) copy-start(s32[2048]{0:T(1024)S(1)} %add_select_fusion.2) | copy-start | bytes 24580
  163.1 7.5 copy-start.6
  163.1 69.3 %copy-start = (s32[90112]{0:T(1024)S(1)}, s32[90112]{0:T(1024)}, u32[]{:S(2)}) copy-start(s32[90112]{0:T(1024)} %param.16) | copy-start | bytes 1081348
  163.1 536.9 %all-to-all-start = ((f32[1408,32,128]{0,2,1:T(8,128)}), f32[1408,32,128]{0,2,1:T(8,128)}, u32[]{:S(2)}, u32[]{:S(2)}) async-start(f32[1408,32,128]{0,2,1:T(8,128)} %bitcast.83), calls=%async_computation | async-start | bytes 46137344 | tf_op jit(solution)/shard_map/all_to_all | solution.py:66
  170.5 935.4 %all-gather.4.cloned.1.call-start = ((), (), s32[]{:S(2)}) async-start(), calls=%async_computation.1 | async-start | bytes 28835840 | tf_op jit(solution)/shard_map/all_gather | solution.py:80
  232.5 62.5 %copy-start.9 = (s32[2048]{0:T(1024)S(1)}, s32[2048]{0:T(1024)}, u32[]{:S(2)}) copy-start(s32[2048]{0:T(1024)} %copy-done.8) | copy-start | bytes 24580
  232.5 67.6 %copy-start.1 = (s32[2048]{0:T(1024)S(1)}, s32[2048]{0:T(1024)}, u32[]{:S(2)}) copy-start(s32[2048]{0:T(1024)} %param.17) | copy-start | bytes 24580
  849.2 23.6 %copy-start.7 = (s32[11264]{0:T(1024)S(1)}, s32[11264]{0:T(1024)}, u32[]{:S(2)}) copy-start(s32[11264]{0:T(1024)} %fusion.56) | copy-start | bytes 135172
  849.2 23.6 %copy-start.10 = (s32[512]{0:T(512)S(1)}, s32[512]{0:T(512)}, u32[]{:S(2)}) copy-start(s32[512]{0:T(512)} %fusion.74) | copy-start | bytes 6148
  849.2 23.6 %copy-start.11 = (f32[512]{0:T(512)S(1)}, f32[512]{0:T(512)}, u32[]{:S(2)}) copy-start(f32[512]{0:T(512)} %param.15) | copy-start | bytes 6148
  849.2 23.6 %copy-start.12 = (pred[512]{0:T(512)(128)(4,1)S(1)}, pred[512]{0:T(512)(128)(4,1)}, u32[]{:S(2)}) copy-start(pred[512]{0:T(512)(128)(4,1)} %compare_and_fusion.4) | copy-start | bytes 1540
  888.4 8.2 copy-start.3
  899.6 237.3 %all-gather.6.cloned.1.call-start = ((), (), s32[]{:S(2)}) async-start(), calls=%async_computation.2 | async-start | bytes 2359296 | tf_op jit(solution)/shard_map/all_gather | solution.py:83
  1107.6 351.7 %all-gather.8.cloned.1.call-start = ((), (), s32[]{:S(2)}) async-start(), calls=%async_computation.3 | async-start | bytes 4718592 | tf_op jit(solution)/shard_map/all_gather | solution.py:88
  1235.2 1.0 copy-start.4
  1374.3 7.7 copy-start.2
Sparse Core Ops, SparseCore 0:
  899.7 206.1 all-gather.3
  1107.7 29.0 all-gather.5
  1383.0 46.6 all-gather.7
where the time goes:
time: 1530 us; the launch traced here: 1520 us
  waiting for transfers between devices  615 us (40%)
  local copies, waits for them, and re-layouts  500 us (33%)
  other arithmetic  279 us (18%)
  matrix products  104 us (7%)
  between operations  17.6 us (1%)
    all_to_all x1, waiting for transfers between devices, shards(): lax.all_to_all(packed, ('prow', 'pcol'), split_axis=1, concat_axis=1, til...  382 us
    all_gather x1, waiting for transfers between devices, shards(): lax.all_gather(first_block, 'pcol', axis=1, tiled=True)[:, :PANEL]  206 us
    another operation x14, other arithmetic, cholesky_block(): factor = jnp.linalg.cholesky(symmetric)  79 us
    sort x2, other arithmetic, placement(): jnp.argsort(owners, stable=True)  66.8 us
    gather x2, local copies, waits for them, and re-layouts, placement(): places = jnp.take(targets, sources) - device * amount  65.6 us
    gather x1, local copies, waits for them, and re-layouts, shards(): jnp.take(arrived, placement(row_target, row_owner, row_id, rows_here), ax...  55.3 us
    gather x1, local copies, waits for them, and re-layouts, shards(): jnp.take(grace_slab, send_rows, axis=0)  55.1 us
    gather x2, local copies, waits for them, and re-layouts, shards(): jnp.take(local_factors, jnp.minimum(order_cols, PANEL - 1), axis=1)  52.7 us
  transfers between devices with their start and end apart: 4, of which 3 were waited for; matrix products, arithmetic and copies ran while one was open for 15% of the time, Pallas kernels for 0%

commit v1 on v0

v1 whole, which is shorter than its diff:
```python
import functools

import jax
import jax.numpy as jnp
from jax import lax
from jax.experimental import pallas as pl
from jax.experimental.pallas import tpu as pltpu
from jax.sharding import PartitionSpec as P

SLAB = 2048
PANEL = 512
BLOCK = 128
LANES = 128
SUBLANES = 8
VMEM_LIMIT = 56 * 1024 * 1024


def order_index(amount, device, groups, block_size):
    local = jnp.arange(amount, dtype=jnp.int32)
    return (local // block_size * groups + device) * block_size + local % block_size


def group_step(groups, width, most=1024):
    best = 1
    for size in range(1, groups + 1):
        if groups % size == 0 and size * width <= most:
            best = size
    return best


def chunk_widths(total, head):
    rest = total - head
    widths = [head]
    for part in (rest // 3, rest // 3, 2 * rest // 9):
        widths.append(part // 16 * 16)
    widths.append(total - sum(widths))
    return widths


def row_view(array):
    rows, cols = array.shape
    tiles = cols // LANES
    shaped = array.reshape(rows // SUBLANES, SUBLANES, tiles, LANES)
    return shaped.transpose(0, 2, 1, 3).reshape(rows * tiles, LANES)


def view_base(index, tiles):
    return index // SUBLANES * (SUBLANES * tiles) + index % SUBLANES


def split(value):
    high = value.astype(jnp.bfloat16)
    low = (value - high.astype(jnp.float32)).astype(jnp.bfloat16)
    return high, low


def split_array(value):
    high = lax.reduce_precision(value, 8, 7)
    return high.astype(jnp.bfloat16), (value - high).astype(jnp.bfloat16)


def product(left, right):
    return jnp.dot(left, right, preferred_element_type=jnp.float32)


def copy_rows(index_ref, first, source, target, count, tiles):
    def move(step, carry):
        for lane in range(SUBLANES):
            base = index_ref[first + step * SUBLANES + lane]
            target[pl.ds(step * SUBLANES * tiles + lane, tiles, stride=SUBLANES), :] = source[
                pl.ds(base, tiles, stride=SUBLANES), :
            ]
        return carry

    lax.fori_loop(0, count // SUBLANES, move, 0, unroll=4)


def from_view(value, rows, tiles):
    shaped = value.reshape(rows // SUBLANES, tiles, SUBLANES, LANES)
    return jnp.concatenate([shaped[:, t].reshape(rows, LANES) for t in range(tiles)], axis=1)


def pack_kernel(chunks, tiles, direct, index_ref, source_hbm, onehot_ref, *refs):
    outs = refs[: len(chunks)]
    held, picked, sem = refs[len(chunks) :]
    step = pl.program_id(0)

    @pl.when(step == 0)
    def _():
        copy = pltpu.make_async_copy(source_hbm, held, sem)
        copy.start()
        copy.wait()

    for (first_step, steps, first_row, groups, width), out_ref in zip(chunks, outs):

        @pl.when((step >= first_step) & (step < first_step + steps))
        def _():
            rows = groups * width
            first = first_row + (step - first_step) * rows
            copy_rows(index_ref, first, held, picked, rows, tiles)
            high, low = split(from_view(picked[: rows * tiles], rows, tiles))
            moved = product(high, onehot_ref[...]) + product(low, onehot_ref[...])
            if direct:
                lanes = out_ref.shape[3]
                for c in range(out_ref.shape[1]):
                    part = moved[:, c * lanes : (c + 1) * lanes]
                    out_ref[:, c] = part.reshape(groups, width, lanes)
            else:
                out_ref[...] = moved.reshape(groups, width, moved.shape[1])


def chunk_map(first_step, steps, zeros, step):
    return (jnp.clip(step - first_step, 0, steps - 1),) + (0,) * zeros


def pack(view, bases, onehot, row_devices, col_devices, widths):
    cols = onehot.shape[0]
    tiles = cols // LANES
    group = cols // col_devices
    direct = group % LANES == 0
    chunks, shapes, specs, first_step, first_row = [], [], [], 0, 0
    for width in widths:
        groups = group_step(row_devices, width)
        steps = row_devices // groups
        chunks.append((first_step, steps, first_row, groups, width))
        inner = (col_devices, width, group) if direct else (width, cols)
        shapes.append(jax.ShapeDtypeStruct((row_devices,) + inner, jnp.float32))
        place = functools.partial(chunk_map, first_step, steps, len(inner))
        specs.append(pl.BlockSpec((groups,) + inner, place))
        first_step += steps
        first_row += row_devices * width
    most = max(groups * width for _, _, _, groups, width in chunks)
    outs = pl.pallas_call(
        functools.partial(pack_kernel, tuple(chunks), tiles, direct),
        out_shape=shapes,
        grid=(first_step,),
        in_specs=[
            pl.BlockSpec(memory_space=pltpu.SMEM),
            pl.BlockSpec(memory_space=pl.ANY),
            pl.BlockSpec((cols, cols), lambda i: (0, 0)),
        ],
        out_specs=specs,
        scratch_shapes=[
            pltpu.VMEM(view.shape, jnp.float32),
            pltpu.VMEM((most * tiles, LANES), jnp.float32),
            pltpu.SemaphoreType.DMA,
        ],
        compiler_params=pltpu.CompilerParams(vmem_limit_bytes=VMEM_LIMIT),
        cost_estimate=pl.CostEstimate(
            flops=4 * first_row * cols * cols,
            bytes_accessed=4 * view.size + 24 * first_row * cols,
            transcendentals=0,
        ),
        name="pack",
    )(bases, view, onehot)
    packets = []
    for out, width in zip(outs, widths):
        if not direct:
            out = out.reshape(row_devices, width, col_devices, group).transpose(0, 2, 1, 3)
        packets.append(out.reshape(row_devices * col_devices, width, group))
    return packets


def arrived_spec(received, groups):
    shape = (groups,) + received.shape[1:]
    return pl.BlockSpec(shape, lambda i: (i,) + (0,) * (len(shape) - 1))


def load_arrived(ref):
    if len(ref.shape) == 4:
        groups, devices, width, lanes = ref.shape
        parts = [ref[:, c].reshape(groups * width, lanes) for c in range(devices)]
        return jnp.concatenate(parts, axis=1)
    groups, width, lanes = ref.shape
    return ref[...].reshape(groups * width, lanes)


def panel_kernel(rows, index_ref, weight_ref, received_ref, onehot_ref, goce_hbm, out_ref, held, picked, sem):
    step = pl.program_id(0)

    @pl.when(step == 0)
    def _():
        copy = pltpu.make_async_copy(goce_hbm.at[:, pl.ds(0, BLOCK)], held, sem)
        copy.start()
        copy.wait()

    copy_rows(index_ref, step * rows, held, picked, rows, 1)
    high, low = split(load_arrived(received_ref))
    moved = product(high, onehot_ref[...]) + product(low, onehot_ref[...])
    out_ref[...] = weight_ref[0] * moved + weight_ref[1] * picked[...]


def panel_part(received, places, weights, onehot, goce):
    row_devices, width = received.shape[0], received.shape[-2]
    cols = onehot.shape[0]
    groups = group_step(row_devices, width)
    rows = groups * width
    return pl.pallas_call(
        functools.partial(panel_kernel, rows),
        out_shape=jax.ShapeDtypeStruct((row_devices * width, BLOCK), jnp.float32),
        grid=(row_devices // groups,),
        in_specs=[
            pl.BlockSpec(memory_space=pltpu.SMEM),
            pl.BlockSpec(memory_space=pltpu.SMEM),
            arrived_spec(received, groups),
            pl.BlockSpec((cols, BLOCK), lambda i: (0, 0)),
            pl.BlockSpec(memory_space=pl.ANY),
        ],
        out_specs=pl.BlockSpec((rows, BLOCK), lambda i: (i, 0)),
        scratch_shapes=[
            pltpu.VMEM((goce.shape[0], BLOCK), jnp.float32),
            pltpu.VMEM((rows, BLOCK), jnp.float32),
            pltpu.SemaphoreType.DMA,
        ],
        compiler_params=pltpu.CompilerParams(vmem_limit_bytes=VMEM_LIMIT),
        cost_estimate=pl.CostEstimate(
            flops=4 * row_devices * width * cols * BLOCK,
            bytes_accessed=4 * goce.shape[0] * BLOCK + 16 * row_devices * width * cols,
            transcendentals=0,
        ),
        name="panel",
    )(places, weights, received, onehot, goce)


def update_kernel(masked, weight_ref, received_ref, raw_ref, keep_ref, onehot_ref, high_ref, low_ref, out_ref):
    panels = high_ref.shape[0] // BLOCK
    raw = jnp.concatenate([raw_ref[p] for p in range(panels)], axis=1)
    if masked:
        raw = raw * keep_ref[...]
    high, low = split(raw)
    total = product(high, high_ref[...]) + product(low, high_ref[...]) + product(high, low_ref[...])
    high, low = split(load_arrived(received_ref))
    moved = product(high, onehot_ref[...]) + product(low, onehot_ref[...])
    total = total + weight_ref[0] * moved
    rows, cols = total.shape
    for t in range(cols // LANES):
        out_ref[:, t] = total[:, t * LANES : (t + 1) * LANES].reshape(rows // SUBLANES, SUBLANES, LANES)


def update_part(received, raw, keep, weights, onehot, high, low, masked):
    row_devices, width = received.shape[0], received.shape[-2]
    cols = onehot.shape[0]
    tiles = cols // LANES
    groups = group_step(row_devices, width)
    rows = groups * width
    total = row_devices * width
    return pl.pallas_call(
        functools.partial(update_kernel, masked),
        out_shape=jax.ShapeDtypeStruct((total // SUBLANES, tiles, SUBLANES, LANES), jnp.float32),
        grid=(total // rows,),
        in_specs=[
            pl.BlockSpec(memory_space=pltpu.SMEM),
            arrived_spec(received, groups),
            pl.BlockSpec((PANEL // BLOCK, rows, BLOCK), lambda i: (0, i, 0)),
            pl.BlockSpec((rows, 1), (lambda i: (i, 0)) if masked else (lambda i: (0, 0))),
            pl.BlockSpec(onehot.shape, lambda i: (0, 0)),
            pl.BlockSpec(high.shape, lambda i: (0, 0)),
            pl.BlockSpec(low.shape, lambda i: (0, 0)),
        ],
        out_specs=pl.BlockSpec((rows // SUBLANES, tiles, SUBLANES, LANES), lambda i: (i, 0, 0, 0)),
        compiler_params=pltpu.CompilerParams(vmem_limit_bytes=VMEM_LIMIT),
        cost_estimate=pl.CostEstimate(
            flops=2 * total * cols * (3 * PANEL + 2 * cols),
            bytes_accessed=4 * total * (2 * cols + PANEL),
            transcendentals=0,
        ),
        name="update",
    )(weights, received, raw, keep, onehot, high, low)


def finish_kernel(rows, tiles, has_head, bounds_ref, index_ref, part_hbm, head_ref, base_hbm, out_hbm, held, picked, before, after, part_sem, in_sem, out_sem):
    size = part_hbm.shape[0]
    first, last = bounds_ref[0], bounds_ref[1]
    for source in range(1, bounds_ref.shape[0] // 2):
        first = jnp.minimum(first, bounds_ref[2 * source])
        last = jnp.maximum(last, bounds_ref[2 * source + 1])
    first = first // rows
    steps = last // rows + 1 - first

    def block(step):
        return pl.ds(pl.multiple_of((first + step) * rows, rows), rows)

    def fetch(step, slot):
        return pltpu.make_async_copy(out_hbm.at[block(step)], before.at[slot], in_sem.at[slot])

    def store(step, slot):
        return pltpu.make_async_copy(after.at[slot], out_hbm.at[block(step)], out_sem.at[slot])

    part_copy = pltpu.make_async_copy(part_hbm, held.at[pl.ds(0, size)], part_sem)
    part_copy.start()
    fetch(0, 0).start()
    held[pl.ds(size, SUBLANES * tiles), :] = jnp.zeros((SUBLANES * tiles, LANES), jnp.float32)
    part_copy.wait()

    def body(step, carry):
        slot = lax.rem(step, 2)

        @pl.when(step + 1 < steps)
        def _():
            fetch(step + 1, 1 - slot).start()

        copy_rows(index_ref, (first + step) * rows, held, picked, rows, tiles)
        fetch(step, slot).wait()

        @pl.when(step >= 2)
        def _():
            store(step - 2, slot).wait()

        after[slot] = before[slot] + from_view(picked[...], rows, tiles)
        if has_head:

            @pl.when(step == 0)
            def _():
                count = head_ref.shape[0]
                after[0, :count] = after[0, :count] + head_ref[...]

        store(step, slot).start()
        return carry

    lax.fori_loop(0, steps, body, 0)

    @pl.when(steps >= 2)
    def _():
        store(steps - 2, lax.rem(steps, 2)).wait()

    store(steps - 1, lax.rem(steps + 1, 2)).wait()


def finish_part(base, part, bounds, positions, offset, head, has_head):
    total, cols = base.shape
    tiles = cols // LANES
    rows = head.shape[0]
    while rows < 512 and total % (2 * rows) == 0:
        rows *= 2
    count = part.shape[0] // tiles
    local = positions - offset
    index = jnp.where((local >= 0) & (local < count), local, count)
    return pl.pallas_call(
        functools.partial(finish_kernel, rows, tiles, has_head),
        out_shape=jax.ShapeDtypeStruct((total, cols), jnp.float32),
        in_specs=[
            pl.BlockSpec(memory_space=pltpu.SMEM),
            pl.BlockSpec(memory_space=pltpu.SMEM),
            pl.BlockSpec(memory_space=pl.ANY),
            pl.BlockSpec(memory_space=pltpu.VMEM),
            pl.BlockSpec(memory_space=pl.ANY),
        ],
        out_specs=pl.BlockSpec(memory_space=pl.ANY),
        scratch_shapes=[
            pltpu.VMEM((part.shape[0] + SUBLANES * tiles, LANES), jnp.float32),
            pltpu.VMEM((rows * tiles, LANES), jnp.float32),
            pltpu.VMEM((2, rows, cols), jnp.float32),
            pltpu.VMEM((2, rows, cols), jnp.float32),
            pltpu.SemaphoreType.DMA,
            pltpu.SemaphoreType.DMA((2,)),
            pltpu.SemaphoreType.DMA((2,)),
        ],
        input_output_aliases={4: 0},
        compiler_params=pltpu.CompilerParams(vmem_limit_bytes=VMEM_LIMIT),
        cost_estimate=pl.CostEstimate(
            flops=2 * count * cols, bytes_accessed=16 * count * cols, transcendentals=0
        ),
        name="finish",
    )(bounds, view_base(index, tiles), part, head, base)


def precise(left, right):
    return jnp.dot(left, right, precision=lax.Precision.HIGHEST)


def cholesky_inverse(blocks, pause):
    count = len(blocks)
    size = blocks[0][0].shape[0]
    identity = jnp.eye(size, dtype=jnp.float32)
    factor, inverse = {}, {}
    for b in range(count):
        pivot = jnp.tril(blocks[b][b]) + jnp.tril(blocks[b][b], -1).T
        if b:
            left = jnp.concatenate([factor[b, k] for k in range(b)], axis=1)
            pivot = pivot - precise(left, left.T)
        factor[b, b] = jnp.linalg.cholesky(pivot, symmetrize_input=False)
        inverse[b, b] = jax.scipy.linalg.solve_triangular(factor[b, b], identity, lower=True)
        if b + 1 < count:
            below = jnp.concatenate([blocks[i][b] for i in range(b + 1, count)], axis=0)
            if b:
                rows = [
                    jnp.concatenate([factor[i, k] for k in range(b)], axis=1)
                    for i in range(b + 1, count)
                ]
                below = below - precise(jnp.concatenate(rows, axis=0), left.T)
            below = pause(b, precise(below, inverse[b, b].T))
            for i in range(b + 1, count):
                factor[i, b] = below[(i - b - 1) * size : (i - b) * size]
    zero = jnp.zeros((size, size), jnp.float32)
    for b in range(1, count):
        left = jnp.concatenate([factor[b, k] for k in range(b)], axis=1)
        above = [
            jnp.concatenate([inverse[k, j] if k >= j else zero for j in range(b)], axis=1)
            for k in range(b)
        ]
        solved = -precise(inverse[b, b], precise(left, jnp.concatenate(above, axis=0)))
        for j in range(b):
            inverse[b, j] = solved[:, j * size : (j + 1) * size]
    whole = [
        [
            jnp.concatenate([part[i, j] if i >= j else zero for j in range(count)], axis=1)
            for i in range(count)
        ]
        for part in (factor, inverse)
    ]
    return jnp.concatenate(whole[0], axis=0), jnp.concatenate(whole[1], axis=0)


def shards(
    grace_slab, goce_slab, grace_weight, goce_weight, kaula_prior, row_target, column_target
):
    row_devices = lax.axis_size("prow")
    col_devices = lax.axis_size("pcol")
    row_id = lax.axis_index("prow")
    col_id = lax.axis_index("pcol")
    rows_here, cols_here = grace_slab.shape
    tiles = cols_here // LANES
    row_group = rows_here // row_devices
    col_group = cols_here // col_devices
    per_device = SLAB // (BLOCK * row_devices)
    lead = per_device * BLOCK
    widths = chunk_widths(row_group, lead)
    starts = [sum(widths[:n]) for n in range(len(widths))]
    weights = jnp.concatenate([grace_weight, goce_weight])

    bits = (rows_here - 1).bit_length()
    mask = (1 << bits) - 1
    local = jnp.arange(rows_here, dtype=jnp.int32)
    mine = lax.dynamic_slice_in_dim(row_target, row_id * rows_here, rows_here)
    sources = (jnp.sort(mine * (1 << bits) + local) & mask).reshape(row_devices, row_group)
    source_bases = view_base(sources, tiles)
    my_cols = lax.dynamic_slice_in_dim(column_target, col_id * cols_here, cols_here)
    col_places = jnp.sum((my_cols[None, :] < my_cols[:, None]).astype(jnp.int32), axis=1)
    col_iota = jnp.arange(cols_here, dtype=jnp.int32)
    send_onehot = (col_places[:, None] == col_iota[None, :]).astype(jnp.bfloat16)

    view = row_view(grace_slab)
    chunk_bases = [
        source_bases[:, start : start + width].reshape(-1) for start, width in zip(starts, widths)
    ]
    packets = pack(view, chunk_bases[0], send_onehot, row_devices, col_devices, widths[:1])
    packets += pack(
        view, jnp.concatenate(chunk_bases[1:]), send_onehot, row_devices, col_devices, widths[1:]
    )

    sorted_rows = jnp.sort(row_target.reshape(row_devices, rows_here), axis=1)
    places = lax.dynamic_slice_in_dim(sorted_rows, row_id * row_group, row_group, axis=1)
    places = places - row_id * rows_here
    chunk_places = [
        places[:, start : start + width].reshape(-1) for start, width in zip(starts, widths)
    ]
    positions = jnp.sort(jnp.concatenate(chunk_places) * (1 << bits) + local) & mask
    sorted_cols = jnp.sort(column_target.reshape(col_devices, cols_here), axis=1)
    col_targets = lax.dynamic_slice_in_dim(sorted_cols, col_id * col_group, col_group, axis=1)
    col_targets = col_targets.reshape(-1) - col_id * cols_here
    take_onehot = (col_targets[:, None] == col_iota[None, :]).astype(jnp.bfloat16)
    order_cols = order_index(cols_here, col_id, col_devices, BLOCK)
    in_panel = order_cols < PANEL
    rest_onehot = jnp.where(in_panel[None, :], jnp.zeros((), jnp.bfloat16), take_onehot)
    scale = jnp.where(in_panel, 0.0, goce_weight[0]).astype(jnp.float32)
    out = goce_slab * scale[None, :]

    def exchange(packet):
        got = lax.all_to_all(packet, ("prow", "pcol"), split_axis=0, concat_axis=0, tiled=True)
        got = got.reshape(row_devices, col_devices, packet.shape[1], col_group)
        if col_group % LANES:
            got = got.transpose(0, 2, 1, 3).reshape(row_devices, packet.shape[1], cols_here)
        return got

    received = {0: exchange(packets[0])}
    panels, raws = {}, {}
    places_ends = jnp.stack(
        [places[:, jnp.array(starts)], places[:, jnp.array([s + w - 1 for s, w in zip(starts, widths)])]],
        axis=-1,
    )
    ends = [places_ends[:, n].reshape(-1) for n in range(len(widths))]

    def begin(n, after):
        packet, after, received[n - 1] = lax.optimization_barrier(
            (packets[n], after, received[n - 1])
        )
        received[n] = exchange(packet)
        return after

    def gather(n):
        panels[n] = panel_part(
            received[n], chunk_places[n], weights, take_onehot[:, :BLOCK], goce_slab
        )
        raws[n] = lax.all_gather(panels[n], "pcol", axis=0)

    all_kaula = lax.all_gather(kaula_prior[:BLOCK], "pcol", axis=0)
    chunk_places, positions, take_onehot, rest_onehot, ends, out, packets[2:], all_kaula = begin(
        1, (chunk_places, positions, take_onehot, rest_onehot, ends, out, packets[2:], all_kaula)
    )
    gather(0)
    my_lead = jnp.take(panels[0], positions[:lead], axis=0)
    lead_all = lax.all_gather(my_lead, ("prow", "pcol"), axis=0)
    lead_all = lead_all.reshape(row_devices, col_devices, per_device, BLOCK, BLOCK)

    def lead_block(row, col):
        return lead_all[row % row_devices, col, row // row_devices]

    panel_blocks = PANEL // BLOCK
    blocks = [
        [
            lead_block(i, j) + (jnp.diag(all_kaula[i]) if i == j else 0.0)
            for j in range(i + 1)
        ]
        for i in range(panel_blocks)
    ]

    def pause(step, value):
        if step == 0:
            value = begin(2, value)
            gather(1)
        return value

    factor, inverse = cholesky_inverse(blocks, pause)
    col_rows = []
    for n in range(cols_here // BLOCK):
        block = n * col_devices + col_id
        rows = lax.dynamic_index_in_dim(lead_all, block % row_devices, 0, keepdims=False)
        rows = lax.dynamic_index_in_dim(rows, block // row_devices, 1, keepdims=False)
        col_rows.append(rows[:panel_blocks].transpose(1, 0, 2).reshape(BLOCK, PANEL))
    col_rows = jnp.concatenate(col_rows, axis=0)
    solved = precise(inverse, col_rows.T)
    panel_iota = jnp.arange(PANEL, dtype=jnp.int32)
    identity = (panel_iota[:, None] == order_cols[None, :]).astype(jnp.float32)
    matrix = precise(inverse.T, jnp.where(in_panel[None, :], identity, -solved))
    matrix_high, matrix_low = split_array(matrix)

    order_rows = order_index(lead, row_id, row_devices, BLOCK)
    on_diagonal = order_rows[:, None] == order_cols[None, :]
    known = jnp.take(
        jnp.take(factor, jnp.minimum(order_rows, PANEL - 1), axis=0),
        jnp.minimum(order_cols, PANEL - 1),
        axis=1,
    )
    in_block = (order_rows[:, None] < PANEL) & in_panel[None, :]
    head = jnp.where(in_block, known, jnp.where(on_diagonal, kaula_prior[None, :], 0.0))
    first = chunk_places[0]
    first_order = (first // BLOCK * row_devices + row_id) * BLOCK + first % BLOCK
    keep = jnp.where(first_order < PANEL, 0.0, 1.0)[:, None].astype(jnp.float32)

    offset = 0
    last = len(widths) - 1
    for n in range(len(widths)):
        if n == last - 1:
            received[last], out = lax.optimization_barrier((received[last], out))
            gather(last)
        part = update_part(
            received[n], raws[n], keep, weights, rest_onehot, matrix_high, matrix_low, masked=n == 0
        ).reshape(-1, LANES)
        out = finish_part(out, part, ends[n], positions, offset, head, has_head=n == 0)
        offset += part.shape[0] // tiles
        if n + 3 <= last:
            out = begin(n + 3, out)
            gather(n + 2)
    return out


def solution(mesh):
    return jax.shard_map(
        shards,
        mesh=mesh,
        in_specs=(P("prow", "pcol"), P("prow", "pcol"), P(), P(), P("pcol"), P(), P()),
        out_specs=P("prow", "pcol"),
        check_vma=False,
    )
```

time: 1530 us -> 736 us (0.48)
  local copies, waits for them, and re-layouts: 500 us -> 27.4 us
  waiting for transfers between devices: 615 us -> 270 us
  Pallas kernels: 0 us -> 200 us
  other arithmetic: 279 us -> 138 us
  matrix products: 104 us -> 11.5 us
  blocking collectives: 0 us -> 29.9 us
  starting transfers between devices: 7.94 us -> 35.3 us
    gather x11 -> x8, local copies, waits for them, and re-layouts: 359 us -> 6.66 us  [the longest x2 2.31 us: shards(): jnp.take(jnp.take(factor, jnp.minimum(order_rows, PANEL - 1), axis=0), jn...]
    all_to_all x1 -> x5, waiting for transfers between devices: 382 us -> 55.5 us  [exchange(): lax.all_to_all(packet, ('prow', 'pcol'), split_axis=0, concat_axis=0, til...]
    pallas_call x0 -> x17, Pallas kernels: none -> 200 us  [the longest x5 53.5 us: update_part(): pl.pallas_call(functools.partial(update_kernel, masked), out_shape=jax.Sh...]
    dot_general x2 -> x16, matrix products: 95.7 us -> 10.6 us  [precise(): return jnp.dot(left, right, precision=lax.Precision.HIGHEST)]
    sort x6 -> x2, other arithmetic: 90.9 us -> 16.4 us  [the longest x1 8.21 us: shards(): jnp.sort(jnp.concatenate(chunk_places) * (1 << bits) + local) & mask]
    select_n x4 -> x1, local copies, waits for them, and re-layouts: 71.1 us -> 0.2 us  [shards(): jnp.take(factor, jnp.minimum(order_rows, PANEL - 1), axis=0)]
    select_n x12 -> x9, other arithmetic: 48 us -> 3.48 us  [the longest x1 0.98 us: shards(): jnp.where(in_panel[None, :], jnp.zeros((), jnp.bfloat16), take_onehot)]
    all_gather x0 -> x1, blocking collectives: none -> 29.9 us  [shards(): all_kaula = lax.all_gather(kaula_prior[:BLOCK], 'pcol', axis=0)]
  transfers between devices with their start and end apart: 4 -> 11, of which waited for: 3 -> 8; matrix products, arithmetic and copies ran while one was open for 15% -> 22% of each run, Pallas kernels for 0% -> 24%
where the time goes in v1:
time: 736 us; the launch traced here: 728 us
  waiting for transfers between devices  270 us (37%)
  Pallas kernels  200 us (27%)
  other arithmetic  138 us (19%)
  starting transfers between devices  35.3 us (5%)
  blocking collectives  29.9 us (4%)
  local copies, waits for them, and re-layouts  27.4 us (4%)
  between operations  16.2 us (2%)
  matrix products  11.5 us (2%)
    all_gather x1, waiting for transfers between devices, shards(): lead_all = lax.all_gather(my_lead, ('prow', 'pcol'), axis=0)  115 us
    all_gather x5, waiting for transfers between devices, gather(): raws[n] = lax.all_gather(panels[n], 'pcol', axis=0)  98.9 us
    all_to_all x5, waiting for transfers between devices, exchange(): lax.all_to_all(packet, ('prow', 'pcol'), split_axis=0, concat_axis=0, til...  55.5 us
    pallas_call x5, Pallas kernels, update_part(): pl.pallas_call(functools.partial(update_kernel, masked), out_shape=jax.Sh...  53.5 us
    pallas_call x2, Pallas kernels, pack(): pl.pallas_call(functools.partial(pack_kernel, tuple(chunks), tiles, direc...  50.1 us
    another operation x12, other arithmetic, cholesky_inverse(): factor[b, b] = jnp.linalg.cholesky(pivot, symmetrize_input=False)  50 us
    pallas_call x5, Pallas kernels, finish_part(): pl.pallas_call(functools.partial(finish_kernel, rows, tiles, has_head), o...  49.3 us
    pallas_call x5, Pallas kernels, panel_part(): pl.pallas_call(functools.partial(panel_kernel, rows), out_shape=jax.Shape...  46.9 us
  transfers between devices with their start and end apart: 11, of which 8 were waited for; matrix products, arithmetic and copies ran while one was open for 22% of the time, Pallas kernels for 24%

profile of v1, /device:TPU:0, one launch (start us, length us, event | category | flops | bytes accessed | tf_op | source)
XLA Modules:
  0.0 727.7 jit_solution(460958803691000681)
XLA Ops:
  8.7 8.2 %sort.43 = (s32[11264]{0:T(1024)S(1)}, s32[11264]{0:T(1024)}) sort(s32[11264]{0:T(1024)S(1)} %iota_add_fusion.1, s32[11264]{0:T(1024)S(1)} %iota.215), dimensions={0}, to_apply=%region_0.0 | sort | flops 157696 | bytes 180224 | tf_op jit(solution)/shard_map/jit(sort)/sort | solution.py:435
  19.6 14.9 %pack.3 = f32[8,4,256,128]{3,2,1,0:T(8,128)} custom-call(s32[2048]{0:T(1024)} %bitcast.195, f32[45056,128]{1,0:T(8,128)} %bitcast.167, bf16[512,512]{1,0:T(8,128)(2,1)} %fusion.15.onehot_ref), custom_call_target="tpu_custom_call" | custom-call | flops 2147483648 | bytes 48234496 | tf_op jit(solution)/shard_map/pack/pallas_call | solution.py:133
  34.5 7.4 %all-to-all-start = ((f32[32,256,128]{2,1,0:T(8,128)}), f32[32,256,128]{2,1,0:T(8,128)}, u32[]{:S(2)}, u32[]{:S(2)}) async-start(f32[32,256,128]{2,1,0:T(8,128)} %bitcast.169), calls=%async_computation | async-start | bytes 8388608 | tf_op jit(solution)/shard_map/all_to_all | solution.py:469
  44.3 29.9 %all-gather.6 = f32[4,1,128]{2,1,0:T(1,128)S(1)} all-gather(f32[1,1,128]{2,1,0:T(1,128)S(1)} %slice_bitcast_fusion.14), channel_id=2, replica_groups=mesh['prow'=8,'pcol'=4] {'pcol'}, dimensions={0}, use_global_device_ids=true | all-gather | bytes 2560 | tf_op jit(solution)/shard_map/all_gather | solution.py:496
  76.1 35.2 %pack.2 = (f32[8,4,384,128]{3,2,1,0:T(8,128)}, f32[8,4,384,128]{3,2,1,0:T(8,128)}, f32[8,4,256,128]{3,2,1,0:T(8,128)}, f32[8,4,128,128]{3,2,1,0:T(8,128)}) custom-call(s32[9216]{0:T(1024)} %pad_add_fusion.index_ref, f32[45056,128]{1,0:T(8,128)} %bitcast.168, bf16[512,512]{1,0:T(8,128)(2,1)} %fusion.15.onehot_ref), custom_call_target="tpu_custom_call" | custom-call | flops 9663676416 | bytes 136314880 | tf_op jit(solution)/shard_map/pack/pallas_call | solution.py:133
  111.3 16.1 %broadcast_multiply_fusion.base_hbm = f32[11264,512]{1,0:T(8,128)} fusion(f32[11264,512]{1,0:T(8,128)} %goce_hbm.9, f32[512]{0:T(512)S(1)} %broadcast_select_fusion.2), kind=kLoop, calls=%fused_computation.5 | loop fusion | flops 5767168 | bytes 46139392 | tf_op jit(solution)/shard_map/mul | solution.py:466
  136.2 8.2 %sort.45 = (s32[11264]{0:T(1024)S(1)}, s32[11264]{0:T(1024)}) sort(s32[11264]{0:T(1024)S(1)} %iota_add_fusion, s32[11264]{0:T(1024)S(1)} %iota.217), dimensions={0}, to_apply=%region_3.4 | sort | flops 157696 | bytes 180224 | tf_op jit(solution)/shard_map/jit(sort)/sort | solution.py:457
  145.1 8.9 %all-to-all-start.1 = ((f32[32,384,128]{2,1,0:T(8,128)}), f32[32,384,128]{2,1,0:T(8,128)}, u32[]{:S(2)}, u32[]{:S(2)}) async-start(f32[32,384,128]{2,1,0:T(8,128)} %bitcast.173), calls=%async_computation.1 | async-start | bytes 12582912 | tf_op jit(solution)/shard_map/all_to_all | solution.py:469
  154.6 9.0 %panel.5 = f32[2048,128]{1,0:T(8,128)} custom-call(s32[2048]{0:T(1024)} %bitcast.190, f32[2]{0:T(128)} %pad_maximum_fusion.11.weight_ref, f32[8,4,256,128]{3,2,1,0:T(8,128)} %bitcast.20.received_ref, bf16[512,128]{1,0:T(8,128)(2,1)} %slice.149.onehot_ref, f32[11264,512]{1,0:T(8,128)} %goce_hbm.9), custom_call_target="tpu_custom_call" | custom-call | flops 536870912 | bytes 22544384 | tf_op jit(solution)/shard_map/panel/pallas_call | solution.py:198
  163.7 1.9 gather_fusion.2
  167.1 114.7 %all-gather.14.cloned.1.call-done = f32[32,256,128]{2,1,0:T(8,128)} async-done(((f32[1,256,128]{2,1,0:T(8,128)}), f32[32,256,128]{2,1,0:T(8,128)}) %all-gather.14.cloned.1.call-update) | async-done | bytes 4194320 | tf_op jit(solution)/shard_map/all_gather | solution.py:502
  282.9 11.7 %cholesky.75 = f32[128,128]{1,0:T(8,128)S(1)} custom-call(f32[128,128]{1,0:T(8,128)S(1)} %bitcast_add_fusion.6), custom_call_target="Cholesky" | custom-call | tf_op jit(solution)/shard_map/jit(cholesky)/cholesky | solution.py:381
  295.9 9.8 %custom-call.8 = f32[1,128,128]{1,2,0:T(8,128)S(1)} custom-call(f32[1,128,128]{2,1,0:T(8,128)S(1)} %get-tuple-element.89), custom_call_target="InvertDiagBlocksLowerTriangular" | custom-call | tf_op jit(solution)/shard_map/jit(_solve_triangular)/triangular_solve | solution.py:382
  307.4 5.1 all-to-all-done.1
  312.5 7.6 %all-to-all-start.2 = ((f32[32,384,128]{2,1,0:T(8,128)}), f32[32,384,128]{2,1,0:T(8,128)}, u32[]{:S(2)}, u32[]{:S(2)}) async-start(f32[32,384,128]{2,1,0:T(8,128)} %bitcast.172), calls=%async_computation.2 | async-start | bytes 12582912 | tf_op jit(solution)/shard_map/all_to_all | solution.py:469
  321.1 10.9 %panel.6 = f32[3072,128]{1,0:T(8,128)} custom-call(s32[3072]{0:T(1024)} %copy-done.7, f32[2]{0:T(128)} %pad_maximum_fusion.11.weight_ref, f32[8,4,384,128]{3,2,1,0:T(8,128)} %bitcast.31.received_ref, bf16[512,128]{1,0:T(8,128)(2,1)} %slice.149.onehot_ref, f32[11264,512]{1,0:T(8,128)} %goce_hbm.9), custom_call_target="tpu_custom_call" | custom-call | flops 805306368 | bytes 30932992 | tf_op jit(solution)/shard_map/panel/pallas_call | solution.py:198
  336.4 1.4 copy.305.keep_ref
  341.4 11.7 %cholesky.86 = f32[128,128]{1,0:T(8,128)S(1)} custom-call(f32[128,128]{1,0:T(8,128)S(1)} %convolution_subtract_fusion.3), custom_call_target="Cholesky" | custom-call | tf_op jit(solution)/shard_map/jit(cholesky)/cholesky | solution.py:381
  354.5 9.8 %custom-call.9 = f32[1,128,128]{1,2,0:T(8,128)S(1)} custom-call(f32[1,128,128]{2,1,0:T(8,128)S(1)} %get-tuple-element.87), custom_call_target="InvertDiagBlocksLowerTriangular" | custom-call | tf_op jit(solution)/shard_map/jit(_solve_triangular)/triangular_solve | solution.py:382
  366.1 11.7 %cholesky.97 = f32[128,128]{1,0:T(8,128)S(1)} custom-call(f32[128,128]{1,0:T(8,128)S(1)} %convolution_subtract_fusion.2), custom_call_target="Cholesky" | custom-call | tf_op jit(solution)/shard_map/jit(cholesky)/cholesky | solution.py:381
  379.4 9.8 %custom-call.10 = f32[1,128,128]{1,2,0:T(8,128)S(1)} custom-call(f32[1,128,128]{2,1,0:T(8,128)S(1)} %get-tuple-element.85), custom_call_target="InvertDiagBlocksLowerTriangular" | custom-call | tf_op jit(solution)/shard_map/jit(_solve_triangular)/triangular_solve | solution.py:382
  392.7 11.7 %cholesky.108 = f32[128,128]{1,0:T(8,128)S(1)} custom-call(f32[128,128]{1,0:T(8,128)S(1)} %copy.297), custom_call_target="Cholesky" | custom-call | tf_op jit(solution)/shard_map/jit(cholesky)/cholesky | solution.py:381
  405.8 9.8 %custom-call.11 = f32[1,128,128]{1,2,0:T(8,128)S(1)} custom-call(f32[1,128,128]{2,1,0:T(8,128)S(1)} %get-tuple-element.83), custom_call_target="InvertDiagBlocksLowerTriangular" | custom-call | tf_op jit(solution)/shard_map/jit(_solve_triangular)/triangular_solve | solution.py:382
  419.4 2.1 gather_fusion.4
  424.8 1.9 fusion
  426.7 2.9 fusion.1
  429.6 10.1 %update.6 = f32[256,4,8,128]{3,2,1,0:T(8,128)} custom-call(f32[2]{0:T(128)} %pad_maximum_fusion.11.weight_ref, f32[8,4,256,128]{3,2,1,0:T(8,128)} %bitcast.20.received_ref, f32[4,2048,128]{2,1,0:T(8,128)} %bitcast.209, f32[2048,1]{1,0:T(8,128)} %copy.305.keep_ref, bf16[512,512]{1,0:T(8,128)(2,1)} %broadcast_select_fusion.onehot_ref, ...), custom_call_target="tpu_custom_call" | custom-call | flops 5368709120 | bytes 12582912 | tf_op jit(solution)/shard_map/update/pallas_call | solution.py:247
  439.7 9.2 %finish.5.base_hbm = f32[11264,512]{1,0:T(8,128)} custom-call(s32[16]{0:T(128)} %reshape_squeeze.15.bounds_ref, s32[11264]{0:T(1024)} %get-tuple-element.115.index_ref, f32[8192,128]{1,0:T(8,128)} %bitcast.177, f32[256,512]{1,0:T(8,128)} %bitcast_select_fusion.head_ref, f32[11264,512]{1,0:T(8,128)} %broadcast_multiply_fusion.base_hbm), custom_call_target="tpu_custom_call", output_to_operand_aliasing={{}: (4, {})} | custom-call | flops 2097152 | bytes 16777216 | tf_op jit(solution)/shard_map/finish/pallas_call | solution.py:338
  448.9 11.3 %all-to-all-done.2 = f32[32,384,128]{2,1,0:T(8,128)} async-done(((f32[32,384,128]{2,1,0:T(8,128)}), f32[32,384,128]{2,1,0:T(8,128)}, u32[]{:S(2)}, u32[]{:S(2)}) %all-to-all-start.2) | async-done | bytes 6291488 | tf_op jit(solution)/shard_map/all_to_all | solution.py:469
  460.2 10.9 %panel.7 = f32[3072,128]{1,0:T(8,128)} custom-call(s32[3072]{0:T(1024)} %copy-done.6, f32[2]{0:T(128)} %pad_maximum_fusion.11.weight_ref, f32[8,4,384,128]{3,2,1,0:T(8,128)} %bitcast.70.received_ref, bf16[512,128]{1,0:T(8,128)(2,1)} %slice.149.onehot_ref, f32[11264,512]{1,0:T(8,128)} %goce_hbm.9), custom_call_target="tpu_custom_call" | custom-call | flops 805306368 | bytes 30932992 | tf_op jit(solution)/shard_map/panel/pallas_call | solution.py:198
  471.1 5.6 all-to-all-start.3
  476.9 30.4 %all-gather.16.cloned.1.call-done = f32[12288,128]{1,0:T(8,128)} async-done(((f32[3072,128]{1,0:T(8,128)}), f32[12288,128]{1,0:T(8,128)}) %all-gather.16.cloned.1.call-update) | async-done | bytes 6291472 | tf_op jit(solution)/shard_map/all_gather | solution.py:494
  507.2 13.1 %update.5 = f32[384,4,8,128]{3,2,1,0:T(8,128)} custom-call(f32[2]{0:T(128)} %pad_maximum_fusion.11.weight_ref, f32[8,4,384,128]{3,2,1,0:T(8,128)} %bitcast.31.received_ref, f32[4,3072,128]{2,1,0:T(8,128)} %bitcast.207, f32[2048,1]{1,0:T(8,128)} %copy.305.keep_ref, bf16[512,512]{1,0:T(8,128)(2,1)} %broadcast_select_fusion.onehot_ref, ...), custom_call_target="tpu_custom_call" | custom-call | flops 8053063680 | bytes 18874368 | tf_op jit(solution)/shard_map/update/pallas_call | solution.py:247
  520.3 12.0 %finish.6.base_hbm = f32[11264,512]{1,0:T(8,128)} custom-call(s32[16]{0:T(128)} %reshape_squeeze.16.bounds_ref, s32[11264]{0:T(1024)} %get-tuple-element.117.index_ref, f32[12288,128]{1,0:T(8,128)} %bitcast.174, f32[256,512]{1,0:T(8,128)} %bitcast_select_fusion.head_ref, f32[11264,512]{1,0:T(8,128)} %finish.5.base_hbm), custom_call_target="tpu_custom_call", output_to_operand_aliasing={{}: (4, {})} | custom-call | flops 3145728 | bytes 25165824 | tf_op jit(solution)/shard_map/finish/pallas_call | solution.py:338
  532.3 39.1 %all-to-all-done.3 = f32[32,256,128]{2,1,0:T(8,128)} async-done(((f32[32,256,128]{2,1,0:T(8,128)}), f32[32,256,128]{2,1,0:T(8,128)}, u32[]{:S(2)}, u32[]{:S(2)}) %all-to-all-start.3) | async-done | bytes 4194336 | tf_op jit(solution)/shard_map/all_to_all | solution.py:469
  571.5 9.0 %panel.9 = f32[2048,128]{1,0:T(8,128)} custom-call(s32[2048]{0:T(1024)} %bitcast.193, f32[2]{0:T(128)} %pad_maximum_fusion.11.weight_ref, f32[8,4,256,128]{3,2,1,0:T(8,128)} %bitcast.71.received_ref, bf16[512,128]{1,0:T(8,128)(2,1)} %slice.149.onehot_ref, f32[11264,512]{1,0:T(8,128)} %goce_hbm.9), custom_call_target="tpu_custom_call" | custom-call | flops 536870912 | bytes 22544384 | tf_op jit(solution)/shard_map/panel/pallas_call | solution.py:198
  580.5 4.8 all-to-all-start.4
  585.4 29.0 %all-gather.20.cloned.1.call-done = f32[12288,128]{1,0:T(8,128)} async-done(((f32[3072,128]{1,0:T(8,128)}), f32[12288,128]{1,0:T(8,128)}) %all-gather.20.cloned.1.call-update) | async-done | bytes 6291472 | tf_op jit(solution)/shard_map/all_gather | solution.py:494
  614.4 13.3 %update.7 = f32[384,4,8,128]{3,2,1,0:T(8,128)} custom-call(f32[2]{0:T(128)} %pad_maximum_fusion.11.weight_ref, f32[8,4,384,128]{3,2,1,0:T(8,128)} %bitcast.70.received_ref, f32[4,3072,128]{2,1,0:T(8,128)} %bitcast.208, f32[2048,1]{1,0:T(8,128)} %copy.305.keep_ref, bf16[512,512]{1,0:T(8,128)(2,1)} %broadcast_select_fusion.onehot_ref, ...), custom_call_target="tpu_custom_call" | custom-call | flops 8053063680 | bytes 18874368 | tf_op jit(solution)/shard_map/update/pallas_call | solution.py:247
  627.7 12.0 %finish.7.base_hbm = f32[11264,512]{1,0:T(8,128)} custom-call(s32[16]{0:T(128)} %reshape_squeeze.17.bounds_ref, s32[11264]{0:T(1024)} %get-tuple-element.116.index_ref, f32[12288,128]{1,0:T(8,128)} %bitcast.175, f32[256,512]{1,0:T(8,128)} %bitcast_select_fusion.head_ref, f32[11264,512]{1,0:T(8,128)} %finish.6.base_hbm), custom_call_target="tpu_custom_call", output_to_operand_aliasing={{}: (4, {})} | custom-call | flops 3145728 | bytes 25165824 | tf_op jit(solution)/shard_map/finish/pallas_call | solution.py:338
  639.7 1.3 copy-done
  641.1 6.9 panel.8
  648.0 22.0 %all-gather.24.cloned.1.call-done = f32[8192,128]{1,0:T(8,128)} async-done(((f32[2048,128]{1,0:T(8,128)}), f32[8192,128]{1,0:T(8,128)}) %all-gather.24.cloned.1.call-update) | async-done | bytes 4194320 | tf_op jit(solution)/shard_map/all_gather | solution.py:494
  670.0 10.0 %update.9 = f32[256,4,8,128]{3,2,1,0:T(8,128)} custom-call(f32[2]{0:T(128)} %pad_maximum_fusion.11.weight_ref, f32[8,4,256,128]{3,2,1,0:T(8,128)} %bitcast.71.received_ref, f32[4,2048,128]{2,1,0:T(8,128)} %bitcast.210, f32[2048,1]{1,0:T(8,128)} %copy.305.keep_ref, bf16[512,512]{1,0:T(8,128)(2,1)} %broadcast_select_fusion.onehot_ref, ...), custom_call_target="tpu_custom_call" | custom-call | flops 5368709120 | bytes 12582912 | tf_op jit(solution)/shard_map/update/pallas_call | solution.py:247
  680.0 9.6 %finish.8.base_hbm = f32[11264,512]{1,0:T(8,128)} custom-call(s32[16]{0:T(128)} %reshape_squeeze.18.bounds_ref, s32[11264]{0:T(1024)} %get-tuple-element.114.index_ref, f32[8192,128]{1,0:T(8,128)} %bitcast.178, f32[256,512]{1,0:T(8,128)} %bitcast_select_fusion.head_ref, f32[11264,512]{1,0:T(8,128)} %finish.7.base_hbm), custom_call_target="tpu_custom_call", output_to_operand_aliasing={{}: (4, {})} | custom-call | flops 2097152 | bytes 16777216 | tf_op jit(solution)/shard_map/finish/pallas_call | solution.py:338
  689.6 17.6 %all-gather.22.cloned.1.call-done = f32[4096,128]{1,0:T(8,128)} async-done(((f32[1024,128]{1,0:T(8,128)}), f32[4096,128]{1,0:T(8,128)}) %all-gather.22.cloned.1.call-update) | async-done | bytes 2097168 | tf_op jit(solution)/shard_map/all_gather | solution.py:494
  707.2 7.0 update.8
  714.2 6.5 finish.9
  (214 shorter events, 48.3 us)
Async XLA Ops:
  6.5 120.8 %sort.50.cloned.1.call-start = ((), (), s32[]{:S(2)}) async-start(), calls=%async_computation.12 | async-start | bytes 24608 | tf_op jit(solution)/shard_map/jit(sort)/sort | solution.py:458
  34.4 7.5 %copy-start.1 = (s32[90112]{0:T(1024)S(1)}, s32[90112]{0:T(1024)}, u32[]{:S(2)}) copy-start(s32[90112]{0:T(1024)} %param.17) | copy-start | bytes 1081348
  34.5 8.4 %copy-start.21 = (s32[5]{0:T(128)S(1)}, s32[5]{0:T(128)}, u32[]{:S(2)}) copy-start(s32[5]{0:T(128)} %constant.527) | copy-start | bytes 64
  34.5 8.5 %copy-start.20 = (s32[5]{0:T(128)S(1)}, s32[5]{0:T(128)}, u32[]{:S(2)}) copy-start(s32[5]{0:T(128)} %constant.526) | copy-start | bytes 64
  34.5 109.9 %all-to-all-start = ((f32[32,256,128]{2,1,0:T(8,128)}), f32[32,256,128]{2,1,0:T(8,128)}, u32[]{:S(2)}, u32[]{:S(2)}) async-start(f32[32,256,128]{2,1,0:T(8,128)} %bitcast.169), calls=%async_computation | async-start | bytes 8388608 | tf_op jit(solution)/shard_map/all_to_all | solution.py:469
  41.9 87.2 %sort.48.cloned.1.call-start = ((), (), s32[]{:S(2)}) async-start(), calls=%async_computation.11 | async-start | bytes 1081376 | tf_op jit(solution)/shard_map/jit(sort)/sort | solution.py:451
  42.8 85.3 %copy-start.15 = (pred[512]{0:T(512)(128)(4,1)}, pred[512]{0:T(512)(128)(4,1)S(1)}, u32[]{:S(2)}) copy-start(pred[512]{0:T(512)(128)(4,1)S(1)} %broadcast_compare_fusion) | copy-start | bytes 1540
  130.4 14.7 %copy-start.4 = (s32[1,2,8,128]{3,1,2,0:T(2,128)}, s32[1,2,8,128]{3,1,2,0:T(2,128)S(1)}, u32[]{:S(2)}) copy-start(s32[1,2,8,128]{3,1,2,0:T(2,128)S(1)} %copy.330) | copy-start | bytes 24580
  130.5 14.6 %copy-start.7 = (s32[3072]{0:T(1024)}, s32[3072]{0:T(1024)S(1)}, u32[]{:S(2)}) copy-start(s32[3072]{0:T(1024)S(1)} %reshape.372.index_ref) | copy-start | bytes 36868
  130.6 14.5 %copy-start.6 = (s32[3072]{0:T(1024)}, s32[3072]{0:T(1024)S(1)}, u32[]{:S(2)}) copy-start(s32[3072]{0:T(1024)S(1)} %reshape.373.index_ref) | copy-start | bytes 36868
  130.7 14.4 %copy-start.8 = (s32[1,2,8,128]{3,1,2,0:T(2,128)}, s32[1,2,8,128]{3,1,2,0:T(2,128)S(1)}, u32[]{:S(2)}) copy-start(s32[1,2,8,128]{3,1,2,0:T(2,128)S(1)} %copy.331) | copy-start | bytes 24580
  130.8 14.3 %copy-start.12 = (s32[8,128]{1,0:T(8,128)}, s32[8,128]{1,0:T(8,128)S(1)}, u32[]{:S(2)}) copy-start(s32[8,128]{1,0:T(8,128)S(1)} %copy.264) | copy-start | bytes 12292
  145.1 167.4 %all-to-all-start.1 = ((f32[32,384,128]{2,1,0:T(8,128)}), f32[32,384,128]{2,1,0:T(8,128)}, u32[]{:S(2)}, u32[]{:S(2)}) async-start(f32[32,384,128]{2,1,0:T(8,128)} %bitcast.173), calls=%async_computation.1 | async-start | bytes 12582912 | tf_op jit(solution)/shard_map/all_to_all | solution.py:469
  154.0 127.8 %all-gather.14.cloned.1.call-start = ((), (), s32[]{:S(2)}) async-start(), calls=%async_computation.5 | async-start | bytes 4325376 | tf_op jit(solution)/shard_map/all_gather | solution.py:502
  166.4 263.3 %all-gather.18.cloned.1.call-start = ((), (), s32[]{:S(2)}) async-start(), calls=%async_computation.7 | async-start | bytes 5242880 | tf_op jit(solution)/shard_map/all_gather | solution.py:494
  312.5 147.7 %all-to-all-start.2 = ((f32[32,384,128]{2,1,0:T(8,128)}), f32[32,384,128]{2,1,0:T(8,128)}, u32[]{:S(2)}, u32[]{:S(2)}) async-start(f32[32,384,128]{2,1,0:T(8,128)} %bitcast.172), calls=%async_computation.2 | async-start | bytes 12582912 | tf_op jit(solution)/shard_map/all_to_all | solution.py:469
  320.1 187.1 %all-gather.16.cloned.1.call-start = ((), (), s32[]{:S(2)}) async-start(), calls=%async_computation.6 | async-start | bytes 7864320 | tf_op jit(solution)/shard_map/all_gather | solution.py:494
  321.1 15.3 %copy-start.5 = (s32[1,2,8,128]{3,1,2,0:T(2,128)S(1)}, s32[1,2,8,128]{3,1,2,0:T(2,128)}, u32[]{:S(2)}) copy-start(s32[1,2,8,128]{3,1,2,0:T(2,128)} %copy-done.4) | copy-start | bytes 24580
  332.1 282.3 %all-gather.20.cloned.1.call-start = ((), (), s32[]{:S(2)}) async-start(), calls=%async_computation.8 | async-start | bytes 7864320 | tf_op jit(solution)/shard_map/all_gather | solution.py:494
  416.6 0.6 copy-start.2
  418.4 5.4 copy-start.13
  418.4 5.4 copy-start.14
  418.4 5.4 copy-start.16
  418.4 5.4 copy-start.17
  419.2 3.1 copy-start.9
  419.2 3.7 copy-start.3
  419.2 3.7 copy-start.10
  419.2 4.7 copy-start.18
  419.2 4.7 copy-start.19
  419.2 5.6 copy-start.11
  471.1 100.3 %all-to-all-start.3 = ((f32[32,256,128]{2,1,0:T(8,128)}), f32[32,256,128]{2,1,0:T(8,128)}, u32[]{:S(2)}, u32[]{:S(2)}) async-start(f32[32,256,128]{2,1,0:T(8,128)} %bitcast.176), calls=%async_computation.3 | async-start | bytes 8388608 | tf_op jit(solution)/shard_map/all_to_all | solution.py:469
  476.8 193.2 %all-gather.24.cloned.1.call-start = ((), (), s32[]{:S(2)}) async-start(), calls=%async_computation.10 | async-start | bytes 5242880 | tf_op jit(solution)/shard_map/all_gather | solution.py:494
  580.5 59.2 %all-to-all-start.4 = ((f32[32,128,128]{2,1,0:T(8,128)}), f32[32,128,128]{2,1,0:T(8,128)S(1)}, u32[]{:S(2)}, u32[]{:S(2)}) async-start(f32[32,128,128]{2,1,0:T(8,128)} %bitcast.180), calls=%async_computation.4 | async-start | bytes 4194304 | tf_op jit(solution)/shard_map/all_to_all | solution.py:469
  585.3 121.9 %all-gather.22.cloned.1.call-start = ((), (), s32[]{:S(2)}) async-start(), calls=%async_computation.9 | async-start | bytes 2621440 | tf_op jit(solution)/shard_map/all_gather | solution.py:494
  639.7 1.3 copy-start
Sparse Core Ops, SparseCore 0:
  9.7 2.8 sort.54.cloned.1.call-done
  45.2 19.4 sort.52.cloned.1.call-done
  166.5 115.3 all-gather.13
  283.6 112.3 all-gather.17
  397.6 109.5 all-gather.15
  508.9 105.4 all-gather.19
  616.2 53.7 all-gather.23
  671.8 35.3 all-gather.21
  (2 shorter events, 0.0 us)

commit v2 on v1

v2 whole, which is shorter than its diff:
```python
import functools

import jax
import jax.numpy as jnp
from jax import lax
from jax.experimental import pallas as pl
from jax.experimental.pallas import tpu as pltpu
from jax.sharding import PartitionSpec as P

SLAB = 2048
PANEL = 512
BLOCK = 128
LANES = 128
SUBLANES = 8
LIGHT = pl.CostEstimate(flops=1, bytes_accessed=1, transcendentals=0)
HEAVY = pl.CostEstimate(flops=1, bytes_accessed=700_000_000, transcendentals=0)
VMEM_LIMIT = 56 * 1024 * 1024


def order_index(amount, device, groups, block_size):
    local = jnp.arange(amount, dtype=jnp.int32)
    return (local // block_size * groups + device) * block_size + local % block_size


def group_step(groups, width, most=1024):
    best = 1
    for size in range(1, groups + 1):
        if groups % size == 0 and size * width <= most:
            best = size
    return best


def chunk_widths(total, head):
    first = max(head, total * 7 // 22 // 16 * 16)
    second = min(total - first, total * 25 // 88) // 16 * 16
    return first, second, total - first - second


def row_view(array):
    rows, cols = array.shape
    tiles = cols // LANES
    shaped = array.reshape(rows // SUBLANES, SUBLANES, tiles, LANES)
    return shaped.transpose(0, 2, 1, 3).reshape(rows * tiles, LANES)


def view_base(index, tiles):
    return index // SUBLANES * (SUBLANES * tiles) + index % SUBLANES


def split(value):
    high = value.astype(jnp.bfloat16)
    low = (value - high.astype(jnp.float32)).astype(jnp.bfloat16)
    return high, low


def split_array(value):
    high = lax.reduce_precision(value, 8, 7)
    return high.astype(jnp.bfloat16), (value - high).astype(jnp.bfloat16)


def product(left, right):
    return jnp.dot(left, right, preferred_element_type=jnp.float32)


def copy_rows(index_ref, first, source, target, count, tiles, stride):
    def move(step, carry):
        for lane in range(SUBLANES):
            base = index_ref[first + step * SUBLANES + lane]
            target[pl.ds(step * SUBLANES * tiles + lane, tiles, stride=SUBLANES), :] = source[
                pl.ds(base, tiles, stride=stride), :
            ]
        return carry

    lax.fori_loop(0, count // SUBLANES, move, 0, unroll=4)


def from_view(value, rows, tiles):
    shaped = value.reshape(rows // SUBLANES, tiles, SUBLANES, LANES)
    return jnp.concatenate([shaped[:, t].reshape(rows, LANES) for t in range(tiles)], axis=1)


def pack_kernel(rows, tiles, index_ref, source_hbm, onehot_ref, *refs):
    outs, (held, picked, sem) = refs[:-3], refs[-3:]
    step = pl.program_id(0)

    @pl.when(step == 0)
    def _():
        copy = pltpu.make_async_copy(source_hbm, held, sem)
        copy.start()
        copy.wait()

    copy_rows(index_ref, step * rows, held, picked, rows, tiles, SUBLANES)
    high, low = split(from_view(picked[...], rows, tiles))
    places = [(out, None) for out in outs]
    if len(outs) == 1:
        places = [(outs[0], d) for d in range(outs[0].shape[1])]
    lanes = onehot_ref.shape[2]
    if lanes % LANES == 0:
        whole = jnp.concatenate([onehot_ref[d] for d in range(len(places))], axis=1)
        moved = product(high, whole) + product(low, whole)
        parts = [moved[:, d * lanes : (d + 1) * lanes] for d in range(len(places))]
    else:
        parts = [
            product(high, onehot_ref[d]) + product(low, onehot_ref[d]) for d in range(len(places))
        ]
    for part, (out, d) in zip(parts, places):
        if d is None:
            out[...] = part.reshape(out.shape)
        else:
            out[:, d] = part.reshape(out.shape[0], out.shape[2], lanes)


def pack(view, bases, onehot, row_devices, width, apart):
    col_devices, cols, group = onehot.shape
    tiles = cols // LANES
    groups = group_step(row_devices, width)
    rows = groups * width
    if apart:
        shapes = [jax.ShapeDtypeStruct((row_devices, width, group), jnp.float32)] * col_devices
        specs = [pl.BlockSpec((groups, width, group), lambda i: (i, 0, 0))] * col_devices
    else:
        shapes = [jax.ShapeDtypeStruct((row_devices, col_devices, width, group), jnp.float32)]
        specs = [pl.BlockSpec((groups, col_devices, width, group), lambda i: (i, 0, 0, 0))]
    return pl.pallas_call(
        functools.partial(pack_kernel, rows, tiles),
        out_shape=shapes,
        grid=(row_devices // groups,),
        in_specs=[
            pl.BlockSpec(memory_space=pltpu.SMEM),
            pl.BlockSpec(memory_space=pl.ANY),
            pl.BlockSpec(onehot.shape, lambda i: (0, 0, 0)),
        ],
        out_specs=specs,
        scratch_shapes=[
            pltpu.VMEM(view.shape, jnp.float32),
            pltpu.VMEM((rows * tiles, LANES), jnp.float32),
            pltpu.SemaphoreType.DMA,
        ],
        compiler_params=pltpu.CompilerParams(vmem_limit_bytes=VMEM_LIMIT),
        cost_estimate=LIGHT,
        name="pack",
    )(bases, view, onehot)


def place_columns(pieces, onehot_ref, rows):
    if len(pieces[0].shape) == 4:
        pieces = [pieces[0][:, c] for c in range(pieces[0].shape[1])]
    values = [piece[...].reshape(rows, piece.shape[-1]) for piece in pieces]
    if values[0].shape[1] % LANES == 0:
        high, low = split(jnp.concatenate(values, axis=1))
        whole = onehot_ref[...].reshape(high.shape[1], onehot_ref.shape[2])
        return product(high, whole) + product(low, whole)
    total = None
    for d, value in enumerate(values):
        high, low = split(value)
        part = product(high, onehot_ref[d]) + product(low, onehot_ref[d])
        total = part if total is None else total + part
    return total


def mix_kernel(rows, counts, onehot_ref, *refs):
    pieces, outs = refs[: -len(counts)], refs[-len(counts) :]
    moved = place_columns(pieces, onehot_ref, rows)
    tile = 0
    for count, out in zip(counts, outs):
        for t in range(count):
            part = moved[:, (tile + t) * LANES : (tile + t + 1) * LANES]
            out[:, t] = part.reshape(out.shape[0], out.shape[2], LANES)
        tile += count


def mix(pieces, onehot, counts):
    row_devices, width, lanes = pieces[0].shape
    groups = group_step(row_devices, width)
    rows = groups * width
    return pl.pallas_call(
        functools.partial(mix_kernel, rows, counts),
        out_shape=[
            jax.ShapeDtypeStruct((row_devices, count, width, LANES), jnp.float32) for count in counts
        ],
        grid=(row_devices // groups,),
        in_specs=[pl.BlockSpec(onehot.shape, lambda i: (0, 0, 0))]
        + [pl.BlockSpec((groups, width, lanes), lambda i: (i, 0, 0))] * len(pieces),
        out_specs=[
            pl.BlockSpec((groups, count, width, LANES), lambda i: (i, 0, 0, 0)) for count in counts
        ],
        compiler_params=pltpu.CompilerParams(vmem_limit_bytes=VMEM_LIMIT),
        cost_estimate=LIGHT,
        name="mix",
    )(onehot, *pieces)


def goce_rows_kernel(rows, index_ref, weight_ref, goce_hbm, out_ref, held, picked, sem):
    step = pl.program_id(0)

    @pl.when(step == 0)
    def _():
        copy = pltpu.make_async_copy(goce_hbm.at[:, pl.ds(0, BLOCK)], held, sem)
        copy.start()
        copy.wait()

    copy_rows(index_ref, step * rows, held, picked, rows, 1, 1)
    out_ref[...] = weight_ref[1] * picked[...]


def goce_rows(places, weights, goce, row_devices):
    total = places.shape[0]
    rows = total // row_devices * group_step(row_devices, total // row_devices)
    return pl.pallas_call(
        functools.partial(goce_rows_kernel, rows),
        out_shape=jax.ShapeDtypeStruct((total, BLOCK), jnp.float32),
        grid=(total // rows,),
        in_specs=[
            pl.BlockSpec(memory_space=pltpu.SMEM),
            pl.BlockSpec(memory_space=pltpu.SMEM),
            pl.BlockSpec(memory_space=pl.ANY),
        ],
        out_specs=pl.BlockSpec((rows, BLOCK), lambda i: (i, 0)),
        scratch_shapes=[
            pltpu.VMEM((goce.shape[0], BLOCK), jnp.float32),
            pltpu.VMEM((rows, BLOCK), jnp.float32),
            pltpu.SemaphoreType.DMA,
        ],
        compiler_params=pltpu.CompilerParams(vmem_limit_bytes=VMEM_LIMIT),
        cost_estimate=LIGHT,
        name="goce_rows",
    )(places, weights, goce)


def panel_kernel(rows, weight_ref, added_ref, onehot_ref, received_ref, out_ref):
    moved = place_columns([received_ref], onehot_ref, rows)
    out_ref[...] = weight_ref[0] * moved + added_ref[...]


def panel_part(received, added, weights, onehot):
    row_devices, width = received.shape[0], received.shape[2]
    groups = group_step(row_devices, width)
    rows = groups * width
    return pl.pallas_call(
        functools.partial(panel_kernel, rows),
        out_shape=jax.ShapeDtypeStruct((row_devices * width, BLOCK), jnp.float32),
        grid=(row_devices // groups,),
        in_specs=[
            pl.BlockSpec(memory_space=pltpu.SMEM),
            pl.BlockSpec((rows, BLOCK), lambda i: (i, 0)),
            pl.BlockSpec(onehot.shape, lambda i: (0, 0, 0)),
            pl.BlockSpec((groups,) + received.shape[1:], lambda i: (i, 0, 0, 0)),
        ],
        out_specs=pl.BlockSpec((rows, BLOCK), lambda i: (i, 0)),
        compiler_params=pltpu.CompilerParams(vmem_limit_bytes=VMEM_LIMIT),
        cost_estimate=HEAVY,
        name="panel",
    )(weights, added, onehot, received)


def update_kernel(rows, placed, parts, weight_ref, mask_ref, keep_ref, high_ref, low_ref, *refs):
    step = pl.program_id(0)
    raw_count = sum(count for _, _, count in parts)
    raws, arrays, out_ref = refs[:raw_count], refs[raw_count:-1], refs[-1]

    def compute(pieces):
        raw = jnp.concatenate(pieces, axis=1)
        if not placed:
            raw = raw * keep_ref[...]
        high, low = split(raw)
        total = product(high, high_ref[...]) + product(low, high_ref[...])
        total = total + product(high, low_ref[...])
        if placed:
            shape = arrays[0].shape
            tiles = [arrays[0][:, t].reshape(rows, LANES) for t in range(shape[1])]
        else:
            moved = place_columns(arrays[1:], arrays[0], rows)
            tiles = [moved[:, t * LANES : (t + 1) * LANES] for t in range(moved.shape[1] // LANES)]
        for t in range(total.shape[1] // LANES):
            lanes = slice(t * LANES, (t + 1) * LANES)
            part = total[:, lanes]
            if t < len(tiles):
                part = part + (weight_ref[0] * mask_ref[:, lanes]) * tiles[t]
            out_ref[:, t] = part.reshape(rows // SUBLANES, SUBLANES, LANES)

    used = 0
    for first, steps, count in parts:
        mine = raws[used : used + count]
        used += count

        @pl.when((step >= first) & (step < first + steps))
        def _():
            if count == 1:
                compute([mine[0][p] for p in range(high_ref.shape[0] // BLOCK)])
            else:
                compute([ref[...] for ref in mine])


def part_map(first, steps, step):
    return (jnp.clip(step - first, 0, steps - 1), 0)


def update_part(arrays, raw, keep, weights, mask, onehot, high, low):
    placed = onehot is None
    row_devices, width, lanes = arrays[0].shape[0], arrays[0].shape[-2], arrays[0].shape[-1]
    cols = high.shape[1]
    tiles = cols // LANES
    groups = group_step(row_devices, width)
    rows = groups * width
    total = row_devices * width
    if isinstance(raw, list):
        parts, raw_specs, flat, first = [], [], [], 0
        for pieces in raw:
            steps = pieces[0].shape[0] // rows
            parts.append((first, steps, len(pieces)))
            place = functools.partial(part_map, first, steps)
            raw_specs += [pl.BlockSpec((rows, BLOCK), place)] * len(pieces)
            flat += pieces
            first += steps
    else:
        parts = [(0, row_devices // groups, 1)]
        raw_specs = [pl.BlockSpec((high.shape[0] // BLOCK, rows, BLOCK), lambda i: (0, i, 0))]
        flat = [raw]
    if placed:
        specs = [pl.BlockSpec((groups,) + arrays[0].shape[1:], lambda i: (i, 0, 0, 0))]
    else:
        specs = [pl.BlockSpec((groups,) + arrays[0].shape[1:], lambda i: (i, 0, 0, 0))]
        specs = [pl.BlockSpec(onehot.shape, lambda i: (0, 0, 0))] + specs
        arrays = [onehot] + list(arrays)
    return pl.pallas_call(
        functools.partial(update_kernel, rows, placed, tuple(parts)),
        out_shape=jax.ShapeDtypeStruct((total // SUBLANES, tiles, SUBLANES, LANES), jnp.float32),
        grid=(row_devices // groups,),
        in_specs=[
            pl.BlockSpec(memory_space=pltpu.SMEM),
            pl.BlockSpec((1, cols), lambda i: (0, 0)),
            pl.BlockSpec((rows if not placed else SUBLANES, 1), lambda i: (0 if placed else i, 0)),
            pl.BlockSpec(high.shape, lambda i: (0, 0)),
            pl.BlockSpec(low.shape, lambda i: (0, 0)),
        ]
        + raw_specs
        + specs,
        out_specs=pl.BlockSpec((rows // SUBLANES, tiles, SUBLANES, LANES), lambda i: (i, 0, 0, 0)),
        compiler_params=pltpu.CompilerParams(vmem_limit_bytes=VMEM_LIMIT),
        cost_estimate=LIGHT,
        name="update",
    )(weights, mask, keep, high, low, *flat, *arrays).reshape(-1, LANES)


def finish_kernel(rows, tiles, lane, stride, weighted, has_head, bounds_ref, index_ref, weight_ref, part_hbm, head_ref, base_hbm, out_hbm, held, picked, before, after, part_sem, in_sem, out_sem):
    size = part_hbm.shape[0]
    first, last = bounds_ref[0], bounds_ref[1]
    for source in range(1, bounds_ref.shape[0] // 2):
        first = jnp.minimum(first, bounds_ref[2 * source])
        last = jnp.maximum(last, bounds_ref[2 * source + 1])
    first = first // rows
    steps = last // rows + 1 - first
    lanes = pl.ds(lane, tiles * LANES)

    def block(step):
        return pl.ds(pl.multiple_of((first + step) * rows, rows), rows)

    def fetch(step, slot):
        return pltpu.make_async_copy(out_hbm.at[block(step), lanes], before.at[slot], in_sem.at[slot])

    def store(step, slot):
        return pltpu.make_async_copy(after.at[slot], out_hbm.at[block(step), lanes], out_sem.at[slot])

    part_copy = pltpu.make_async_copy(part_hbm, held.at[pl.ds(0, size)], part_sem)
    part_copy.start()
    fetch(0, 0).start()
    held[pl.ds(size, held.shape[0] - size), :] = jnp.zeros((held.shape[0] - size, LANES), jnp.float32)
    part_copy.wait()

    def body(step, carry):
        slot = lax.rem(step, 2)

        @pl.when(step + 1 < steps)
        def _():
            fetch(step + 1, 1 - slot).start()

        copy_rows(index_ref, (first + step) * rows, held, picked, rows, tiles, stride)
        fetch(step, slot).wait()

        @pl.when(step >= 2)
        def _():
            store(step - 2, slot).wait()

        added = from_view(picked[...], rows, tiles)
        if weighted:
            added = weight_ref[0] * added
        after[slot] = before[slot] + added
        if has_head:

            @pl.when(step == 0)
            def _():
                count = head_ref.shape[0]
                after[0, :count] = after[0, :count] + head_ref[...]

        store(step, slot).start()
        return carry

    lax.fori_loop(0, steps, body, 0)

    @pl.when(steps >= 2)
    def _():
        store(steps - 2, lax.rem(steps, 2)).wait()

    store(steps - 1, lax.rem(steps + 1, 2)).wait()


def finish_part(base, part, bounds, local, count, weights, head, width, has_head):
    total, cols = base.shape
    tiles = cols // LANES
    rows = head.shape[0]
    while rows < 512 and total % (2 * rows) == 0:
        rows *= 2
    lane, stride = 0, SUBLANES
    index = view_base(local, tiles)
    if width:
        tiles -= 1
        lane, stride = LANES, width
        index = local // width * (width * tiles) + local % width
    index = jnp.where((local >= 0) & (local < count), index, part.shape[0])
    spare = -(-(stride * (tiles - 1) + 1) // SUBLANES) * SUBLANES
    return pl.pallas_call(
        functools.partial(finish_kernel, rows, tiles, lane, stride, bool(width), has_head),
        out_shape=jax.ShapeDtypeStruct((total, cols), jnp.float32),
        in_specs=[
            pl.BlockSpec(memory_space=pltpu.SMEM),
            pl.BlockSpec(memory_space=pltpu.SMEM),
            pl.BlockSpec(memory_space=pltpu.SMEM),
            pl.BlockSpec(memory_space=pl.ANY),
            pl.BlockSpec(memory_space=pltpu.VMEM),
            pl.BlockSpec(memory_space=pl.ANY),
        ],
        out_specs=pl.BlockSpec(memory_space=pl.ANY),
        scratch_shapes=[
            pltpu.VMEM((part.shape[0] + spare, LANES), jnp.float32),
            pltpu.VMEM((rows * tiles, LANES), jnp.float32),
            pltpu.VMEM((2, rows, tiles * LANES), jnp.float32),
            pltpu.VMEM((2, rows, tiles * LANES), jnp.float32),
            pltpu.SemaphoreType.DMA,
            pltpu.SemaphoreType.DMA((2,)),
            pltpu.SemaphoreType.DMA((2,)),
        ],
        input_output_aliases={5: 0},
        compiler_params=pltpu.CompilerParams(vmem_limit_bytes=VMEM_LIMIT),
        cost_estimate=LIGHT,
        name="finish",
    )(bounds, index, weights, part, head, base)


def precise(left, right):
    return jnp.dot(left, right, precision=lax.Precision.HIGHEST)


def cholesky_inverse(blocks, pause):
    count = len(blocks)
    size = blocks[0][0].shape[0]
    identity = jnp.eye(size, dtype=jnp.float32)
    factor, inverse = {}, {}
    for b in range(count):
        pivot = jnp.tril(blocks[b][b]) + jnp.tril(blocks[b][b], -1).T
        if b:
            left = jnp.concatenate([factor[b, k] for k in range(b)], axis=1)
            pivot = pivot - precise(left, left.T)
        factor[b, b] = jnp.linalg.cholesky(pivot, symmetrize_input=False)
        inverse[b, b] = jax.scipy.linalg.solve_triangular(factor[b, b], identity, lower=True)
        if b + 1 < count:
            below = jnp.concatenate([blocks[i][b] for i in range(b + 1, count)], axis=0)
            if b:
                rows = [
                    jnp.concatenate([factor[i, k] for k in range(b)], axis=1)
                    for i in range(b + 1, count)
                ]
                below = below - precise(jnp.concatenate(rows, axis=0), left.T)
            below = pause(b, precise(below, inverse[b, b].T))
            for i in range(b + 1, count):
                factor[i, b] = below[(i - b - 1) * size : (i - b) * size]
    zero = jnp.zeros((size, size), jnp.float32)
    for b in range(1, count):
        left = jnp.concatenate([factor[b, k] for k in range(b)], axis=1)
        above = [
            jnp.concatenate([inverse[k, j] if k >= j else zero for j in range(b)], axis=1)
            for k in range(b)
        ]
        solved = -precise(inverse[b, b], precise(left, jnp.concatenate(above, axis=0)))
        for j in range(b):
            inverse[b, j] = solved[:, j * size : (j + 1) * size]
    whole = [
        [
            jnp.concatenate([part[i, j] if i >= j else zero for j in range(count)], axis=1)
            for i in range(count)
        ]
        for part in (factor, inverse)
    ]
    return jnp.concatenate(whole[0], axis=0), jnp.concatenate(whole[1], axis=0)


def shards(
    grace_slab, goce_slab, grace_weight, goce_weight, kaula_prior, row_target, column_target
):
    row_devices = lax.axis_size("prow")
    col_devices = lax.axis_size("pcol")
    row_id = lax.axis_index("prow")
    col_id = lax.axis_index("pcol")
    rows_here, cols_here = grace_slab.shape
    tiles = cols_here // LANES
    row_group = rows_here // row_devices
    col_group = cols_here // col_devices
    per_device = SLAB // (BLOCK * row_devices)
    lead = per_device * BLOCK
    widths = chunk_widths(row_group, lead)
    starts = [sum(widths[:n]) for n in range(len(widths))]
    counts = [row_devices * width for width in widths]
    weights = jnp.concatenate([grace_weight, goce_weight])
    tie = lax.optimization_barrier

    bits = (rows_here - 1).bit_length()
    mask = (1 << bits) - 1
    local = jnp.arange(rows_here, dtype=jnp.int32)
    mine = lax.dynamic_slice_in_dim(row_target, row_id * rows_here, rows_here)
    sources = (jnp.sort(mine * (1 << bits) + local) & mask).reshape(row_devices, row_group)
    source_bases = view_base(sources, tiles)
    chunk_bases = [
        source_bases[:, start : start + width].reshape(-1) for start, width in zip(starts, widths)
    ]
    my_cols = lax.dynamic_slice_in_dim(column_target, col_id * cols_here, cols_here)
    col_ranks = jnp.sum((my_cols[None, :] < my_cols[:, None]).astype(jnp.int32), axis=1)
    distance = jnp.arange(col_devices, dtype=jnp.int32)
    group_iota = jnp.arange(col_group, dtype=jnp.int32)

    def column_onehot(owners):
        return (
            ((col_ranks // col_group)[None, :, None] == owners[:, None, None])
            & ((col_ranks % col_group)[None, :, None] == group_iota[None, None, :])
        ).astype(jnp.bfloat16)

    whole_onehot = column_onehot(distance)
    send_onehot = column_onehot(distance ^ col_id)

    def exchange(packet, axes, devices):
        sent = packet.reshape(devices, -1, packet.shape[-1])
        got = lax.all_to_all(sent, axes, split_axis=0, concat_axis=0, tiled=True)
        return got.reshape(packet.shape)

    def over_rows(packet):
        return exchange(packet, "prow", row_devices)

    def over_cols(pieces):
        got = [pieces[0]]
        for d in range(1, col_devices):
            pairs = [(i, i ^ d) for i in range(col_devices)]
            got.append(lax.ppermute(pieces[d], "pcol", pairs))
        return got

    view = row_view(grace_slab)
    (packet,) = pack(view, chunk_bases[0], whole_onehot, row_devices, widths[0], False)
    first_got = exchange(packet, ("prow", "pcol"), row_devices * col_devices)
    (chunk_bases[1], packet) = tie((chunk_bases[1], packet))
    second = over_cols(pack(view, chunk_bases[1], send_onehot, row_devices, widths[1], True))
    third = pack(view, chunk_bases[2], send_onehot, row_devices, widths[2], True)

    sorted_rows = jnp.sort(row_target.reshape(row_devices, rows_here), axis=1)
    places = lax.dynamic_slice_in_dim(sorted_rows, row_id * row_group, row_group, axis=1)
    places = places - row_id * rows_here
    chunk_places = [
        places[:, start : start + width].reshape(-1) for start, width in zip(starts, widths)
    ]
    ends = [
        jnp.stack([places[:, start], places[:, start + width - 1]], axis=-1).reshape(-1)
        for start, width in zip(starts, widths)
    ]
    positions = jnp.sort(jnp.concatenate(chunk_places) * (1 << bits) + local) & mask
    sorted_cols = jnp.sort(column_target.reshape(col_devices, cols_here), axis=1)
    col_targets = lax.dynamic_slice_in_dim(sorted_cols, col_id * col_group, col_group, axis=1)
    col_targets = col_targets - col_id * cols_here
    col_iota = jnp.arange(cols_here, dtype=jnp.int32)
    take_whole = (col_targets[:, :, None] == col_iota[None, None, :]).astype(jnp.bfloat16)
    take_onehot = jnp.take(take_whole, distance ^ col_id, axis=0)
    order_cols = order_index(cols_here, col_id, col_devices, BLOCK)
    in_panel = order_cols < PANEL
    outside = jnp.where(in_panel, 0.0, 1.0)[None, :].astype(jnp.float32)
    out = goce_slab * (goce_weight[0] * outside)

    added = [goce_rows(where, weights, goce_slab, row_devices) for where in chunk_places]

    second, third, added, ends, positions, take_onehot, take_whole, out = tie(
        (second, third, added, ends, positions, take_onehot, take_whole, out)
    )
    third = over_cols(third)
    (second_packet,) = mix(second, take_onehot, (tiles,))
    second_packet, first_got = tie((second_packet, first_got))
    second_got = over_rows(second_packet)
    panels = [panel_part(first_got, added[0], weights, take_whole[:, :, :BLOCK])]
    panel_blocks = PANEL // BLOCK
    my_lead = jnp.take(panels[0], positions[:lead], axis=0).reshape(per_device, BLOCK, BLOCK)
    lead_order = jnp.arange(per_device, dtype=jnp.int32) * row_devices + row_id
    my_diag = jnp.where(lead_order[:, None] == col_id, kaula_prior[None, :BLOCK], 0.0)
    my_lead = my_lead + my_diag[:, :, None] * jnp.eye(BLOCK, dtype=jnp.float32)
    lead_cols = lax.all_gather(my_lead, "prow", axis=0)
    lead_cols = lead_cols.transpose(1, 0, 2, 3).reshape(-1, BLOCK, BLOCK)
    outer = [n for n in range(tiles) if (n + 1) * col_devices > panel_blocks]
    lead_parts = []
    for d in range(col_devices):
        wanted = jnp.array(outer, dtype=jnp.int32) * col_devices + (col_id ^ d)
        lead_parts.append(
            jnp.concatenate([lead_cols[:panel_blocks], jnp.take(lead_cols, wanted, axis=0)], axis=0)
        )
    lead_all = jnp.take(jnp.stack(over_cols(lead_parts)), distance ^ col_id, axis=0)[:panel_blocks]

    third_packets = list(mix(third, take_onehot, (1, tiles - 1)))
    lead_all, third_packets = tie((lead_all, third_packets))
    blocks = [[lead_all[j, i] for j in range(i + 1)] for i in range(panel_blocks)]
    late = {}

    def pause(step, value):
        if step == 0:
            value, late["second"], packet = tie((value, second_got, third_packets[0]))
            late["panel"] = over_rows(packet)
        if step == panel_blocks - 2:
            value, late["panel"], packet = tie((value, late["panel"], third_packets[1]))
            late["rest"] = over_rows(packet)
        return value

    factor, inverse = cholesky_inverse(blocks, pause)
    second_got, third_panel, third_rest = late["second"], late["panel"], late["rest"]
    col_rows = []
    for n in range(tiles):
        if n in outer:
            rows = lead_all[:, panel_blocks + outer.index(n)]
            col_rows.append(rows.transpose(1, 0, 2).reshape(BLOCK, PANEL))
        else:
            col_rows.append(jnp.zeros((BLOCK, PANEL), jnp.float32))
    col_rows = jnp.concatenate(col_rows, axis=0)
    solved = precise(inverse, col_rows.T)
    panel_iota = jnp.arange(PANEL, dtype=jnp.int32)
    identity = (panel_iota[:, None] == order_cols[None, :]).astype(jnp.float32)
    matrix = precise(inverse.T, jnp.where(in_panel[None, :], identity, -solved))
    matrix_high, matrix_low = split_array(matrix)

    order_rows = order_index(lead, row_id, row_devices, BLOCK)
    on_diagonal = order_rows[:, None] == order_cols[None, :]
    known = jnp.take(
        jnp.take(factor, jnp.minimum(order_rows, PANEL - 1), axis=0),
        jnp.minimum(order_cols, PANEL - 1),
        axis=1,
    )
    in_block = (order_rows[:, None] < PANEL) & in_panel[None, :]
    head = jnp.where(in_block, known, jnp.where(on_diagonal, kaula_prior[None, :], 0.0))
    first = chunk_places[0]
    first_order = (first // BLOCK * row_devices + row_id) * BLOCK + first % BLOCK
    keep = jnp.where(first_order < PANEL, 0.0, 1.0)[:, None].astype(jnp.float32)

    panels[0], third = tie((panels[0], third))
    for n, got in ((1, second_got), (2, third_panel)):
        panels.append(grace_weight[0] * got[:, 0].reshape(-1, BLOCK) + added[n])
    raws = [lax.all_gather(panel, "pcol", axis=0) for panel in panels]
    arrays = [[first_got], [second_got], [third_panel]]
    offset = 0
    for n in range(len(widths)):
        part = update_part(
            arrays[n],
            raws[n],
            keep,
            weights,
            outside,
            take_whole if n == 0 else None,
            matrix_high,
            matrix_low,
        )
        out = finish_part(
            out, part, ends[n], positions - offset, counts[n], weights, head, 0, n == 0
        )
        offset += counts[n]
    out, third_rest = tie((out, third_rest))
    return finish_part(
        out,
        third_rest.reshape(-1, LANES),
        ends[-1],
        positions - (offset - counts[-1]),
        counts[-1],
        weights,
        head,
        widths[-1],
        False,
    )


def solution(mesh):
    return jax.shard_map(
        shards,
        mesh=mesh,
        in_specs=(P("prow", "pcol"), P("prow", "pcol"), P(), P(), P("pcol"), P(), P()),
        out_specs=P("prow", "pcol"),
        check_vma=False,
    )
```

time: 736 us -> 647 us (0.88)
  waiting for transfers between devices: 270 us -> 177 us
  blocking collectives: 29.9 us -> 0 us
  local copies, waits for them, and re-layouts: 27.4 us -> 36.8 us
  starting transfers between devices: 35.3 us -> 44.6 us
    all_gather x6 -> x4, waiting for transfers between devices: 214 us -> 18.6 us  [the longest x3 18.5 us: shards(): raws = [lax.all_gather(panel, 'pcol', axis=0) for panel in panels]]
    ppermute x0 -> x9, waiting for transfers between devices: none -> 145 us  [over_cols(): got.append(lax.ppermute(pieces[d], 'pcol', pairs))]
    pallas_call x12 -> x15, Pallas kernels: 153 us -> 197 us  [the longest x3 58 us: pack(): pl.pallas_call(functools.partial(pack_kernel, rows, tiles), out_shape=sha...]
    all_to_all x5 -> x4, waiting for transfers between devices: 55.5 us -> 13.6 us  [exchange(): got = lax.all_to_all(sent, axes, split_axis=0, concat_axis=0, tiled=True)]
    pallas_call x5 -> x1, Pallas kernels: 46.9 us -> 6.53 us  [panel_part(): pl.pallas_call(functools.partial(panel_kernel, rows), out_shape=jax.Shape...]
    all_gather x1 -> x0, blocking collectives: 29.9 us -> none  [shards(): all_kaula = lax.all_gather(kaula_prior[:BLOCK], 'pcol', axis=0)]
    ppermute x0 -> x9, starting transfers between devices: none -> 11.4 us  [over_cols(): got.append(lax.ppermute(pieces[d], 'pcol', pairs))]
    gather x5 -> x8, local copies, waits for them, and re-layouts: 3.24 us -> 14.6 us  [the longest x4 7.13 us: shards(): jnp.take(lead_cols, wanted, axis=0)]
  transfers between devices with their start and end apart: 11 -> 17, of which waited for: 8 -> 13; matrix products, arithmetic and copies ran while one was open for 22% -> 28% of each run, Pallas kernels for 24% -> 27%
where the time goes in v2:
time: 647 us; the launch traced here: 637 us
  Pallas kernels  203 us (31%)
  waiting for transfers between devices  177 us (27%)
  other arithmetic  145 us (22%)
  starting transfers between devices  44.6 us (7%)
  local copies, waits for them, and re-layouts  36.8 us (6%)
  between operations  16.2 us (3%)
  matrix products  14.1 us (2%)
    ppermute x9, waiting for transfers between devices, over_cols(): got.append(lax.ppermute(pieces[d], 'pcol', pairs))  145 us
    pallas_call x3, Pallas kernels, pack(): pl.pallas_call(functools.partial(pack_kernel, rows, tiles), out_shape=sha...  58 us
    pallas_call x4, Pallas kernels, finish_part(): pl.pallas_call(functools.partial(finish_kernel, rows, tiles, lane, stride...  53.4 us
    another operation x12, other arithmetic, cholesky_inverse(): factor[b, b] = jnp.linalg.cholesky(pivot, symmetrize_input=False)  49.7 us
    another operation x9, other arithmetic, cholesky_inverse(): jax.scipy.linalg.solve_triangular(factor[b, b], identity, lower=True)  41.9 us
    pallas_call x3, Pallas kernels, update_part(): pl.pallas_call(functools.partial(update_kernel, rows, placed, tuple(parts...  39 us
    all_to_all x4, starting transfers between devices, exchange(): got = lax.all_to_all(sent, axes, split_axis=0, concat_axis=0, tiled=True)  32.2 us
    pallas_call x3, Pallas kernels, goce_rows(): pl.pallas_call(functools.partial(goce_rows_kernel, rows), out_shape=jax.S...  26.4 us
  transfers between devices with their start and end apart: 17, of which 13 were waited for; matrix products, arithmetic and copies ran while one was open for 28% of the time, Pallas kernels for 27%

profile of v2, /device:TPU:0, one launch (start us, length us, event | category | flops | bytes accessed | tf_op | source)
XLA Modules:
  0.0 636.9 jit_solution(12463152637784915922)
XLA Ops:
  8.4 8.2 %sort.43 = (s32[11264]{0:T(1024)S(1)}, s32[11264]{0:T(1024)}) sort(s32[11264]{0:T(1024)S(1)} %iota_add_fusion, s32[11264]{0:T(1024)S(1)} %iota.228), dimensions={0}, to_apply=%region_0.0 | sort | flops 157696 | bytes 180224 | tf_op jit(solution)/shard_map/jit(sort)/sort | solution.py:519
  19.0 18.6 %pack.3 = f32[8,4,448,128]{3,2,1,0:T(8,128)} custom-call(s32[3584]{0:T(1024)} %reshape.674.index_ref, f32[45056,128]{1,0:T(8,128)} %bitcast.138, bf16[4,512,128]{2,1,0:T(8,128)(2,1)} %get-tuple-element.139.onehot_ref), custom_call_target="tpu_custom_call" | custom-call | flops 1 | bytes 1 | tf_op jit(solution)/shard_map/pack/pallas_call | solution.py:124
  37.7 7.4 %all-to-all-start = ((f32[32,448,128]{2,1,0:T(8,128)}), f32[32,448,128]{2,1,0:T(8,128)}, u32[]{:S(2)}, u32[]{:S(2)}) async-start(f32[32,448,128]{2,1,0:T(8,128)} %bitcast.142), calls=%async_computation | async-start | bytes 14680064 | tf_op jit(solution)/shard_map/all_to_all | solution.py:540
  46.7 17.9 %pack.4 = (f32[8,400,128]{2,1,0:T(8,128)}, f32[8,400,128]{2,1,0:T(8,128)}, f32[8,400,128]{2,1,0:T(8,128)}, f32[8,400,128]{2,1,0:T(8,128)}) custom-call(s32[3200]{0:T(1024)} %reshape.673.index_ref, f32[45056,128]{1,0:T(8,128)} %bitcast.139, bf16[4,512,128]{2,1,0:T(8,128)(2,1)} %get-tuple-element.138.onehot_ref), custom_call_target="tpu_custom_call" | custom-call | flops 1 | bytes 1 | tf_op jit(solution)/shard_map/pack/pallas_call | solution.py:124
  70.0 21.5 %pack.5 = (f32[8,560,128]{2,1,0:T(8,128)}, f32[8,560,128]{2,1,0:T(8,128)}, f32[8,560,128]{2,1,0:T(8,128)}, f32[8,560,128]{2,1,0:T(8,128)}) custom-call(s32[4480]{0:T(1024)} %reshape.677.index_ref, f32[45056,128]{1,0:T(8,128)} %bitcast.140, bf16[4,512,128]{2,1,0:T(8,128)(2,1)} %get-tuple-element.138.onehot_ref), custom_call_target="tpu_custom_call" | custom-call | flops 1 | bytes 1 | tf_op jit(solution)/shard_map/pack/pallas_call | solution.py:124
  93.5 16.1 %broadcast_multiply_fusion.base_hbm = f32[11264,512]{1,0:T(8,128)} fusion(f32[11264,512]{1,0:T(8,128)} %goce_hbm.5, f32[512]{0:T(512)S(1)} %select_multiply_fusion), kind=kLoop, calls=%fused_computation.9 | loop fusion | flops 5767168 | bytes 46139392 | tf_op jit(solution)/shard_map/mul | solution.py:580
  115.0 8.0 %goce_rows.4 = f32[3200,128]{1,0:T(8,128)} custom-call(s32[3200]{0:T(1024)} %reshape.680.index_ref, f32[2]{0:T(128)} %pad_maximum_fusion.16.weight_ref, f32[11264,512]{1,0:T(8,128)} %goce_hbm.5), custom_call_target="tpu_custom_call" | custom-call | flops 1 | bytes 1 | tf_op jit(solution)/shard_map/goce_rows/pallas_call | solution.py:209
  123.0 8.5 %goce_rows.3.added_ref = f32[3584,128]{1,0:T(8,128)} custom-call(s32[3584]{0:T(1024)} %reshape.679.index_ref, f32[2]{0:T(128)} %pad_maximum_fusion.16.weight_ref, f32[11264,512]{1,0:T(8,128)} %goce_hbm.5), custom_call_target="tpu_custom_call" | custom-call | flops 1 | bytes 1 | tf_op jit(solution)/shard_map/goce_rows/pallas_call | solution.py:209
  131.6 9.8 %goce_rows.5 = f32[4480,128]{1,0:T(8,128)} custom-call(s32[4480]{0:T(1024)} %reshape.681.index_ref, f32[2]{0:T(128)} %pad_maximum_fusion.16.weight_ref, f32[11264,512]{1,0:T(8,128)} %goce_hbm.5), custom_call_target="tpu_custom_call" | custom-call | flops 1 | bytes 1 | tf_op jit(solution)/shard_map/goce_rows/pallas_call | solution.py:209
  143.5 8.2 %sort.45 = (s32[11264]{0:T(1024)S(1)}, s32[11264]{0:T(1024)}) sort(s32[11264]{0:T(1024)S(1)} %fusion.92, s32[11264]{0:T(1024)S(1)} %iota.231), dimensions={0}, to_apply=%region_3.4 | sort | flops 157696 | bytes 180224 | tf_op jit(solution)/shard_map/jit(sort)/sort | solution.py:570
  153.3 11.5 %collective-permute-done.1.refs_2_ = f32[8,400,128]{2,1,0:T(8,128)} collective-permute-done((f32[8,400,128]{2,1,0:T(8,128)}, f32[8,400,128]{2,1,0:T(8,128)}, u32[]{:S(2)}, u32[]{:S(2)}) %collective-permute-start.1) | collective-permute-done | bytes 1638432 | tf_op jit(solution)/shard_map/ppermute | solution.py:550
  164.8 37.2 %collective-permute-done.2.refs_3_ = f32[8,400,128]{2,1,0:T(8,128)} collective-permute-done((f32[8,400,128]{2,1,0:T(8,128)}, f32[8,400,128]{2,1,0:T(8,128)}, u32[]{:S(2)}, u32[]{:S(2)}) %collective-permute-start.2) | collective-permute-done | bytes 1638432 | tf_op jit(solution)/shard_map/ppermute | solution.py:550
  202.0 2.4 collective-permute-start.6
  205.9 8.2 %mix.2 = f32[8,4,400,128]{3,2,1,0:T(8,128)} custom-call(bf16[4,128,512]{2,1,0:T(8,128)(2,1)} %broadcast_select_fusion.1.onehot_ref, f32[8,400,128]{2,1,0:T(8,128)} %get-tuple-element.71.refs_0_, f32[8,400,128]{2,1,0:T(8,128)} %copy-done.6, f32[8,400,128]{2,1,0:T(8,128)} %collective-permute-done.1.refs_2_, f32[8,400,128]{2,1,0:T(8,128)} %collective-permute-done.2.refs_3_), custom_call_target="tpu_custom_call" | custom-call | flops 1 | bytes 1 | tf_op jit(solution)/shard_map/mix/pallas_call | solution.py:176
  216.2 6.5 %panel.1 = f32[3584,128]{1,0:T(8,128)} custom-call(f32[2]{0:T(128)} %pad_maximum_fusion.16.weight_ref, f32[3584,128]{1,0:T(8,128)} %goce_rows.3.added_ref, bf16[4,128,128]{2,1,0:T(8,128)(2,1)} %slice.147.onehot_ref, f32[8,4,448,128]{3,2,1,0:T(8,128)} %bitcast.9.received_ref.refs_2_), custom_call_target="tpu_custom_call" | custom-call | flops 1 | bytes 700000000 | tf_op jit(solution)/shard_map/panel/pallas_call | solution.py:239
  222.7 2.2 gather_fusion.1
  225.7 7.7 %all-to-all-start.1 = ((f32[8,1600,128]{2,1,0:T(8,128)}), f32[8,1600,128]{2,1,0:T(8,128)}, u32[]{:S(2)}, u32[]{:S(2)}) async-start(f32[8,1600,128]{2,1,0:T(8,128)} %bitcast.144), calls=%async_computation.1 | async-start | bytes 13107200 | tf_op jit(solution)/shard_map/all_to_all | solution.py:540
  233.5 24.0 %collective-permute-done.6.refs_1_ = f32[8,560,128]{2,1,0:T(8,128)S(1)} collective-permute-done((f32[8,560,128]{2,1,0:T(8,128)}, f32[8,560,128]{2,1,0:T(8,128)S(1)}, u32[]{:S(2)}, u32[]{:S(2)}) %collective-permute-start.6) | collective-permute-done | bytes 2293792 | tf_op jit(solution)/shard_map/ppermute | solution.py:550
  257.5 47.1 %collective-permute-done.7.refs_2_ = f32[8,560,128]{2,1,0:T(8,128)} collective-permute-done((f32[8,560,128]{2,1,0:T(8,128)}, f32[8,560,128]{2,1,0:T(8,128)}, u32[]{:S(2)}, u32[]{:S(2)}) %collective-permute-start.7) | collective-permute-done | bytes 2293792 | tf_op jit(solution)/shard_map/ppermute | solution.py:550
  314.3 3.9 collective-permute-start.4
  318.2 11.8 %mix.3 = (f32[8,1,560,128]{3,2,1,0:T(8,128)}, f32[8,3,560,128]{3,2,1,0:T(8,128)}) custom-call(bf16[4,128,512]{2,1,0:T(8,128)(2,1)} %broadcast_select_fusion.1.onehot_ref, f32[8,560,128]{2,1,0:T(8,128)} %get-tuple-element.76.refs_0_, f32[8,560,128]{2,1,0:T(8,128)} %copy-done.5, f32[8,560,128]{2,1,0:T(8,128)} %collective-permute-done.7.refs_2_, ...), custom_call_target="tpu_custom_call" | custom-call | flops 1 | bytes 1 | tf_op jit(solution)/shard_map/mix/pallas_call | solution.py:176
  330.0 4.1 collective-permute-done.3
  334.2 8.8 %collective-permute-done.4 = f32[7,128,128]{2,1,0:T(8,128)S(1)} collective-permute-done((f32[7,128,128]{2,1,0:T(8,128)S(1)}, f32[7,128,128]{2,1,0:T(8,128)S(1)}, u32[]{:S(2)}, u32[]{:S(2)}) %collective-permute-start.4) | collective-permute-done | bytes 458784 | tf_op jit(solution)/shard_map/ppermute | solution.py:550
  343.0 10.3 %collective-permute-done.5 = f32[7,128,128]{2,1,0:T(8,128)S(1)} collective-permute-done((f32[7,128,128]{2,1,0:T(8,128)S(1)}, f32[7,128,128]{2,1,0:T(8,128)S(1)}, u32[]{:S(2)}, u32[]{:S(2)}) %collective-permute-start.5) | collective-permute-done | bytes 458784 | tf_op jit(solution)/shard_map/ppermute | solution.py:550
  355.3 2.8 copy.152
  363.6 11.7 %cholesky.75 = f32[128,128]{1,0:T(8,128)S(1)} custom-call(f32[128,128]{1,0:T(8,128)S(1)} %bitcast_add_fusion.5), custom_call_target="Cholesky" | custom-call | tf_op jit(solution)/shard_map/jit(cholesky)/cholesky | solution.py:463
  376.7 9.8 %custom-call.8 = f32[1,128,128]{1,2,0:T(8,128)S(1)} custom-call(f32[1,128,128]{2,1,0:T(8,128)S(1)} %get-tuple-element.106), custom_call_target="InvertDiagBlocksLowerTriangular" | custom-call | tf_op jit(solution)/shard_map/jit(_solve_triangular)/triangular_solve | solution.py:464
  390.3 12.2 %all-to-all-start.2 = ((f32[8,560,128]{2,1,0:T(8,128)}), f32[8,560,128]{2,1,0:T(8,128)S(1)}, u32[]{:S(2)}, u32[]{:S(2)}) async-start(f32[8,560,128]{2,1,0:T(8,128)} %bitcast.152), calls=%async_computation.2 | async-start | bytes 4587520 | tf_op jit(solution)/shard_map/all_to_all | solution.py:540
  404.1 11.7 %cholesky.86 = f32[128,128]{1,0:T(8,128)S(1)} custom-call(f32[128,128]{1,0:T(8,128)S(1)} %convolution_subtract_fusion.3), custom_call_target="Cholesky" | custom-call | tf_op jit(solution)/shard_map/jit(cholesky)/cholesky | solution.py:463
  417.0 9.8 %custom-call.9 = f32[1,128,128]{1,2,0:T(8,128)S(1)} custom-call(f32[1,128,128]{2,1,0:T(8,128)S(1)} %get-tuple-element.104), custom_call_target="InvertDiagBlocksLowerTriangular" | custom-call | tf_op jit(solution)/shard_map/jit(_solve_triangular)/triangular_solve | solution.py:464
  429.0 11.7 %cholesky.97 = f32[128,128]{1,0:T(8,128)S(1)} custom-call(f32[128,128]{1,0:T(8,128)S(1)} %convolution_subtract_fusion.2), custom_call_target="Cholesky" | custom-call | tf_op jit(solution)/shard_map/jit(cholesky)/cholesky | solution.py:463
  441.9 10.0 %custom-call.10 = f32[1,128,128]{1,2,0:T(8,128)S(1)} custom-call(f32[1,128,128]{2,1,0:T(8,128)S(1)} %get-tuple-element.102), custom_call_target="InvertDiagBlocksLowerTriangular" | custom-call | tf_op jit(solution)/shard_map/jit(_solve_triangular)/triangular_solve | solution.py:464
  453.6 2.2 all-to-all-done.2
  459.9 4.8 all-to-all-start.3
  467.4 3.1 fusion.9.keep_ref
  475.3 11.7 %cholesky.108 = f32[128,128]{1,0:T(8,128)S(1)} custom-call(f32[128,128]{1,0:T(8,128)S(1)} %copy.173), custom_call_target="Cholesky" | custom-call | tf_op jit(solution)/shard_map/jit(cholesky)/cholesky | solution.py:463
  488.4 9.8 %custom-call.11 = f32[1,128,128]{1,2,0:T(8,128)S(1)} custom-call(f32[1,128,128]{2,1,0:T(8,128)S(1)} %get-tuple-element.100), custom_call_target="InvertDiagBlocksLowerTriangular" | custom-call | tf_op jit(solution)/shard_map/jit(_solve_triangular)/triangular_solve | solution.py:464
  499.5 2.1 fusion.10
  501.6 2.9 fusion.11
  504.5 14.7 %update.5 = f32[448,4,8,128]{3,2,1,0:T(8,128)} custom-call(f32[2]{0:T(128)} %pad_maximum_fusion.16.weight_ref, f32[1,512]{1,0:T(1,128)} %compare_select_fusion.1.mask_ref, f32[3584,1]{1,0:T(8,128)} %fusion.9.keep_ref, bf16[512,512]{1,0:T(8,128)(2,1)} %get-tuple-element.128.high_ref, bf16[512,512]{1,0:T(8,128)(2,1)} %get-tuple-element.127.low_ref, ...), custom_call_target="tpu_custom_call" | custom-call | flops 1 | bytes 1 | tf_op jit(solution)/shard_map/update/pallas_call | solution.py:325
  523.4 13.5 %finish.4.base_hbm = f32[11264,512]{1,0:T(8,128)} custom-call(s32[16]{0:T(128)} %reshape.682.bounds_ref, s32[11264]{0:T(1024)} %get-tuple-element.140.index_ref, f32[2]{0:T(128)} %pad_maximum_fusion.16.weight_ref, f32[14336,128]{1,0:T(8,128)} %bitcast.143, f32[256,512]{1,0:T(8,128)} %bitcast_select_fusion.head_ref, ...), custom_call_target="tpu_custom_call", output_to_operand_aliasing={{}: (5, {})} | custom-call | flops 1 | bytes 1 | tf_op jit(solution)/shard_map/finish/pallas_call | solution.py:421
  536.9 10.6 %update.4 = f32[400,4,8,128]{3,2,1,0:T(8,128)} custom-call(f32[2]{0:T(128)} %pad_maximum_fusion.16.weight_ref, f32[1,512]{1,0:T(1,128)} %compare_select_fusion.1.mask_ref, f32[3584,1]{1,0:T(8,128)} %fusion.9.keep_ref, bf16[512,512]{1,0:T(8,128)(2,1)} %get-tuple-element.128.high_ref, bf16[512,512]{1,0:T(8,128)(2,1)} %get-tuple-element.127.low_ref, ...), custom_call_target="tpu_custom_call" | custom-call | flops 1 | bytes 1 | tf_op jit(solution)/shard_map/update/pallas_call | solution.py:325
  547.5 12.1 %finish.5.base_hbm = f32[11264,512]{1,0:T(8,128)} custom-call(s32[16]{0:T(128)} %reshape.683.bounds_ref, s32[11264]{0:T(1024)} %get-tuple-element.142.index_ref, f32[2]{0:T(128)} %pad_maximum_fusion.16.weight_ref, f32[12800,128]{1,0:T(8,128)} %bitcast.145, f32[256,512]{1,0:T(8,128)} %bitcast_select_fusion.head_ref, ...), custom_call_target="tpu_custom_call", output_to_operand_aliasing={{}: (5, {})} | custom-call | flops 1 | bytes 1 | tf_op jit(solution)/shard_map/finish/pallas_call | solution.py:421
  559.6 18.5 %all-gather.10.cloned.1.call-done = f32[17920,128]{1,0:T(8,128)} async-done(((f32[4480,128]{1,0:T(8,128)}), f32[17920,128]{1,0:T(8,128)}) %all-gather.10.cloned.1.call-update) | async-done | bytes 9175056 | tf_op jit(solution)/shard_map/all_gather | solution.py:654
  578.1 13.6 %update.3 = f32[560,4,8,128]{3,2,1,0:T(8,128)} custom-call(f32[2]{0:T(128)} %pad_maximum_fusion.16.weight_ref, f32[1,512]{1,0:T(1,128)} %compare_select_fusion.1.mask_ref, f32[3584,1]{1,0:T(8,128)} %fusion.9.keep_ref, bf16[512,512]{1,0:T(8,128)(2,1)} %get-tuple-element.128.high_ref, bf16[512,512]{1,0:T(8,128)(2,1)} %get-tuple-element.127.low_ref, ...), custom_call_target="tpu_custom_call" | custom-call | flops 1 | bytes 1 | tf_op jit(solution)/shard_map/update/pallas_call | solution.py:325
  591.7 14.6 %finish.6.base_hbm = f32[11264,512]{1,0:T(8,128)} custom-call(s32[16]{0:T(128)} %reshape.684.bounds_ref, s32[11264]{0:T(1024)} %get-tuple-element.143.index_ref, f32[2]{0:T(128)} %pad_maximum_fusion.16.weight_ref, f32[17920,128]{1,0:T(8,128)} %bitcast.141, f32[256,512]{1,0:T(8,128)} %bitcast_select_fusion.head_ref, ...), custom_call_target="tpu_custom_call", output_to_operand_aliasing={{}: (5, {})} | custom-call | flops 1 | bytes 1 | tf_op jit(solution)/shard_map/finish/pallas_call | solution.py:421
  606.4 10.0 %all-to-all-done.3 = f32[8,1680,128]{2,1,0:T(8,128)} async-done(((f32[8,1680,128]{2,1,0:T(8,128)}), f32[8,1680,128]{2,1,0:T(8,128)}, u32[]{:S(2)}, u32[]{:S(2)}) %all-to-all-start.3) | async-done | bytes 6881312 | tf_op jit(solution)/shard_map/all_to_all | solution.py:540
  616.4 13.2 %finish.7 = f32[11264,512]{1,0:T(8,128)} custom-call(s32[16]{0:T(128)} %reshape.684.bounds_ref, s32[11264]{0:T(1024)} %get-tuple-element.141.index_ref, f32[2]{0:T(128)} %pad_maximum_fusion.16.weight_ref, f32[13440,128]{1,0:T(8,128)} %bitcast.68.part_hbm, f32[256,512]{1,0:T(8,128)} %bitcast_select_fusion.head_ref, ...), custom_call_target="tpu_custom_call", output_to_operand_aliasing={{}: (5, {})} | custom-call | flops 1 | bytes 1 | tf_op jit(solution)/shard_map/finish/pallas_call | solution.py:421
  (204 shorter events, 73.4 us)
Async XLA Ops:
  37.7 7.5 %copy-start.11 = (s32[2048]{0:T(1024)S(1)}, s32[2048]{0:T(1024)}, u32[]{:S(2)}) copy-start(s32[2048]{0:T(1024)} %param.22) | copy-start | bytes 24580
  37.7 178.5 %all-to-all-start = ((f32[32,448,128]{2,1,0:T(8,128)}), f32[32,448,128]{2,1,0:T(8,128)}, u32[]{:S(2)}, u32[]{:S(2)}) async-start(f32[32,448,128]{2,1,0:T(8,128)} %bitcast.142), calls=%async_computation | async-start | bytes 14680064 | tf_op jit(solution)/shard_map/all_to_all | solution.py:540
  45.1 64.5 %sort.50.cloned.1.call-start = ((), (), s32[]{:S(2)}) async-start(), calls=%async_computation.9 | async-start | bytes 24608 | tf_op jit(solution)/shard_map/jit(sort)/sort | solution.py:571
  45.9 65.2 %sort.48.cloned.1.call-start = ((), (), s32[]{:S(2)}) async-start(), calls=%async_computation.8 | async-start | bytes 1081376 | tf_op jit(solution)/shard_map/jit(sort)/sort | solution.py:560
  46.7 21.5 %copy-start.7 = (s32[90112]{0:T(1024)S(1)}, s32[90112]{0:T(1024)}, u32[]{:S(2)}) copy-start(s32[90112]{0:T(1024)} %param.21) | copy-start | bytes 1081348
  64.6 88.7 %collective-permute-start = (f32[8,400,128]{2,1,0:T(8,128)}, f32[8,400,128]{2,1,0:T(8,128)S(1)}, u32[]{:S(2)}, u32[]{:S(2)}) collective-permute-start(f32[8,400,128]{2,1,0:T(8,128)} %get-tuple-element.58), channel_id=1, source_target_pairs={{0,1},{1,0},{2,3},{3,2},{4,5},{5,4},{6,7},{7,6},{8,9},{9,8},{10,11... | collective-permute-start | bytes 4915208 | tf_op jit(solution)/shard_map/ppermute | solution.py:550
  66.3 98.5 %collective-permute-start.1 = (f32[8,400,128]{2,1,0:T(8,128)}, f32[8,400,128]{2,1,0:T(8,128)}, u32[]{:S(2)}, u32[]{:S(2)}) collective-permute-start(f32[8,400,128]{2,1,0:T(8,128)} %get-tuple-element.59), channel_id=1, source_target_pairs={{0,2},{1,3},{2,0},{3,1},{4,6},{5,7},{6,4},{7,5},{8,10},{9,11},{10,... | collective-permute-start | bytes 4915208 | tf_op jit(solution)/shard_map/ppermute | solution.py:550
  67.8 134.2 %collective-permute-start.2 = (f32[8,400,128]{2,1,0:T(8,128)}, f32[8,400,128]{2,1,0:T(8,128)}, u32[]{:S(2)}, u32[]{:S(2)}) collective-permute-start(f32[8,400,128]{2,1,0:T(8,128)} %get-tuple-element.60), channel_id=1, source_target_pairs={{0,3},{1,2},{2,1},{3,0},{4,7},{5,6},{6,5},{7,4},{8,11},{9,10},{10,... | collective-permute-start | bytes 4915208 | tf_op jit(solution)/shard_map/ppermute | solution.py:550
  69.7 23.8 %slice-start = ((f32[512]{0:T(512)}), f32[128]{0:T(128)S(1)}, s32[]{:S(2)}) async-start(f32[512]{0:T(512)} %param.20), calls=%async_computation.12 | async-start | bytes 1024 | tf_op jit(solution)/shard_map/slice | solution.py:595
  69.7 235.7 %all-gather.8.cloned.1.call-start = ((), (), s32[]{:S(2)}) async-start(), calls=%async_computation.4 | async-start | bytes 1179648 | tf_op jit(solution)/shard_map/all_gather | solution.py:597
  110.4 103.7 %copy-start.4 = (bf16[4,128,512]{2,1,0:T(8,128)(2,1)}, bf16[4,128,512]{2,1,0:T(8,128)(2,1)S(1)}, u32[]{:S(2)}) copy-start(bf16[4,128,512]{2,1,0:T(8,128)(2,1)S(1)} %fusion.24.refs_1_) | copy-start | bytes 1572868
  131.5 12.0 %copy-start.8 = (s32[4480]{0:T(1024)S(1)}, s32[4480]{0:T(1024)}, u32[]{:S(2)}) copy-start(s32[4480]{0:T(1024)} %reshape.681.index_ref) | copy-start | bytes 53764
  131.5 12.0 %copy-start.9 = (s32[3584]{0:T(1024)S(1)}, s32[3584]{0:T(1024)}, u32[]{:S(2)}) copy-start(s32[3584]{0:T(1024)} %reshape.679.index_ref) | copy-start | bytes 43012
  131.5 12.0 %copy-start.10 = (s32[3200]{0:T(1024)S(1)}, s32[3200]{0:T(1024)}, u32[]{:S(2)}) copy-start(s32[3200]{0:T(1024)} %reshape.680.index_ref) | copy-start | bytes 38404
  153.3 48.7 %copy-start.6 = (f32[8,400,128]{2,1,0:T(8,128)}, f32[8,400,128]{2,1,0:T(8,128)S(1)}, u32[]{:S(2)}) copy-start(f32[8,400,128]{2,1,0:T(8,128)S(1)} %collective-permute-done.refs_1_) | copy-start | bytes 4915204
  202.0 55.5 %collective-permute-start.6 = (f32[8,560,128]{2,1,0:T(8,128)}, f32[8,560,128]{2,1,0:T(8,128)S(1)}, u32[]{:S(2)}, u32[]{:S(2)}) collective-permute-start(f32[8,560,128]{2,1,0:T(8,128)} %get-tuple-element.77), channel_id=1, source_target_pairs={{0,1},{1,0},{2,3},{3,2},{4,5},{5,4},{6,7},{7,6},{8,9},{9,8},{10,11... | collective-permute-start | bytes 6881288 | tf_op jit(solution)/shard_map/ppermute | solution.py:550
  204.4 100.2 %collective-permute-start.7 = (f32[8,560,128]{2,1,0:T(8,128)}, f32[8,560,128]{2,1,0:T(8,128)}, u32[]{:S(2)}, u32[]{:S(2)}) collective-permute-start(f32[8,560,128]{2,1,0:T(8,128)} %get-tuple-element.78), channel_id=1, source_target_pairs={{0,2},{1,3},{2,0},{3,1},{4,6},{5,7},{6,4},{7,5},{8,10},{9,11},{10,... | collective-permute-start | bytes 6881288 | tf_op jit(solution)/shard_map/ppermute | solution.py:550
  204.4 100.5 %collective-permute-start.8 = (f32[8,560,128]{2,1,0:T(8,128)}, f32[8,560,128]{2,1,0:T(8,128)}, u32[]{:S(2)}, u32[]{:S(2)}) collective-permute-start(f32[8,560,128]{2,1,0:T(8,128)} %get-tuple-element.79), channel_id=1, source_target_pairs={{0,3},{1,2},{2,1},{3,0},{4,7},{5,6},{6,5},{7,4},{8,11},{9,10},{10,... | collective-permute-start | bytes 6881288 | tf_op jit(solution)/shard_map/ppermute | solution.py:550
  225.7 161.6 %all-to-all-start.1 = ((f32[8,1600,128]{2,1,0:T(8,128)}), f32[8,1600,128]{2,1,0:T(8,128)}, u32[]{:S(2)}, u32[]{:S(2)}) async-start(f32[8,1600,128]{2,1,0:T(8,128)} %bitcast.144), calls=%async_computation.1 | async-start | bytes 13107200 | tf_op jit(solution)/shard_map/all_to_all | solution.py:540
  233.5 71.9 %copy-start.13 = (s32[3]{0:T(128)S(1)}, s32[3]{0:T(128)}, u32[]{:S(2)}) copy-start(s32[3]{0:T(128)} %constant.390) | copy-start | bytes 40
  233.5 271.0 %all-gather.14.cloned.1.call-start = ((), (), s32[]{:S(2)}) async-start(), calls=%async_computation.7 | async-start | bytes 9175040 | tf_op jit(solution)/shard_map/all_gather | solution.py:654
  257.5 56.1 %copy-start.5 = (f32[8,560,128]{2,1,0:T(8,128)}, f32[8,560,128]{2,1,0:T(8,128)S(1)}, u32[]{:S(2)}) copy-start(f32[8,560,128]{2,1,0:T(8,128)S(1)} %collective-permute-done.6.refs_1_) | copy-start | bytes 6881284
  304.9 232.0 %all-gather.12.cloned.1.call-start = ((), (), s32[]{:S(2)}) async-start(), calls=%async_computation.6 | async-start | bytes 8192000 | tf_op jit(solution)/shard_map/all_gather | solution.py:654
  314.2 20.0 %collective-permute-start.3 = (f32[7,128,128]{2,1,0:T(8,128)S(1)}, f32[7,128,128]{2,1,0:T(8,128)S(1)}, u32[]{:S(2)}, u32[]{:S(2)}) collective-permute-start(f32[7,128,128]{2,1,0:T(8,128)S(1)} %get-tuple-element.130), channel_id=1, source_target_pairs={{0,1},{1,0},{2,3},{3,2},{4,5},{5,4},{6,7},{7,6},{8,9},{9,8},{10,11... | collective-permute-start | bytes 1376264 | tf_op jit(solution)/shard_map/ppermute | solution.py:550
  314.3 28.7 %collective-permute-start.4 = (f32[7,128,128]{2,1,0:T(8,128)S(1)}, f32[7,128,128]{2,1,0:T(8,128)S(1)}, u32[]{:S(2)}, u32[]{:S(2)}) collective-permute-start(f32[7,128,128]{2,1,0:T(8,128)S(1)} %get-tuple-element.131), channel_id=1, source_target_pairs={{0,2},{1,3},{2,0},{3,1},{4,6},{5,7},{6,4},{7,5},{8,10},{9,11},{10,... | collective-permute-start | bytes 1376264 | tf_op jit(solution)/shard_map/ppermute | solution.py:550
  318.2 35.1 %collective-permute-start.5 = (f32[7,128,128]{2,1,0:T(8,128)S(1)}, f32[7,128,128]{2,1,0:T(8,128)S(1)}, u32[]{:S(2)}, u32[]{:S(2)}) collective-permute-start(f32[7,128,128]{2,1,0:T(8,128)S(1)} %get-tuple-element.132), channel_id=1, source_target_pairs={{0,3},{1,2},{2,1},{3,0},{4,7},{5,6},{6,5},{7,4},{8,11},{9,10},{10,... | collective-permute-start | bytes 1376264 | tf_op jit(solution)/shard_map/ppermute | solution.py:550
  359.8 27.0 %copy-start.1 = (f32[4,7,128,128]{2,3,1,0:T(8,128)}, f32[4,7,128,128]{2,3,1,0:T(8,128)S(1)}, u32[]{:S(2)}) copy-start(f32[4,7,128,128]{2,3,1,0:T(8,128)S(1)} %broadcast_select_fusion) | copy-start | bytes 5505028
  386.9 2.1 copy-start.3
  390.3 65.5 %all-to-all-start.2 = ((f32[8,560,128]{2,1,0:T(8,128)}), f32[8,560,128]{2,1,0:T(8,128)S(1)}, u32[]{:S(2)}, u32[]{:S(2)}) async-start(f32[8,560,128]{2,1,0:T(8,128)} %bitcast.152), calls=%async_computation.2 | async-start | bytes 4587520 | tf_op jit(solution)/shard_map/all_to_all | solution.py:540
  402.5 175.6 %all-gather.10.cloned.1.call-start = ((), (), s32[]{:S(2)}) async-start(), calls=%async_computation.5 | async-start | bytes 11468800 | tf_op jit(solution)/shard_map/all_gather | solution.py:654
  455.8 1.4 copy-start
  455.8 2.5 copy-start.2
  459.9 156.4 %all-to-all-start.3 = ((f32[8,1680,128]{2,1,0:T(8,128)}), f32[8,1680,128]{2,1,0:T(8,128)}, u32[]{:S(2)}, u32[]{:S(2)}) async-start(f32[8,1680,128]{2,1,0:T(8,128)} %bitcast.150), calls=%async_computation.3 | async-start | bytes 13762560 | tf_op jit(solution)/shard_map/all_to_all | solution.py:540
  520.6 1.8 copy-start.12
Sparse Core Ops, SparseCore 0:
  48.3 3.2 sort.54.cloned.1.call-done
  69.8 19.9 sort.52.cloned.1.call-done
  225.9 35.1 all-gather.7
  305.0 102.2 all-gather.13
  409.1 72.9 all-gather.11
  483.8 94.2 all-gather.9
  (2 shorter events, 0.0 us)

commit v3 on v2

--- a/solution.py
+++ b/solution.py
@@ -12,6 +12,7 @@
 BLOCK = 128
 LANES = 128
 SUBLANES = 8
+REST_STEP = 1
 LIGHT = pl.CostEstimate(flops=1, bytes_accessed=1, transcendentals=0)
 HEAVY = pl.CostEstimate(flops=1, bytes_accessed=700_000_000, transcendentals=0)
 VMEM_LIMIT = 56 * 1024 * 1024
@@ -404,19 +405,24 @@
     store(steps - 1, lax.rem(steps + 1, 2)).wait()
 
 
-def finish_part(base, part, bounds, local, count, weights, head, width, has_head):
+def finish_index(local, count, tiles, width):
+    index, size = view_base(local, tiles), count * tiles
+    if width:
+        index = local // width * (width * (tiles - 1)) + local % width
+        size = count * (tiles - 1)
+    return jnp.where((local >= 0) & (local < count), index, size)
+
+
+def finish_part(base, part, bounds, index, weights, head, width, has_head):
     total, cols = base.shape
     tiles = cols // LANES
     rows = head.shape[0]
     while rows < 512 and total % (2 * rows) == 0:
         rows *= 2
     lane, stride = 0, SUBLANES
-    index = view_base(local, tiles)
     if width:
         tiles -= 1
         lane, stride = LANES, width
-        index = local // width * (width * tiles) + local % width
-    index = jnp.where((local >= 0) & (local < count), index, part.shape[0])
     spare = -(-(stride * (tiles - 1) + 1) // SUBLANES) * SUBLANES
     return pl.pallas_call(
         functools.partial(finish_kernel, rows, tiles, lane, stride, bool(width), has_head),
@@ -579,10 +585,19 @@
     outside = jnp.where(in_panel, 0.0, 1.0)[None, :].astype(jnp.float32)
     out = goce_slab * (goce_weight[0] * outside)
 
+    first = chunk_places[0]
+    first_order = (first // BLOCK * row_devices + row_id) * BLOCK + first % BLOCK
+    keep = jnp.where(first_order < PANEL, 0.0, 1.0)[:, None].astype(jnp.float32)
+
+    offsets = [sum(counts[:n]) for n in range(len(counts))]
+    indices = [
+        finish_index(positions - offset, count, tiles, 0) for offset, count in zip(offsets, counts)
+    ]
+    indices.append(finish_index(positions - offsets[-1], counts[-1], tiles, widths[-1]))
     added = [goce_rows(where, weights, goce_slab, row_devices) for where in chunk_places]
 
-    second, third, added, ends, positions, take_onehot, take_whole, out = tie(
-        (second, third, added, ends, positions, take_onehot, take_whole, out)
+    second, third, added, ends, positions, take_onehot, take_whole, out, keep, indices = tie(
+        (second, third, added, ends, positions, take_onehot, take_whole, out, keep, indices)
     )
     third = over_cols(third)
     (second_packet,) = mix(second, take_onehot, (tiles,))
@@ -614,7 +629,7 @@
         if step == 0:
             value, late["second"], packet = tie((value, second_got, third_packets[0]))
             late["panel"] = over_rows(packet)
-        if step == panel_blocks - 2:
+        if step == min(REST_STEP, panel_blocks - 2):
             value, late["panel"], packet = tie((value, late["panel"], third_packets[1]))
             late["rest"] = over_rows(packet)
         return value
@@ -644,16 +659,11 @@
     )
     in_block = (order_rows[:, None] < PANEL) & in_panel[None, :]
     head = jnp.where(in_block, known, jnp.where(on_diagonal, kaula_prior[None, :], 0.0))
-    first = chunk_places[0]
-    first_order = (first // BLOCK * row_devices + row_id) * BLOCK + first % BLOCK
-    keep = jnp.where(first_order < PANEL, 0.0, 1.0)[:, None].astype(jnp.float32)
-
     panels[0], third = tie((panels[0], third))
     for n, got in ((1, second_got), (2, third_panel)):
         panels.append(grace_weight[0] * got[:, 0].reshape(-1, BLOCK) + added[n])
     raws = [lax.all_gather(panel, "pcol", axis=0) for panel in panels]
     arrays = [[first_got], [second_got], [third_panel]]
-    offset = 0
     for n in range(len(widths)):
         part = update_part(
             arrays[n],
@@ -665,22 +675,10 @@
             matrix_high,
             matrix_low,
         )
-        out = finish_part(
-            out, part, ends[n], positions - offset, counts[n], weights, head, 0, n == 0
-        )
-        offset += counts[n]
+        out = finish_part(out, part, ends[n], indices[n], weights, head, 0, n == 0)
     out, third_rest = tie((out, third_rest))
-    return finish_part(
-        out,
-        third_rest.reshape(-1, LANES),
-        ends[-1],
-        positions - (offset - counts[-1]),
-        counts[-1],
-        weights,
-        head,
-        widths[-1],
-        False,
-    )
+    rest_rows = third_rest.reshape(-1, LANES)
+    return finish_part(out, rest_rows, ends[-1], indices[-1], weights, head, widths[-1], False)
 
 
 def solution(mesh):

time: 647 us -> 646 us (level)
  waiting for transfers between devices: 177 us -> 170 us
    all_gather x3, waiting for transfers between devices: 18.5 us -> 0.04 us  [shards(): raws = [lax.all_gather(panel, 'pcol', axis=0) for panel in panels]]
    all_to_all x4, waiting for transfers between devices: 13.6 us -> 31 us  [exchange(): got = lax.all_to_all(sent, axes, split_axis=0, concat_axis=0, tiled=True)]
  transfers between devices with their start and end apart: 17 -> 17, of which waited for: 13 -> 12; matrix products, arithmetic and copies ran while one was open for 28% -> 30% of each run, Pallas kernels for 27% -> 27%
where the time goes in v3:
time: 646 us; the launch traced here: 636 us
  Pallas kernels  203 us (31%)
  waiting for transfers between devices  170 us (26%)
  other arithmetic  150 us (23%)
  starting transfers between devices  44.3 us (7%)
  local copies, waits for them, and re-layouts  40.1 us (6%)
  between operations  16.3 us (3%)
  matrix products  13.8 us (2%)
    ppermute x9, waiting for transfers between devices, over_cols(): got.append(lax.ppermute(pieces[d], 'pcol', pairs))  138 us
    pallas_call x3, Pallas kernels, pack(): pl.pallas_call(functools.partial(pack_kernel, rows, tiles), out_shape=sha...  57.9 us
    pallas_call x4, Pallas kernels, finish_part(): pl.pallas_call(functools.partial(finish_kernel, rows, tiles, lane, stride...  52.3 us
    another operation x12, other arithmetic, cholesky_inverse(): factor[b, b] = jnp.linalg.cholesky(pivot, symmetrize_input=False)  49.8 us
    another operation x9, other arithmetic, cholesky_inverse(): jax.scipy.linalg.solve_triangular(factor[b, b], identity, lower=True)  42.8 us
    pallas_call x3, Pallas kernels, update_part(): pl.pallas_call(functools.partial(update_kernel, rows, placed, tuple(parts...  39 us
    all_to_all x4, starting transfers between devices, exchange(): got = lax.all_to_all(sent, axes, split_axis=0, concat_axis=0, tiled=True)  32.3 us
    all_to_all x4, waiting for transfers between devices, exchange(): got = lax.all_to_all(sent, axes, split_axis=0, concat_axis=0, tiled=True)  31 us
  transfers between devices with their start and end apart: 17, of which 12 were waited for; matrix products, arithmetic and copies ran while one was open for 30% of the time, Pallas kernels for 27%

profile of v3, /device:TPU:0, one launch (start us, length us, event | category | flops | bytes accessed | tf_op | source)
XLA Modules:
  0.0 636.5 jit_solution(1168927259349458748)
XLA Ops:
  8.4 8.2 %sort.43 = (s32[11264]{0:T(1024)S(1)}, s32[11264]{0:T(1024)}) sort(s32[11264]{0:T(1024)S(1)} %iota_add_fusion, s32[11264]{0:T(1024)S(1)} %iota.228), dimensions={0}, to_apply=%region_0.0 | sort | flops 157696 | bytes 180224 | tf_op jit(solution)/shard_map/jit(sort)/sort | solution.py:525
  19.1 18.6 %pack.3 = f32[8,4,448,128]{3,2,1,0:T(8,128)} custom-call(s32[3584]{0:T(1024)} %reshape.674.index_ref, f32[45056,128]{1,0:T(8,128)} %bitcast.138, bf16[4,512,128]{2,1,0:T(8,128)(2,1)} %get-tuple-element.149.onehot_ref), custom_call_target="tpu_custom_call" | custom-call | flops 1 | bytes 1 | tf_op jit(solution)/shard_map/pack/pallas_call | solution.py:125
  37.7 7.4 %all-to-all-start = ((f32[32,448,128]{2,1,0:T(8,128)}), f32[32,448,128]{2,1,0:T(8,128)}, u32[]{:S(2)}, u32[]{:S(2)}) async-start(f32[32,448,128]{2,1,0:T(8,128)} %bitcast.142), calls=%async_computation | async-start | bytes 14680064 | tf_op jit(solution)/shard_map/all_to_all | solution.py:546
  46.7 17.8 %pack.4 = (f32[8,400,128]{2,1,0:T(8,128)}, f32[8,400,128]{2,1,0:T(8,128)}, f32[8,400,128]{2,1,0:T(8,128)}, f32[8,400,128]{2,1,0:T(8,128)}) custom-call(s32[3200]{0:T(1024)} %reshape.673.index_ref, f32[45056,128]{1,0:T(8,128)} %bitcast.139, bf16[4,512,128]{2,1,0:T(8,128)(2,1)} %get-tuple-element.148.onehot_ref), custom_call_target="tpu_custom_call" | custom-call | flops 1 | bytes 1 | tf_op jit(solution)/shard_map/pack/pallas_call | solution.py:125
  69.9 21.5 %pack.5 = (f32[8,560,128]{2,1,0:T(8,128)}, f32[8,560,128]{2,1,0:T(8,128)}, f32[8,560,128]{2,1,0:T(8,128)}, f32[8,560,128]{2,1,0:T(8,128)}) custom-call(s32[4480]{0:T(1024)} %reshape.677.index_ref, f32[45056,128]{1,0:T(8,128)} %bitcast.140, bf16[4,512,128]{2,1,0:T(8,128)(2,1)} %get-tuple-element.148.onehot_ref), custom_call_target="tpu_custom_call" | custom-call | flops 1 | bytes 1 | tf_op jit(solution)/shard_map/pack/pallas_call | solution.py:125
  93.6 16.1 %broadcast_multiply_fusion.base_hbm = f32[11264,512]{1,0:T(8,128)} fusion(f32[11264,512]{1,0:T(8,128)} %goce_hbm.5, f32[512]{0:T(512)S(1)} %select_multiply_fusion), kind=kLoop, calls=%fused_computation.9 | loop fusion | flops 5767168 | bytes 46139392 | tf_op jit(solution)/shard_map/mul | solution.py:586
  115.0 8.0 %goce_rows.4 = f32[3200,128]{1,0:T(8,128)} custom-call(s32[3200]{0:T(1024)} %reshape.680.index_ref, f32[2]{0:T(128)} %pad_maximum_fusion.16.weight_ref, f32[11264,512]{1,0:T(8,128)} %goce_hbm.5), custom_call_target="tpu_custom_call" | custom-call | flops 1 | bytes 1 | tf_op jit(solution)/shard_map/goce_rows/pallas_call | solution.py:210
  123.0 8.5 %goce_rows.3.added_ref = f32[3584,128]{1,0:T(8,128)} custom-call(s32[3584]{0:T(1024)} %reshape.679.index_ref, f32[2]{0:T(128)} %pad_maximum_fusion.16.weight_ref, f32[11264,512]{1,0:T(8,128)} %goce_hbm.5), custom_call_target="tpu_custom_call" | custom-call | flops 1 | bytes 1 | tf_op jit(solution)/shard_map/goce_rows/pallas_call | solution.py:210
  131.5 9.8 %goce_rows.5 = f32[4480,128]{1,0:T(8,128)} custom-call(s32[4480]{0:T(1024)} %reshape.681.index_ref, f32[2]{0:T(128)} %pad_maximum_fusion.16.weight_ref, f32[11264,512]{1,0:T(8,128)} %goce_hbm.5), custom_call_target="tpu_custom_call" | custom-call | flops 1 | bytes 1 | tf_op jit(solution)/shard_map/goce_rows/pallas_call | solution.py:210
  145.1 8.2 %sort.45 = (s32[11264]{0:T(1024)S(1)}, s32[11264]{0:T(1024)}) sort(s32[11264]{0:T(1024)S(1)} %fusion.92, s32[11264]{0:T(1024)S(1)} %iota.231), dimensions={0}, to_apply=%region_3.4 | sort | flops 157696 | bytes 180224 | tf_op jit(solution)/shard_map/jit(sort)/sort | solution.py:576
  154.1 3.2 fusion.9.keep_ref
  157.3 7.5 %collective-permute-done.1.refs_2_ = f32[8,400,128]{2,1,0:T(8,128)} collective-permute-done((f32[8,400,128]{2,1,0:T(8,128)}, f32[8,400,128]{2,1,0:T(8,128)}, u32[]{:S(2)}, u32[]{:S(2)}) %collective-permute-start.1) | collective-permute-done | bytes 1638432 | tf_op jit(solution)/shard_map/ppermute | solution.py:556
  164.8 37.2 %collective-permute-done.2.refs_3_ = f32[8,400,128]{2,1,0:T(8,128)} collective-permute-done((f32[8,400,128]{2,1,0:T(8,128)}, f32[8,400,128]{2,1,0:T(8,128)}, u32[]{:S(2)}, u32[]{:S(2)}) %collective-permute-start.2) | collective-permute-done | bytes 1638432 | tf_op jit(solution)/shard_map/ppermute | solution.py:556
  202.0 2.4 collective-permute-start.6
  205.9 8.2 %mix.2 = f32[8,4,400,128]{3,2,1,0:T(8,128)} custom-call(bf16[4,128,512]{2,1,0:T(8,128)(2,1)} %broadcast_select_fusion.1.onehot_ref, f32[8,400,128]{2,1,0:T(8,128)} %get-tuple-element.79.refs_0_, f32[8,400,128]{2,1,0:T(8,128)} %collective-permute-done.refs_1_, f32[8,400,128]{2,1,0:T(8,128)} %collective-permute-done.1.refs_2_, ...), custom_call_target="tpu_custom_call" | custom-call | flops 1 | bytes 1 | tf_op jit(solution)/shard_map/mix/pallas_call | solution.py:177
  216.2 7.0 %panel.1 = f32[3584,128]{1,0:T(8,128)} custom-call(f32[2]{0:T(128)} %pad_maximum_fusion.16.weight_ref, f32[3584,128]{1,0:T(8,128)} %goce_rows.3.added_ref, bf16[4,128,128]{2,1,0:T(8,128)(2,1)} %slice.147.onehot_ref, f32[8,4,448,128]{3,2,1,0:T(8,128)} %bitcast.9.received_ref.refs_2_), custom_call_target="tpu_custom_call" | custom-call | flops 1 | bytes 700000000 | tf_op jit(solution)/shard_map/panel/pallas_call | solution.py:240
  223.2 2.2 gather_fusion.1
  226.2 7.7 %all-to-all-start.1 = ((f32[8,1600,128]{2,1,0:T(8,128)}), f32[8,1600,128]{2,1,0:T(8,128)}, u32[]{:S(2)}, u32[]{:S(2)}) async-start(f32[8,1600,128]{2,1,0:T(8,128)} %bitcast.144), calls=%async_computation.1 | async-start | bytes 13107200 | tf_op jit(solution)/shard_map/all_to_all | solution.py:546
  234.0 23.5 %collective-permute-done.6.refs_1_ = f32[8,560,128]{2,1,0:T(8,128)S(1)} collective-permute-done((f32[8,560,128]{2,1,0:T(8,128)}, f32[8,560,128]{2,1,0:T(8,128)S(1)}, u32[]{:S(2)}, u32[]{:S(2)}) %collective-permute-start.6) | collective-permute-done | bytes 2293792 | tf_op jit(solution)/shard_map/ppermute | solution.py:556
  257.5 47.1 %collective-permute-done.7.refs_2_ = f32[8,560,128]{2,1,0:T(8,128)} collective-permute-done((f32[8,560,128]{2,1,0:T(8,128)}, f32[8,560,128]{2,1,0:T(8,128)}, u32[]{:S(2)}, u32[]{:S(2)}) %collective-permute-start.7) | collective-permute-done | bytes 2293792 | tf_op jit(solution)/shard_map/ppermute | solution.py:556
  313.9 3.9 collective-permute-start.4
  317.8 11.9 %mix.3 = (f32[8,1,560,128]{3,2,1,0:T(8,128)}, f32[8,3,560,128]{3,2,1,0:T(8,128)}) custom-call(bf16[4,128,512]{2,1,0:T(8,128)(2,1)} %broadcast_select_fusion.1.onehot_ref, f32[8,560,128]{2,1,0:T(8,128)} %get-tuple-element.84.refs_0_, f32[8,560,128]{2,1,0:T(8,128)} %copy-done.6, f32[8,560,128]{2,1,0:T(8,128)} %collective-permute-done.7.refs_2_, ...), custom_call_target="tpu_custom_call" | custom-call | flops 1 | bytes 1 | tf_op jit(solution)/shard_map/mix/pallas_call | solution.py:177
  329.7 3.7 collective-permute-done.3
  333.4 8.8 %collective-permute-done.4 = f32[7,128,128]{2,1,0:T(8,128)S(1)} collective-permute-done((f32[7,128,128]{2,1,0:T(8,128)S(1)}, f32[7,128,128]{2,1,0:T(8,128)S(1)}, u32[]{:S(2)}, u32[]{:S(2)}) %collective-permute-start.4) | collective-permute-done | bytes 458784 | tf_op jit(solution)/shard_map/ppermute | solution.py:556
  342.1 10.3 %collective-permute-done.5 = f32[7,128,128]{2,1,0:T(8,128)S(1)} collective-permute-done((f32[7,128,128]{2,1,0:T(8,128)S(1)}, f32[7,128,128]{2,1,0:T(8,128)S(1)}, u32[]{:S(2)}, u32[]{:S(2)}) %collective-permute-start.5) | collective-permute-done | bytes 458784 | tf_op jit(solution)/shard_map/ppermute | solution.py:556
  352.6 1.9 gather_fusion.2
  354.4 2.8 copy.152
  359.0 1.9 copy.153
  362.7 11.7 %cholesky.75 = f32[128,128]{1,0:T(8,128)S(1)} custom-call(f32[128,128]{1,0:T(8,128)S(1)} %bitcast_add_fusion.5), custom_call_target="Cholesky" | custom-call | tf_op jit(solution)/shard_map/jit(cholesky)/cholesky | solution.py:469
  375.9 9.8 %custom-call.8 = f32[1,128,128]{1,2,0:T(8,128)S(1)} custom-call(f32[1,128,128]{2,1,0:T(8,128)S(1)} %get-tuple-element.116), custom_call_target="InvertDiagBlocksLowerTriangular" | custom-call | tf_op jit(solution)/shard_map/jit(_solve_triangular)/triangular_solve | solution.py:470
  390.0 12.0 %all-to-all-start.2 = ((f32[8,560,128]{2,1,0:T(8,128)}), f32[8,560,128]{2,1,0:T(8,128)S(1)}, u32[]{:S(2)}, u32[]{:S(2)}) async-start(f32[8,560,128]{2,1,0:T(8,128)} %bitcast.152), calls=%async_computation.2 | async-start | bytes 4587520 | tf_op jit(solution)/shard_map/all_to_all | solution.py:546
  403.4 11.7 %cholesky.86 = f32[128,128]{1,0:T(8,128)S(1)} custom-call(f32[128,128]{1,0:T(8,128)S(1)} %convolution_subtract_fusion.3), custom_call_target="Cholesky" | custom-call | tf_op jit(solution)/shard_map/jit(cholesky)/cholesky | solution.py:469
  417.2 9.8 %custom-call.9 = f32[1,128,128]{1,2,0:T(8,128)S(1)} custom-call(f32[1,128,128]{2,1,0:T(8,128)S(1)} %get-tuple-element.114), custom_call_target="InvertDiagBlocksLowerTriangular" | custom-call | tf_op jit(solution)/shard_map/jit(_solve_triangular)/triangular_solve | solution.py:470
  428.0 27.3 %all-to-all-done.2 = f32[8,560,128]{2,1,0:T(8,128)S(1)} async-done(((f32[8,560,128]{2,1,0:T(8,128)}), f32[8,560,128]{2,1,0:T(8,128)S(1)}, u32[]{:S(2)}, u32[]{:S(2)}) %all-to-all-start.2) | async-done | bytes 2293792 | tf_op jit(solution)/shard_map/all_to_all | solution.py:546
  459.4 5.2 all-to-all-start.3
  474.6 11.7 %cholesky.97 = f32[128,128]{1,0:T(8,128)S(1)} custom-call(f32[128,128]{1,0:T(8,128)S(1)} %convolution_subtract_fusion.2), custom_call_target="Cholesky" | custom-call | tf_op jit(solution)/shard_map/jit(cholesky)/cholesky | solution.py:469
  487.5 9.8 %custom-call.10 = f32[1,128,128]{1,2,0:T(8,128)S(1)} custom-call(f32[1,128,128]{2,1,0:T(8,128)S(1)} %get-tuple-element.112), custom_call_target="InvertDiagBlocksLowerTriangular" | custom-call | tf_op jit(solution)/shard_map/jit(_solve_triangular)/triangular_solve | solution.py:470
  499.4 11.7 %cholesky.108 = f32[128,128]{1,0:T(8,128)S(1)} custom-call(f32[128,128]{1,0:T(8,128)S(1)} %copy.172), custom_call_target="Cholesky" | custom-call | tf_op jit(solution)/shard_map/jit(cholesky)/cholesky | solution.py:469
  512.6 10.0 %custom-call.11 = f32[1,128,128]{1,2,0:T(8,128)S(1)} custom-call(f32[1,128,128]{2,1,0:T(8,128)S(1)} %get-tuple-element.110), custom_call_target="InvertDiagBlocksLowerTriangular" | custom-call | tf_op jit(solution)/shard_map/jit(_solve_triangular)/triangular_solve | solution.py:470
  526.5 1.8 fusion.10
  528.3 2.9 fusion.11
  531.3 14.7 %update.5 = f32[448,4,8,128]{3,2,1,0:T(8,128)} custom-call(f32[2]{0:T(128)} %pad_maximum_fusion.16.weight_ref, f32[1,512]{1,0:T(1,128)} %compare_select_fusion.1.mask_ref, f32[3584,1]{1,0:T(8,128)} %fusion.9.keep_ref, bf16[512,512]{1,0:T(8,128)(2,1)} %get-tuple-element.138.high_ref, bf16[512,512]{1,0:T(8,128)(2,1)} %get-tuple-element.137.low_ref, ...), custom_call_target="tpu_custom_call" | custom-call | flops 1 | bytes 1 | tf_op jit(solution)/shard_map/update/pallas_call | solution.py:326
  550.7 12.4 %finish.4.base_hbm = f32[11264,512]{1,0:T(8,128)} custom-call(s32[16]{0:T(128)} %reshape.682.bounds_ref, s32[11264]{0:T(1024)} %get-tuple-element.104.index_ref, f32[2]{0:T(128)} %pad_maximum_fusion.16.weight_ref, f32[14336,128]{1,0:T(8,128)} %bitcast.143, f32[256,512]{1,0:T(8,128)} %bitcast_select_fusion.head_ref, ...), custom_call_target="tpu_custom_call", output_to_operand_aliasing={{}: (5, {})} | custom-call | flops 1 | bytes 1 | tf_op jit(solution)/shard_map/finish/pallas_call | solution.py:427
  563.1 10.6 %update.4 = f32[400,4,8,128]{3,2,1,0:T(8,128)} custom-call(f32[2]{0:T(128)} %pad_maximum_fusion.16.weight_ref, f32[1,512]{1,0:T(1,128)} %compare_select_fusion.1.mask_ref, f32[3584,1]{1,0:T(8,128)} %fusion.9.keep_ref, bf16[512,512]{1,0:T(8,128)(2,1)} %get-tuple-element.138.high_ref, bf16[512,512]{1,0:T(8,128)(2,1)} %get-tuple-element.137.low_ref, ...), custom_call_target="tpu_custom_call" | custom-call | flops 1 | bytes 1 | tf_op jit(solution)/shard_map/update/pallas_call | solution.py:326
  573.7 12.1 %finish.5.base_hbm = f32[11264,512]{1,0:T(8,128)} custom-call(s32[16]{0:T(128)} %reshape.683.bounds_ref, s32[11264]{0:T(1024)} %get-tuple-element.100.index_ref, f32[2]{0:T(128)} %pad_maximum_fusion.16.weight_ref, f32[12800,128]{1,0:T(8,128)} %bitcast.145, f32[256,512]{1,0:T(8,128)} %bitcast_select_fusion.head_ref, ...), custom_call_target="tpu_custom_call", output_to_operand_aliasing={{}: (5, {})} | custom-call | flops 1 | bytes 1 | tf_op jit(solution)/shard_map/finish/pallas_call | solution.py:427
  585.8 13.7 %update.3 = f32[560,4,8,128]{3,2,1,0:T(8,128)} custom-call(f32[2]{0:T(128)} %pad_maximum_fusion.16.weight_ref, f32[1,512]{1,0:T(1,128)} %compare_select_fusion.1.mask_ref, f32[3584,1]{1,0:T(8,128)} %fusion.9.keep_ref, bf16[512,512]{1,0:T(8,128)(2,1)} %get-tuple-element.138.high_ref, bf16[512,512]{1,0:T(8,128)(2,1)} %get-tuple-element.137.low_ref, ...), custom_call_target="tpu_custom_call" | custom-call | flops 1 | bytes 1 | tf_op jit(solution)/shard_map/update/pallas_call | solution.py:326
  599.5 14.6 %finish.6.base_hbm = f32[11264,512]{1,0:T(8,128)} custom-call(s32[16]{0:T(128)} %reshape.684.bounds_ref, s32[11264]{0:T(1024)} %get-tuple-element.73.index_ref, f32[2]{0:T(128)} %pad_maximum_fusion.16.weight_ref, f32[17920,128]{1,0:T(8,128)} %bitcast.141, f32[256,512]{1,0:T(8,128)} %bitcast_select_fusion.head_ref, ...), custom_call_target="tpu_custom_call", output_to_operand_aliasing={{}: (5, {})} | custom-call | flops 1 | bytes 1 | tf_op jit(solution)/shard_map/finish/pallas_call | solution.py:427
  615.9 13.2 %finish.7 = f32[11264,512]{1,0:T(8,128)} custom-call(s32[16]{0:T(128)} %reshape.684.bounds_ref, s32[11264]{0:T(1024)} %get-tuple-element.72.index_ref, f32[2]{0:T(128)} %pad_maximum_fusion.16.weight_ref, f32[13440,128]{1,0:T(8,128)} %bitcast.68.part_hbm, f32[256,512]{1,0:T(8,128)} %bitcast_select_fusion.head_ref, ...), custom_call_target="tpu_custom_call", output_to_operand_aliasing={{}: (5, {})} | custom-call | flops 1 | bytes 1 | tf_op jit(solution)/shard_map/finish/pallas_call | solution.py:427
  (237 shorter events, 78.1 us)
Async XLA Ops:
  37.7 7.5 %copy-start.18 = (s32[2048]{0:T(1024)S(1)}, s32[2048]{0:T(1024)}, u32[]{:S(2)}) copy-start(s32[2048]{0:T(1024)} %param.22) | copy-start | bytes 24580
  37.7 178.5 %all-to-all-start = ((f32[32,448,128]{2,1,0:T(8,128)}), f32[32,448,128]{2,1,0:T(8,128)}, u32[]{:S(2)}, u32[]{:S(2)}) async-start(f32[32,448,128]{2,1,0:T(8,128)} %bitcast.142), calls=%async_computation | async-start | bytes 14680064 | tf_op jit(solution)/shard_map/all_to_all | solution.py:546
  45.1 64.5 %sort.50.cloned.1.call-start = ((), (), s32[]{:S(2)}) async-start(), calls=%async_computation.9 | async-start | bytes 24608 | tf_op jit(solution)/shard_map/jit(sort)/sort | solution.py:577
  45.9 65.2 %sort.48.cloned.1.call-start = ((), (), s32[]{:S(2)}) async-start(), calls=%async_computation.8 | async-start | bytes 1081376 | tf_op jit(solution)/shard_map/jit(sort)/sort | solution.py:566
  46.7 21.4 %copy-start.7 = (s32[90112]{0:T(1024)S(1)}, s32[90112]{0:T(1024)}, u32[]{:S(2)}) copy-start(s32[90112]{0:T(1024)} %param.21) | copy-start | bytes 1081348
  64.5 92.8 %collective-permute-start = (f32[8,400,128]{2,1,0:T(8,128)}, f32[8,400,128]{2,1,0:T(8,128)}, u32[]{:S(2)}, u32[]{:S(2)}) collective-permute-start(f32[8,400,128]{2,1,0:T(8,128)} %get-tuple-element.63), channel_id=1, source_target_pairs={{0,1},{1,0},{2,3},{3,2},{4,5},{5,4},{6,7},{7,6},{8,9},{9,8},{10,11... | collective-permute-start | bytes 4915208 | tf_op jit(solution)/shard_map/ppermute | solution.py:556
  66.3 98.6 %collective-permute-start.1 = (f32[8,400,128]{2,1,0:T(8,128)}, f32[8,400,128]{2,1,0:T(8,128)}, u32[]{:S(2)}, u32[]{:S(2)}) collective-permute-start(f32[8,400,128]{2,1,0:T(8,128)} %get-tuple-element.64), channel_id=1, source_target_pairs={{0,2},{1,3},{2,0},{3,1},{4,6},{5,7},{6,4},{7,5},{8,10},{9,11},{10,... | collective-permute-start | bytes 4915208 | tf_op jit(solution)/shard_map/ppermute | solution.py:556
  67.7 134.3 %collective-permute-start.2 = (f32[8,400,128]{2,1,0:T(8,128)}, f32[8,400,128]{2,1,0:T(8,128)}, u32[]{:S(2)}, u32[]{:S(2)}) collective-permute-start(f32[8,400,128]{2,1,0:T(8,128)} %get-tuple-element.65), channel_id=1, source_target_pairs={{0,3},{1,2},{2,1},{3,0},{4,7},{5,6},{6,5},{7,4},{8,11},{9,10},{10,... | collective-permute-start | bytes 4915208 | tf_op jit(solution)/shard_map/ppermute | solution.py:556
  69.7 23.8 %slice-start = ((f32[512]{0:T(512)}), f32[128]{0:T(128)S(1)}, s32[]{:S(2)}) async-start(f32[512]{0:T(512)} %param.20), calls=%async_computation.12 | async-start | bytes 1024 | tf_op jit(solution)/shard_map/slice | solution.py:610
  69.7 235.4 %all-gather.8.cloned.1.call-start = ((), (), s32[]{:S(2)}) async-start(), calls=%async_computation.4 | async-start | bytes 1179648 | tf_op jit(solution)/shard_map/all_gather | solution.py:612
  110.5 103.6 %copy-start.5 = (bf16[4,128,512]{2,1,0:T(8,128)(2,1)}, bf16[4,128,512]{2,1,0:T(8,128)(2,1)S(1)}, u32[]{:S(2)}) copy-start(bf16[4,128,512]{2,1,0:T(8,128)(2,1)S(1)} %fusion.24.refs_1_) | copy-start | bytes 1572868
  141.3 3.7 copy-start.11
  141.3 3.7 copy-start.12
  141.3 3.7 copy-start.13
  202.0 55.5 %collective-permute-start.6 = (f32[8,560,128]{2,1,0:T(8,128)}, f32[8,560,128]{2,1,0:T(8,128)S(1)}, u32[]{:S(2)}, u32[]{:S(2)}) collective-permute-start(f32[8,560,128]{2,1,0:T(8,128)} %get-tuple-element.85), channel_id=1, source_target_pairs={{0,1},{1,0},{2,3},{3,2},{4,5},{5,4},{6,7},{7,6},{8,9},{9,8},{10,11... | collective-permute-start | bytes 6881288 | tf_op jit(solution)/shard_map/ppermute | solution.py:556
  204.4 100.2 %collective-permute-start.7 = (f32[8,560,128]{2,1,0:T(8,128)}, f32[8,560,128]{2,1,0:T(8,128)}, u32[]{:S(2)}, u32[]{:S(2)}) collective-permute-start(f32[8,560,128]{2,1,0:T(8,128)} %get-tuple-element.86), channel_id=1, source_target_pairs={{0,2},{1,3},{2,0},{3,1},{4,6},{5,7},{6,4},{7,5},{8,10},{9,11},{10,... | collective-permute-start | bytes 6881288 | tf_op jit(solution)/shard_map/ppermute | solution.py:556
  204.4 100.5 %collective-permute-start.8 = (f32[8,560,128]{2,1,0:T(8,128)}, f32[8,560,128]{2,1,0:T(8,128)}, u32[]{:S(2)}, u32[]{:S(2)}) collective-permute-start(f32[8,560,128]{2,1,0:T(8,128)} %get-tuple-element.87), channel_id=1, source_target_pairs={{0,3},{1,2},{2,1},{3,0},{4,7},{5,6},{6,5},{7,4},{8,11},{9,10},{10,... | collective-permute-start | bytes 6881288 | tf_op jit(solution)/shard_map/ppermute | solution.py:556
  226.2 160.8 %all-to-all-start.1 = ((f32[8,1600,128]{2,1,0:T(8,128)}), f32[8,1600,128]{2,1,0:T(8,128)}, u32[]{:S(2)}, u32[]{:S(2)}) async-start(f32[8,1600,128]{2,1,0:T(8,128)} %bitcast.144), calls=%async_computation.1 | async-start | bytes 13107200 | tf_op jit(solution)/shard_map/all_to_all | solution.py:546
  233.9 71.1 %copy-start.30 = (s32[3]{0:T(128)S(1)}, s32[3]{0:T(128)}, u32[]{:S(2)}) copy-start(s32[3]{0:T(128)} %constant.390) | copy-start | bytes 40
  233.9 297.3 %all-gather.14.cloned.1.call-start = ((), (), s32[]{:S(2)}) async-start(), calls=%async_computation.7 | async-start | bytes 9175040 | tf_op jit(solution)/shard_map/all_gather | solution.py:665
  257.5 55.7 %copy-start.6 = (f32[8,560,128]{2,1,0:T(8,128)}, f32[8,560,128]{2,1,0:T(8,128)S(1)}, u32[]{:S(2)}) copy-start(f32[8,560,128]{2,1,0:T(8,128)S(1)} %collective-permute-done.6.refs_1_) | copy-start | bytes 6881284
  304.9 258.2 %all-gather.12.cloned.1.call-start = ((), (), s32[]{:S(2)}) async-start(), calls=%async_computation.6 | async-start | bytes 8192000 | tf_op jit(solution)/shard_map/all_gather | solution.py:665
  313.8 19.6 %collective-permute-start.3 = (f32[7,128,128]{2,1,0:T(8,128)S(1)}, f32[7,128,128]{2,1,0:T(8,128)S(1)}, u32[]{:S(2)}, u32[]{:S(2)}) collective-permute-start(f32[7,128,128]{2,1,0:T(8,128)S(1)} %get-tuple-element.140), channel_id=1, source_target_pairs={{0,1},{1,0},{2,3},{3,2},{4,5},{5,4},{6,7},{7,6},{8,9},{9,8},{10,11... | collective-permute-start | bytes 1376264 | tf_op jit(solution)/shard_map/ppermute | solution.py:556
  313.9 28.3 %collective-permute-start.4 = (f32[7,128,128]{2,1,0:T(8,128)S(1)}, f32[7,128,128]{2,1,0:T(8,128)S(1)}, u32[]{:S(2)}, u32[]{:S(2)}) collective-permute-start(f32[7,128,128]{2,1,0:T(8,128)S(1)} %get-tuple-element.141), channel_id=1, source_target_pairs={{0,2},{1,3},{2,0},{3,1},{4,6},{5,7},{6,4},{7,5},{8,10},{9,11},{10,... | collective-permute-start | bytes 1376264 | tf_op jit(solution)/shard_map/ppermute | solution.py:556
  317.8 34.6 %collective-permute-start.5 = (f32[7,128,128]{2,1,0:T(8,128)S(1)}, f32[7,128,128]{2,1,0:T(8,128)S(1)}, u32[]{:S(2)}, u32[]{:S(2)}) collective-permute-start(f32[7,128,128]{2,1,0:T(8,128)S(1)} %get-tuple-element.142), channel_id=1, source_target_pairs={{0,3},{1,2},{2,1},{3,0},{4,7},{5,6},{6,5},{7,4},{8,11},{9,10},{10,... | collective-permute-start | bytes 1376264 | tf_op jit(solution)/shard_map/ppermute | solution.py:556
  317.8 146.8 %copy-start.20 = (s32[128]{0:T(128)}, s32[128]{0:T(128)S(1)}, u32[]{:S(2)}) copy-start(s32[128]{0:T(128)S(1)} %iota_add_fusion.1) | copy-start | bytes 1540
  359.0 27.0 %copy-start.1 = (f32[4,7,128,128]{2,3,1,0:T(8,128)}, f32[4,7,128,128]{2,3,1,0:T(8,128)S(1)}, u32[]{:S(2)}) copy-start(f32[4,7,128,128]{2,3,1,0:T(8,128)S(1)} %broadcast_select_fusion) | copy-start | bytes 5505028
  386.1 2.5 copy-start.4
  390.0 65.3 %all-to-all-start.2 = ((f32[8,560,128]{2,1,0:T(8,128)}), f32[8,560,128]{2,1,0:T(8,128)S(1)}, u32[]{:S(2)}, u32[]{:S(2)}) async-start(f32[8,560,128]{2,1,0:T(8,128)} %bitcast.152), calls=%async_computation.2 | async-start | bytes 4587520 | tf_op jit(solution)/shard_map/all_to_all | solution.py:546
  402.0 183.8 %all-gather.10.cloned.1.call-start = ((), (), s32[]{:S(2)}) async-start(), calls=%async_computation.5 | async-start | bytes 11468800 | tf_op jit(solution)/shard_map/all_gather | solution.py:665
  455.3 2.5 copy-start.3
  459.4 11.6 %copy-start.2 = (f32[4,7,128,128]{2,3,1,0:T(8,128)S(1)}, f32[4,7,128,128]{2,3,1,0:T(8,128)}, u32[]{:S(2)}) copy-start(f32[4,7,128,128]{2,3,1,0:T(8,128)} %copy-done.1) | copy-start | bytes 5505028
  459.4 156.5 %all-to-all-start.3 = ((f32[8,1680,128]{2,1,0:T(8,128)}), f32[8,1680,128]{2,1,0:T(8,128)}, u32[]{:S(2)}, u32[]{:S(2)}) async-start(f32[8,1680,128]{2,1,0:T(8,128)} %bitcast.150), calls=%async_computation.3 | async-start | bytes 13762560 | tf_op jit(solution)/shard_map/all_to_all | solution.py:546
  464.6 9.7 %copy-start.21 = (s32[128]{0:T(128)S(1)}, s32[128]{0:T(128)}, u32[]{:S(2)}) copy-start(s32[128]{0:T(128)} %copy-done.20) | copy-start | bytes 1540
  471.0 27.9 %copy-start.17 = (pred[128,128]{0,1:T(32,128)(4,1)S(1)}, pred[128,128]{0,1:T(32,128)(4,1)}, u32[]{:S(2)}) copy-start(pred[128,128]{0,1:T(32,128)(4,1)} %copy.165) | copy-start | bytes 49156
  523.0 3.4 copy-start.8
  523.0 3.4 copy-start.14
  523.0 3.4 copy-start.15
  523.0 3.4 copy-start.16
  523.0 3.4 copy-start.22
  523.0 3.4 copy-start.24
  523.0 3.4 copy-start.28
  531.2 14.7 %copy-start.9 = (f32[128,128]{1,0:T(8,128)S(1)}, f32[128,128]{1,0:T(8,128)}, u32[]{:S(2)}) copy-start(f32[128,128]{1,0:T(8,128)} %get-tuple-element.115) | copy-start | bytes 196612
  531.3 14.7 %copy-start.10 = (f32[128,128]{1,0:T(8,128)S(1)}, f32[128,128]{1,0:T(8,128)}, u32[]{:S(2)}) copy-start(f32[128,128]{1,0:T(8,128)} %get-tuple-element.143) | copy-start | bytes 196612
  547.9 1.8 copy-start.23
  547.9 1.8 copy-start.25
  547.9 1.8 copy-start.26
  547.9 1.8 copy-start.27
  (3 other events, 3.2 us)
Sparse Core Ops, SparseCore 0:
  48.3 3.2 sort.54.cloned.1.call-done
  69.8 19.8 sort.52.cloned.1.call-done
  226.3 35.1 all-gather.7
  305.0 102.2 all-gather.13
  409.1 72.5 all-gather.11
  483.4 94.4 all-gather.9
  (2 shorter events, 0.0 us)

commit v4 on v3

--- a/solution.py
+++ b/solution.py
@@ -12,7 +12,7 @@
 BLOCK = 128
 LANES = 128
 SUBLANES = 8
-REST_STEP = 1
+REST_STEP = 2
 LIGHT = pl.CostEstimate(flops=1, bytes_accessed=1, transcendentals=0)
 HEAVY = pl.CostEstimate(flops=1, bytes_accessed=700_000_000, transcendentals=0)
 VMEM_LIMIT = 56 * 1024 * 1024
@@ -86,12 +86,13 @@
 
     @pl.when(step == 0)
     def _():
-        copy = pltpu.make_async_copy(source_hbm, held, sem)
+        size = source_hbm.shape[0]
+        copy = pltpu.make_async_copy(source_hbm, held.at[pl.ds(0, size)], sem)
         copy.start()
         copy.wait()
 
     copy_rows(index_ref, step * rows, held, picked, rows, tiles, SUBLANES)
-    high, low = split(from_view(picked[...], rows, tiles))
+    high, low = split(from_view(picked[: rows * tiles], rows, tiles))
     places = [(out, None) for out in outs]
     if len(outs) == 1:
         places = [(outs[0], d) for d in range(outs[0].shape[1])]
@@ -133,8 +134,8 @@
         ],
         out_specs=specs,
         scratch_shapes=[
-            pltpu.VMEM(view.shape, jnp.float32),
-            pltpu.VMEM((rows * tiles, LANES), jnp.float32),
+            pltpu.VMEM((view.shape[0] + SUBLANES * tiles, LANES), jnp.float32),
+            pltpu.VMEM((rows * tiles + SUBLANES * tiles, LANES), jnp.float32),
             pltpu.SemaphoreType.DMA,
         ],
         compiler_params=pltpu.CompilerParams(vmem_limit_bytes=VMEM_LIMIT),
@@ -201,7 +202,7 @@
         copy.wait()
 
     copy_rows(index_ref, step * rows, held, picked, rows, 1, 1)
-    out_ref[...] = weight_ref[1] * picked[...]
+    out_ref[...] = weight_ref[1] * picked[:rows]
 
 
 def goce_rows(places, weights, goce, row_devices):
@@ -219,7 +220,7 @@
         out_specs=pl.BlockSpec((rows, BLOCK), lambda i: (i, 0)),
         scratch_shapes=[
             pltpu.VMEM((goce.shape[0], BLOCK), jnp.float32),
-            pltpu.VMEM((rows, BLOCK), jnp.float32),
+            pltpu.VMEM((rows + SUBLANES, BLOCK), jnp.float32),
             pltpu.SemaphoreType.DMA,
         ],
         compiler_params=pltpu.CompilerParams(vmem_limit_bytes=VMEM_LIMIT),
@@ -382,7 +383,7 @@
         def _():
             store(step - 2, slot).wait()
 
-        added = from_view(picked[...], rows, tiles)
+        added = from_view(picked[: rows * tiles], rows, tiles)
         if weighted:
             added = weight_ref[0] * added
         after[slot] = before[slot] + added
@@ -423,7 +424,7 @@
     if width:
         tiles -= 1
         lane, stride = LANES, width
-    spare = -(-(stride * (tiles - 1) + 1) // SUBLANES) * SUBLANES
+    spare = stride * tiles + SUBLANES
     return pl.pallas_call(
         functools.partial(finish_kernel, rows, tiles, lane, stride, bool(width), has_head),
         out_shape=jax.ShapeDtypeStruct((total, cols), jnp.float32),
@@ -438,7 +439,7 @@
         out_specs=pl.BlockSpec(memory_space=pl.ANY),
         scratch_shapes=[
             pltpu.VMEM((part.shape[0] + spare, LANES), jnp.float32),
-            pltpu.VMEM((rows * tiles, LANES), jnp.float32),
+            pltpu.VMEM((rows * tiles + SUBLANES * tiles, LANES), jnp.float32),
             pltpu.VMEM((2, rows, tiles * LANES), jnp.float32),
             pltpu.VMEM((2, rows, tiles * LANES), jnp.float32),
             pltpu.SemaphoreType.DMA,

time: 646 us -> 646 us (level)
    all_gather x3, waiting for transfers between devices: 0.04 us -> 24.6 us  [shards(): raws = [lax.all_gather(panel, 'pcol', axis=0) for panel in panels]]
    all_to_all x4, waiting for transfers between devices: 31 us -> 13.1 us  [exchange(): got = lax.all_to_all(sent, axes, split_axis=0, concat_axis=0, tiled=True)]
  transfers between devices with their start and end apart: 17 -> 17, of which waited for: 12 -> 13; matrix products, arithmetic and copies ran while one was open for 30% -> 28% of each run, Pallas kernels for 27% -> 27%
where the time goes in v4:
time: 646 us; the launch traced here: 636 us
  Pallas kernels  204 us (32%)
  waiting for transfers between devices  176 us (27%)
  other arithmetic  145 us (22%)
  starting transfers between devices  43.9 us (7%)
  local copies, waits for them, and re-layouts  36.8 us (6%)
  between operations  16.1 us (2%)
  matrix products  13.8 us (2%)
    ppermute x9, waiting for transfers between devices, over_cols(): got.append(lax.ppermute(pieces[d], 'pcol', pairs))  138 us
    pallas_call x3, Pallas kernels, pack(): pl.pallas_call(functools.partial(pack_kernel, rows, tiles), out_shape=sha...  57.9 us
    pallas_call x4, Pallas kernels, finish_part(): pl.pallas_call(functools.partial(finish_kernel, rows, tiles, lane, stride...  54 us
    another operation x12, other arithmetic, cholesky_inverse(): factor[b, b] = jnp.linalg.cholesky(pivot, symmetrize_input=False)  49.6 us
    another operation x9, other arithmetic, cholesky_inverse(): jax.scipy.linalg.solve_triangular(factor[b, b], identity, lower=True)  42 us
    pallas_call x3, Pallas kernels, update_part(): pl.pallas_call(functools.partial(update_kernel, rows, placed, tuple(parts...  39.2 us
    all_to_all x4, starting transfers between devices, exchange(): got = lax.all_to_all(sent, axes, split_axis=0, concat_axis=0, tiled=True)  31.9 us
    pallas_call x3, Pallas kernels, goce_rows(): pl.pallas_call(functools.partial(goce_rows_kernel, rows), out_shape=jax.S...  26.4 us
  transfers between devices with their start and end apart: 17, of which 13 were waited for; matrix products, arithmetic and copies ran while one was open for 28% of the time, Pallas kernels for 27%

profile of v4, /device:TPU:0, one launch (start us, length us, event | category | flops | bytes accessed | tf_op | source)
XLA Modules:
  0.0 636.3 jit_solution(8783635020477115862)
XLA Ops:
  8.4 8.2 %sort.43 = (s32[11264]{0:T(1024)S(1)}, s32[11264]{0:T(1024)}) sort(s32[11264]{0:T(1024)S(1)} %iota_add_fusion, s32[11264]{0:T(1024)S(1)} %iota.228), dimensions={0}, to_apply=%region_0.0 | sort | flops 157696 | bytes 180224 | tf_op jit(solution)/shard_map/jit(sort)/sort | solution.py:526
  19.1 18.6 %pack.3 = f32[8,4,448,128]{3,2,1,0:T(8,128)} custom-call(s32[3584]{0:T(1024)} %reshape.674.index_ref, f32[45056,128]{1,0:T(8,128)} %bitcast.138, bf16[4,512,128]{2,1,0:T(8,128)(2,1)} %get-tuple-element.149.onehot_ref), custom_call_target="tpu_custom_call" | custom-call | flops 1 | bytes 1 | tf_op jit(solution)/shard_map/pack/pallas_call | solution.py:126
  37.7 7.4 %all-to-all-start = ((f32[32,448,128]{2,1,0:T(8,128)}), f32[32,448,128]{2,1,0:T(8,128)}, u32[]{:S(2)}, u32[]{:S(2)}) async-start(f32[32,448,128]{2,1,0:T(8,128)} %bitcast.142), calls=%async_computation | async-start | bytes 14680064 | tf_op jit(solution)/shard_map/all_to_all | solution.py:547
  46.7 17.8 %pack.4 = (f32[8,400,128]{2,1,0:T(8,128)}, f32[8,400,128]{2,1,0:T(8,128)}, f32[8,400,128]{2,1,0:T(8,128)}, f32[8,400,128]{2,1,0:T(8,128)}) custom-call(s32[3200]{0:T(1024)} %reshape.673.index_ref, f32[45056,128]{1,0:T(8,128)} %bitcast.139, bf16[4,512,128]{2,1,0:T(8,128)(2,1)} %get-tuple-element.148.onehot_ref), custom_call_target="tpu_custom_call" | custom-call | flops 1 | bytes 1 | tf_op jit(solution)/shard_map/pack/pallas_call | solution.py:126
  69.9 21.5 %pack.5 = (f32[8,560,128]{2,1,0:T(8,128)}, f32[8,560,128]{2,1,0:T(8,128)}, f32[8,560,128]{2,1,0:T(8,128)}, f32[8,560,128]{2,1,0:T(8,128)}) custom-call(s32[4480]{0:T(1024)} %reshape.677.index_ref, f32[45056,128]{1,0:T(8,128)} %bitcast.140, bf16[4,512,128]{2,1,0:T(8,128)(2,1)} %get-tuple-element.148.onehot_ref), custom_call_target="tpu_custom_call" | custom-call | flops 1 | bytes 1 | tf_op jit(solution)/shard_map/pack/pallas_call | solution.py:126
  93.4 16.1 %broadcast_multiply_fusion.base_hbm = f32[11264,512]{1,0:T(8,128)} fusion(f32[11264,512]{1,0:T(8,128)} %goce_hbm.5, f32[512]{0:T(512)S(1)} %select_multiply_fusion), kind=kLoop, calls=%fused_computation.9 | loop fusion | flops 5767168 | bytes 46139392 | tf_op jit(solution)/shard_map/mul | solution.py:587
  114.9 8.0 %goce_rows.4 = f32[3200,128]{1,0:T(8,128)} custom-call(s32[3200]{0:T(1024)} %reshape.680.index_ref, f32[2]{0:T(128)} %pad_maximum_fusion.16.weight_ref, f32[11264,512]{1,0:T(8,128)} %goce_hbm.5), custom_call_target="tpu_custom_call" | custom-call | flops 1 | bytes 1 | tf_op jit(solution)/shard_map/goce_rows/pallas_call | solution.py:211
  122.9 8.5 %goce_rows.3.added_ref = f32[3584,128]{1,0:T(8,128)} custom-call(s32[3584]{0:T(1024)} %reshape.679.index_ref, f32[2]{0:T(128)} %pad_maximum_fusion.16.weight_ref, f32[11264,512]{1,0:T(8,128)} %goce_hbm.5), custom_call_target="tpu_custom_call" | custom-call | flops 1 | bytes 1 | tf_op jit(solution)/shard_map/goce_rows/pallas_call | solution.py:211
  131.5 9.8 %goce_rows.5 = f32[4480,128]{1,0:T(8,128)} custom-call(s32[4480]{0:T(1024)} %reshape.681.index_ref, f32[2]{0:T(128)} %pad_maximum_fusion.16.weight_ref, f32[11264,512]{1,0:T(8,128)} %goce_hbm.5), custom_call_target="tpu_custom_call" | custom-call | flops 1 | bytes 1 | tf_op jit(solution)/shard_map/goce_rows/pallas_call | solution.py:211
  145.0 8.2 %sort.45 = (s32[11264]{0:T(1024)S(1)}, s32[11264]{0:T(1024)}) sort(s32[11264]{0:T(1024)S(1)} %fusion.92, s32[11264]{0:T(1024)S(1)} %iota.231), dimensions={0}, to_apply=%region_3.4 | sort | flops 157696 | bytes 180224 | tf_op jit(solution)/shard_map/jit(sort)/sort | solution.py:577
  154.1 3.1 fusion.9.keep_ref
  157.2 7.6 %collective-permute-done.1.refs_2_ = f32[8,400,128]{2,1,0:T(8,128)} collective-permute-done((f32[8,400,128]{2,1,0:T(8,128)}, f32[8,400,128]{2,1,0:T(8,128)}, u32[]{:S(2)}, u32[]{:S(2)}) %collective-permute-start.1) | collective-permute-done | bytes 1638432 | tf_op jit(solution)/shard_map/ppermute | solution.py:557
  164.8 37.2 %collective-permute-done.2.refs_3_ = f32[8,400,128]{2,1,0:T(8,128)} collective-permute-done((f32[8,400,128]{2,1,0:T(8,128)}, f32[8,400,128]{2,1,0:T(8,128)}, u32[]{:S(2)}, u32[]{:S(2)}) %collective-permute-start.2) | collective-permute-done | bytes 1638432 | tf_op jit(solution)/shard_map/ppermute | solution.py:557
  202.0 2.4 collective-permute-start.6
  205.9 8.2 %mix.2 = f32[8,4,400,128]{3,2,1,0:T(8,128)} custom-call(bf16[4,128,512]{2,1,0:T(8,128)(2,1)} %broadcast_select_fusion.1.onehot_ref, f32[8,400,128]{2,1,0:T(8,128)} %get-tuple-element.79.refs_0_, f32[8,400,128]{2,1,0:T(8,128)} %collective-permute-done.refs_1_, f32[8,400,128]{2,1,0:T(8,128)} %collective-permute-done.1.refs_2_, ...), custom_call_target="tpu_custom_call" | custom-call | flops 1 | bytes 1 | tf_op jit(solution)/shard_map/mix/pallas_call | solution.py:178
  216.2 7.0 %panel.1 = f32[3584,128]{1,0:T(8,128)} custom-call(f32[2]{0:T(128)} %pad_maximum_fusion.16.weight_ref, f32[3584,128]{1,0:T(8,128)} %goce_rows.3.added_ref, bf16[4,128,128]{2,1,0:T(8,128)(2,1)} %slice.147.onehot_ref, f32[8,4,448,128]{3,2,1,0:T(8,128)} %bitcast.9.received_ref.refs_2_), custom_call_target="tpu_custom_call" | custom-call | flops 1 | bytes 700000000 | tf_op jit(solution)/shard_map/panel/pallas_call | solution.py:241
  223.2 2.2 gather_fusion.1
  226.2 7.8 %all-to-all-start.1 = ((f32[8,1600,128]{2,1,0:T(8,128)}), f32[8,1600,128]{2,1,0:T(8,128)}, u32[]{:S(2)}, u32[]{:S(2)}) async-start(f32[8,1600,128]{2,1,0:T(8,128)} %bitcast.144), calls=%async_computation.1 | async-start | bytes 13107200 | tf_op jit(solution)/shard_map/all_to_all | solution.py:547
  234.0 23.5 %collective-permute-done.6.refs_1_ = f32[8,560,128]{2,1,0:T(8,128)S(1)} collective-permute-done((f32[8,560,128]{2,1,0:T(8,128)}, f32[8,560,128]{2,1,0:T(8,128)S(1)}, u32[]{:S(2)}, u32[]{:S(2)}) %collective-permute-start.6) | collective-permute-done | bytes 2293792 | tf_op jit(solution)/shard_map/ppermute | solution.py:557
  257.5 47.1 %collective-permute-done.7.refs_2_ = f32[8,560,128]{2,1,0:T(8,128)} collective-permute-done((f32[8,560,128]{2,1,0:T(8,128)}, f32[8,560,128]{2,1,0:T(8,128)}, u32[]{:S(2)}, u32[]{:S(2)}) %collective-permute-start.7) | collective-permute-done | bytes 2293792 | tf_op jit(solution)/shard_map/ppermute | solution.py:557
  313.9 3.9 collective-permute-start.4
  317.8 11.9 %mix.3 = (f32[8,1,560,128]{3,2,1,0:T(8,128)}, f32[8,3,560,128]{3,2,1,0:T(8,128)}) custom-call(bf16[4,128,512]{2,1,0:T(8,128)(2,1)} %broadcast_select_fusion.1.onehot_ref, f32[8,560,128]{2,1,0:T(8,128)} %get-tuple-element.84.refs_0_, f32[8,560,128]{2,1,0:T(8,128)} %copy-done.5, f32[8,560,128]{2,1,0:T(8,128)} %collective-permute-done.7.refs_2_, ...), custom_call_target="tpu_custom_call" | custom-call | flops 1 | bytes 1 | tf_op jit(solution)/shard_map/mix/pallas_call | solution.py:178
  329.7 3.7 collective-permute-done.3
  333.4 8.8 %collective-permute-done.4 = f32[7,128,128]{2,1,0:T(8,128)S(1)} collective-permute-done((f32[7,128,128]{2,1,0:T(8,128)S(1)}, f32[7,128,128]{2,1,0:T(8,128)S(1)}, u32[]{:S(2)}, u32[]{:S(2)}) %collective-permute-start.4) | collective-permute-done | bytes 458784 | tf_op jit(solution)/shard_map/ppermute | solution.py:557
  342.1 10.3 %collective-permute-done.5 = f32[7,128,128]{2,1,0:T(8,128)S(1)} collective-permute-done((f32[7,128,128]{2,1,0:T(8,128)S(1)}, f32[7,128,128]{2,1,0:T(8,128)S(1)}, u32[]{:S(2)}, u32[]{:S(2)}) %collective-permute-start.5) | collective-permute-done | bytes 458784 | tf_op jit(solution)/shard_map/ppermute | solution.py:557
  354.5 2.8 copy.152
  359.0 1.9 copy.153
  362.7 11.7 %cholesky.75 = f32[128,128]{1,0:T(8,128)S(1)} custom-call(f32[128,128]{1,0:T(8,128)S(1)} %bitcast_add_fusion.5), custom_call_target="Cholesky" | custom-call | tf_op jit(solution)/shard_map/jit(cholesky)/cholesky | solution.py:470
  375.8 9.8 %custom-call.8 = f32[1,128,128]{1,2,0:T(8,128)S(1)} custom-call(f32[1,128,128]{2,1,0:T(8,128)S(1)} %get-tuple-element.116), custom_call_target="InvertDiagBlocksLowerTriangular" | custom-call | tf_op jit(solution)/shard_map/jit(_solve_triangular)/triangular_solve | solution.py:471
  390.0 11.9 %all-to-all-start.2 = ((f32[8,560,128]{2,1,0:T(8,128)}), f32[8,560,128]{2,1,0:T(8,128)S(1)}, u32[]{:S(2)}, u32[]{:S(2)}) async-start(f32[8,560,128]{2,1,0:T(8,128)} %bitcast.152), calls=%async_computation.2 | async-start | bytes 4587520 | tf_op jit(solution)/shard_map/all_to_all | solution.py:547
  403.4 11.7 %cholesky.86 = f32[128,128]{1,0:T(8,128)S(1)} custom-call(f32[128,128]{1,0:T(8,128)S(1)} %convolution_subtract_fusion.3), custom_call_target="Cholesky" | custom-call | tf_op jit(solution)/shard_map/jit(cholesky)/cholesky | solution.py:470
  416.5 9.8 %custom-call.9 = f32[1,128,128]{1,2,0:T(8,128)S(1)} custom-call(f32[1,128,128]{2,1,0:T(8,128)S(1)} %get-tuple-element.114), custom_call_target="InvertDiagBlocksLowerTriangular" | custom-call | tf_op jit(solution)/shard_map/jit(_solve_triangular)/triangular_solve | solution.py:471
  428.4 11.7 %cholesky.97 = f32[128,128]{1,0:T(8,128)S(1)} custom-call(f32[128,128]{1,0:T(8,128)S(1)} %convolution_subtract_fusion.2), custom_call_target="Cholesky" | custom-call | tf_op jit(solution)/shard_map/jit(cholesky)/cholesky | solution.py:470
  441.5 10.0 %custom-call.10 = f32[1,128,128]{1,2,0:T(8,128)S(1)} custom-call(f32[1,128,128]{2,1,0:T(8,128)S(1)} %get-tuple-element.112), custom_call_target="InvertDiagBlocksLowerTriangular" | custom-call | tf_op jit(solution)/shard_map/jit(_solve_triangular)/triangular_solve | solution.py:471
  453.1 2.0 all-to-all-done.2
  459.3 4.8 all-to-all-start.3
  469.0 11.7 %cholesky.108 = f32[128,128]{1,0:T(8,128)S(1)} custom-call(f32[128,128]{1,0:T(8,128)S(1)} %copy.173), custom_call_target="Cholesky" | custom-call | tf_op jit(solution)/shard_map/jit(cholesky)/cholesky | solution.py:470
  482.1 9.8 %custom-call.11 = f32[1,128,128]{1,2,0:T(8,128)S(1)} custom-call(f32[1,128,128]{2,1,0:T(8,128)S(1)} %get-tuple-element.110), custom_call_target="InvertDiagBlocksLowerTriangular" | custom-call | tf_op jit(solution)/shard_map/jit(_solve_triangular)/triangular_solve | solution.py:471
  495.1 2.9 fusion.11
  497.9 15.0 %update.5 = f32[448,4,8,128]{3,2,1,0:T(8,128)} custom-call(f32[2]{0:T(128)} %pad_maximum_fusion.16.weight_ref, f32[1,512]{1,0:T(1,128)} %compare_select_fusion.1.mask_ref, f32[3584,1]{1,0:T(8,128)} %fusion.9.keep_ref, bf16[512,512]{1,0:T(8,128)(2,1)} %get-tuple-element.138.high_ref, bf16[512,512]{1,0:T(8,128)(2,1)} %get-tuple-element.137.low_ref, ...), custom_call_target="tpu_custom_call" | custom-call | flops 1 | bytes 1 | tf_op jit(solution)/shard_map/update/pallas_call | solution.py:327
  517.1 13.1 %finish.4.base_hbm = f32[11264,512]{1,0:T(8,128)} custom-call(s32[16]{0:T(128)} %reshape.682.bounds_ref, s32[11264]{0:T(1024)} %get-tuple-element.104.index_ref, f32[2]{0:T(128)} %pad_maximum_fusion.16.weight_ref, f32[14336,128]{1,0:T(8,128)} %bitcast.143, f32[256,512]{1,0:T(8,128)} %bitcast_select_fusion.head_ref, ...), custom_call_target="tpu_custom_call", output_to_operand_aliasing={{}: (5, {})} | custom-call | flops 1 | bytes 1 | tf_op jit(solution)/shard_map/finish/pallas_call | solution.py:428
  530.2 10.6 %update.4 = f32[400,4,8,128]{3,2,1,0:T(8,128)} custom-call(f32[2]{0:T(128)} %pad_maximum_fusion.16.weight_ref, f32[1,512]{1,0:T(1,128)} %compare_select_fusion.1.mask_ref, f32[3584,1]{1,0:T(8,128)} %fusion.9.keep_ref, bf16[512,512]{1,0:T(8,128)(2,1)} %get-tuple-element.138.high_ref, bf16[512,512]{1,0:T(8,128)(2,1)} %get-tuple-element.137.low_ref, ...), custom_call_target="tpu_custom_call" | custom-call | flops 1 | bytes 1 | tf_op jit(solution)/shard_map/update/pallas_call | solution.py:327
  540.8 12.5 %finish.5.base_hbm = f32[11264,512]{1,0:T(8,128)} custom-call(s32[16]{0:T(128)} %reshape.683.bounds_ref, s32[11264]{0:T(1024)} %get-tuple-element.100.index_ref, f32[2]{0:T(128)} %pad_maximum_fusion.16.weight_ref, f32[12800,128]{1,0:T(8,128)} %bitcast.145, f32[256,512]{1,0:T(8,128)} %bitcast_select_fusion.head_ref, ...), custom_call_target="tpu_custom_call", output_to_operand_aliasing={{}: (5, {})} | custom-call | flops 1 | bytes 1 | tf_op jit(solution)/shard_map/finish/pallas_call | solution.py:428
  553.3 24.6 %all-gather.10.cloned.1.call-done = f32[17920,128]{1,0:T(8,128)} async-done(((f32[4480,128]{1,0:T(8,128)}), f32[17920,128]{1,0:T(8,128)}) %all-gather.10.cloned.1.call-update) | async-done | bytes 9175056 | tf_op jit(solution)/shard_map/all_gather | solution.py:666
  577.9 13.6 %update.3 = f32[560,4,8,128]{3,2,1,0:T(8,128)} custom-call(f32[2]{0:T(128)} %pad_maximum_fusion.16.weight_ref, f32[1,512]{1,0:T(1,128)} %compare_select_fusion.1.mask_ref, f32[3584,1]{1,0:T(8,128)} %fusion.9.keep_ref, bf16[512,512]{1,0:T(8,128)(2,1)} %get-tuple-element.138.high_ref, bf16[512,512]{1,0:T(8,128)(2,1)} %get-tuple-element.137.low_ref, ...), custom_call_target="tpu_custom_call" | custom-call | flops 1 | bytes 1 | tf_op jit(solution)/shard_map/update/pallas_call | solution.py:327
  591.5 15.1 %finish.6.base_hbm = f32[11264,512]{1,0:T(8,128)} custom-call(s32[16]{0:T(128)} %reshape.684.bounds_ref, s32[11264]{0:T(1024)} %get-tuple-element.73.index_ref, f32[2]{0:T(128)} %pad_maximum_fusion.16.weight_ref, f32[17920,128]{1,0:T(8,128)} %bitcast.141, f32[256,512]{1,0:T(8,128)} %bitcast_select_fusion.head_ref, ...), custom_call_target="tpu_custom_call", output_to_operand_aliasing={{}: (5, {})} | custom-call | flops 1 | bytes 1 | tf_op jit(solution)/shard_map/finish/pallas_call | solution.py:428
  606.7 9.1 %all-to-all-done.3 = f32[8,1680,128]{2,1,0:T(8,128)} async-done(((f32[8,1680,128]{2,1,0:T(8,128)}), f32[8,1680,128]{2,1,0:T(8,128)}, u32[]{:S(2)}, u32[]{:S(2)}) %all-to-all-start.3) | async-done | bytes 6881312 | tf_op jit(solution)/shard_map/all_to_all | solution.py:547
  615.7 13.2 %finish.7 = f32[11264,512]{1,0:T(8,128)} custom-call(s32[16]{0:T(128)} %reshape.684.bounds_ref, s32[11264]{0:T(1024)} %get-tuple-element.72.index_ref, f32[2]{0:T(128)} %pad_maximum_fusion.16.weight_ref, f32[13440,128]{1,0:T(8,128)} %bitcast.68.part_hbm, f32[256,512]{1,0:T(8,128)} %bitcast_select_fusion.head_ref, ...), custom_call_target="tpu_custom_call", output_to_operand_aliasing={{}: (5, {})} | custom-call | flops 1 | bytes 1 | tf_op jit(solution)/shard_map/finish/pallas_call | solution.py:428
  (201 shorter events, 71.9 us)
Async XLA Ops:
  37.7 7.5 %copy-start.10 = (s32[2048]{0:T(1024)S(1)}, s32[2048]{0:T(1024)}, u32[]{:S(2)}) copy-start(s32[2048]{0:T(1024)} %param.22) | copy-start | bytes 24580
  37.7 178.5 %all-to-all-start = ((f32[32,448,128]{2,1,0:T(8,128)}), f32[32,448,128]{2,1,0:T(8,128)}, u32[]{:S(2)}, u32[]{:S(2)}) async-start(f32[32,448,128]{2,1,0:T(8,128)} %bitcast.142), calls=%async_computation | async-start | bytes 14680064 | tf_op jit(solution)/shard_map/all_to_all | solution.py:547
  45.1 64.4 %sort.50.cloned.1.call-start = ((), (), s32[]{:S(2)}) async-start(), calls=%async_computation.9 | async-start | bytes 24608 | tf_op jit(solution)/shard_map/jit(sort)/sort | solution.py:578
  45.9 65.1 %sort.48.cloned.1.call-start = ((), (), s32[]{:S(2)}) async-start(), calls=%async_computation.8 | async-start | bytes 1081376 | tf_op jit(solution)/shard_map/jit(sort)/sort | solution.py:567
  46.7 21.4 %copy-start.6 = (s32[90112]{0:T(1024)S(1)}, s32[90112]{0:T(1024)}, u32[]{:S(2)}) copy-start(s32[90112]{0:T(1024)} %param.21) | copy-start | bytes 1081348
  64.5 92.7 %collective-permute-start = (f32[8,400,128]{2,1,0:T(8,128)}, f32[8,400,128]{2,1,0:T(8,128)}, u32[]{:S(2)}, u32[]{:S(2)}) collective-permute-start(f32[8,400,128]{2,1,0:T(8,128)} %get-tuple-element.63), channel_id=1, source_target_pairs={{0,1},{1,0},{2,3},{3,2},{4,5},{5,4},{6,7},{7,6},{8,9},{9,8},{10,11... | collective-permute-start | bytes 4915208 | tf_op jit(solution)/shard_map/ppermute | solution.py:557
  66.3 98.6 %collective-permute-start.1 = (f32[8,400,128]{2,1,0:T(8,128)}, f32[8,400,128]{2,1,0:T(8,128)}, u32[]{:S(2)}, u32[]{:S(2)}) collective-permute-start(f32[8,400,128]{2,1,0:T(8,128)} %get-tuple-element.64), channel_id=1, source_target_pairs={{0,2},{1,3},{2,0},{3,1},{4,6},{5,7},{6,4},{7,5},{8,10},{9,11},{10,... | collective-permute-start | bytes 4915208 | tf_op jit(solution)/shard_map/ppermute | solution.py:557
  67.7 134.3 %collective-permute-start.2 = (f32[8,400,128]{2,1,0:T(8,128)}, f32[8,400,128]{2,1,0:T(8,128)}, u32[]{:S(2)}, u32[]{:S(2)}) collective-permute-start(f32[8,400,128]{2,1,0:T(8,128)} %get-tuple-element.65), channel_id=1, source_target_pairs={{0,3},{1,2},{2,1},{3,0},{4,7},{5,6},{6,5},{7,4},{8,11},{9,10},{10,... | collective-permute-start | bytes 4915208 | tf_op jit(solution)/shard_map/ppermute | solution.py:557
  69.6 23.7 %slice-start = ((f32[512]{0:T(512)}), f32[128]{0:T(128)S(1)}, s32[]{:S(2)}) async-start(f32[512]{0:T(512)} %param.20), calls=%async_computation.12 | async-start | bytes 1024 | tf_op jit(solution)/shard_map/slice | solution.py:611
  69.6 235.4 %all-gather.8.cloned.1.call-start = ((), (), s32[]{:S(2)}) async-start(), calls=%async_computation.4 | async-start | bytes 1179648 | tf_op jit(solution)/shard_map/all_gather | solution.py:613
  110.3 103.8 %copy-start.4 = (bf16[4,128,512]{2,1,0:T(8,128)(2,1)}, bf16[4,128,512]{2,1,0:T(8,128)(2,1)S(1)}, u32[]{:S(2)}) copy-start(bf16[4,128,512]{2,1,0:T(8,128)(2,1)S(1)} %fusion.24.refs_1_) | copy-start | bytes 1572868
  141.3 3.7 copy-start.7
  141.3 3.7 copy-start.8
  141.3 3.7 copy-start.9
  202.0 55.5 %collective-permute-start.6 = (f32[8,560,128]{2,1,0:T(8,128)}, f32[8,560,128]{2,1,0:T(8,128)S(1)}, u32[]{:S(2)}, u32[]{:S(2)}) collective-permute-start(f32[8,560,128]{2,1,0:T(8,128)} %get-tuple-element.85), channel_id=1, source_target_pairs={{0,1},{1,0},{2,3},{3,2},{4,5},{5,4},{6,7},{7,6},{8,9},{9,8},{10,11... | collective-permute-start | bytes 6881288 | tf_op jit(solution)/shard_map/ppermute | solution.py:557
  204.4 100.2 %collective-permute-start.7 = (f32[8,560,128]{2,1,0:T(8,128)}, f32[8,560,128]{2,1,0:T(8,128)}, u32[]{:S(2)}, u32[]{:S(2)}) collective-permute-start(f32[8,560,128]{2,1,0:T(8,128)} %get-tuple-element.86), channel_id=1, source_target_pairs={{0,2},{1,3},{2,0},{3,1},{4,6},{5,7},{6,4},{7,5},{8,10},{9,11},{10,... | collective-permute-start | bytes 6881288 | tf_op jit(solution)/shard_map/ppermute | solution.py:557
  204.4 100.5 %collective-permute-start.8 = (f32[8,560,128]{2,1,0:T(8,128)}, f32[8,560,128]{2,1,0:T(8,128)}, u32[]{:S(2)}, u32[]{:S(2)}) collective-permute-start(f32[8,560,128]{2,1,0:T(8,128)} %get-tuple-element.87), channel_id=1, source_target_pairs={{0,3},{1,2},{2,1},{3,0},{4,7},{5,6},{6,5},{7,4},{8,11},{9,10},{10,... | collective-permute-start | bytes 6881288 | tf_op jit(solution)/shard_map/ppermute | solution.py:557
  226.2 160.9 %all-to-all-start.1 = ((f32[8,1600,128]{2,1,0:T(8,128)}), f32[8,1600,128]{2,1,0:T(8,128)}, u32[]{:S(2)}, u32[]{:S(2)}) async-start(f32[8,1600,128]{2,1,0:T(8,128)} %bitcast.144), calls=%async_computation.1 | async-start | bytes 13107200 | tf_op jit(solution)/shard_map/all_to_all | solution.py:547
  233.9 71.0 %copy-start.12 = (s32[3]{0:T(128)S(1)}, s32[3]{0:T(128)}, u32[]{:S(2)}) copy-start(s32[3]{0:T(128)} %constant.390) | copy-start | bytes 40
  233.9 264.0 %all-gather.14.cloned.1.call-start = ((), (), s32[]{:S(2)}) async-start(), calls=%async_computation.7 | async-start | bytes 9175040 | tf_op jit(solution)/shard_map/all_gather | solution.py:666
  257.5 55.7 %copy-start.5 = (f32[8,560,128]{2,1,0:T(8,128)}, f32[8,560,128]{2,1,0:T(8,128)S(1)}, u32[]{:S(2)}) copy-start(f32[8,560,128]{2,1,0:T(8,128)S(1)} %collective-permute-done.6.refs_1_) | copy-start | bytes 6881284
  304.9 225.3 %all-gather.12.cloned.1.call-start = ((), (), s32[]{:S(2)}) async-start(), calls=%async_computation.6 | async-start | bytes 8192000 | tf_op jit(solution)/shard_map/all_gather | solution.py:666
  313.8 19.6 %collective-permute-start.3 = (f32[7,128,128]{2,1,0:T(8,128)S(1)}, f32[7,128,128]{2,1,0:T(8,128)S(1)}, u32[]{:S(2)}, u32[]{:S(2)}) collective-permute-start(f32[7,128,128]{2,1,0:T(8,128)S(1)} %get-tuple-element.140), channel_id=1, source_target_pairs={{0,1},{1,0},{2,3},{3,2},{4,5},{5,4},{6,7},{7,6},{8,9},{9,8},{10,11... | collective-permute-start | bytes 1376264 | tf_op jit(solution)/shard_map/ppermute | solution.py:557
  313.9 28.3 %collective-permute-start.4 = (f32[7,128,128]{2,1,0:T(8,128)S(1)}, f32[7,128,128]{2,1,0:T(8,128)S(1)}, u32[]{:S(2)}, u32[]{:S(2)}) collective-permute-start(f32[7,128,128]{2,1,0:T(8,128)S(1)} %get-tuple-element.141), channel_id=1, source_target_pairs={{0,2},{1,3},{2,0},{3,1},{4,6},{5,7},{6,4},{7,5},{8,10},{9,11},{10,... | collective-permute-start | bytes 1376264 | tf_op jit(solution)/shard_map/ppermute | solution.py:557
  317.8 34.6 %collective-permute-start.5 = (f32[7,128,128]{2,1,0:T(8,128)S(1)}, f32[7,128,128]{2,1,0:T(8,128)S(1)}, u32[]{:S(2)}, u32[]{:S(2)}) collective-permute-start(f32[7,128,128]{2,1,0:T(8,128)S(1)} %get-tuple-element.142), channel_id=1, source_target_pairs={{0,3},{1,2},{2,1},{3,0},{4,7},{5,6},{6,5},{7,4},{8,11},{9,10},{10,... | collective-permute-start | bytes 1376264 | tf_op jit(solution)/shard_map/ppermute | solution.py:557
  359.0 26.9 %copy-start.1 = (f32[4,7,128,128]{2,3,1,0:T(8,128)}, f32[4,7,128,128]{2,3,1,0:T(8,128)S(1)}, u32[]{:S(2)}) copy-start(f32[4,7,128,128]{2,3,1,0:T(8,128)S(1)} %broadcast_select_fusion) | copy-start | bytes 5505028
  386.0 2.6 copy-start.3
  390.0 65.2 %all-to-all-start.2 = ((f32[8,560,128]{2,1,0:T(8,128)}), f32[8,560,128]{2,1,0:T(8,128)S(1)}, u32[]{:S(2)}, u32[]{:S(2)}) async-start(f32[8,560,128]{2,1,0:T(8,128)} %bitcast.152), calls=%async_computation.2 | async-start | bytes 4587520 | tf_op jit(solution)/shard_map/all_to_all | solution.py:547
  401.9 176.0 %all-gather.10.cloned.1.call-start = ((), (), s32[]{:S(2)}) async-start(), calls=%async_computation.5 | async-start | bytes 11468800 | tf_op jit(solution)/shard_map/all_gather | solution.py:666
  455.2 1.4 copy-start
  455.2 2.5 copy-start.2
  459.3 156.4 %all-to-all-start.3 = ((f32[8,1680,128]{2,1,0:T(8,128)}), f32[8,1680,128]{2,1,0:T(8,128)}, u32[]{:S(2)}, u32[]{:S(2)}) async-start(f32[8,1680,128]{2,1,0:T(8,128)} %bitcast.150), calls=%async_computation.3 | async-start | bytes 13762560 | tf_op jit(solution)/shard_map/all_to_all | solution.py:547
  514.3 1.8 copy-start.11
Sparse Core Ops, SparseCore 0:
  48.3 3.2 sort.54.cloned.1.call-done
  69.8 19.8 sort.52.cloned.1.call-done
  226.3 35.1 all-gather.7
  305.0 102.3 all-gather.13
  409.1 73.0 all-gather.11
  483.8 94.0 all-gather.9
  (2 shorter events, 0.0 us)
